TPU v7x, 128 devices: a whole 4x4x4 slice. The times are simulated.
128 devices in a mesh: seq: 8 (over x, core), cand: 16 (over y, z).
Axes of the slice: x: 4, y: 4, z: 4, core: 2. Of those that a mesh axis runs over, the one named last changes fastest.
Arguments:
- events: bfloat16 [16, 4096, 1024], P('cand', 'seq'), may hold values from -6 to 6
- lengths: int32 [16], P('cand'), may hold values from 1024 to 4096, as said below
- target_pos: int32 [16, 32], P('cand'), may hold values from 0 to 4095, as said below
- target_ids: int32 [16, 32], P('cand', 'seq'), may hold values from 0 to 524287
- items: bfloat16 [524288, 1024], P(('seq', 'cand')), may hold values from -0.1875 to 0.1875
- item_block: int32 [128], P(('seq', 'cand')), may hold values from 0 to 127, each once
- temper: float32 [16], replicated, may hold values from 1 to 64
- in_gain: float32 [1024], replicated, may hold values from 0.25 to 1.75
- w_xbc: bfloat16 [1024, 2304], replicated, may hold values from -0.1875 to 0.1875
- w_z: bfloat16 [1024, 2048], replicated, may hold values from -0.1875 to 0.1875
- w_dt: bfloat16 [1024, 32], replicated, may hold values from -0.1875 to 0.1875
- conv_w: float32 [4, 2304], replicated, may hold values from -3 to 3
- conv_b: float32 [2304], replicated, may hold values from -0.5 to 0.5
- dt_bias: float32 [32], replicated, may hold values from -8 to -3
- a_log: float32 [32], replicated, may hold values from -1.5 to 2.8
- d_skip: float32 [32], replicated, may hold values from 0.5 to 1.5
- norm_gain: float32 [2048], replicated, may hold values from 0.25 to 1.75
- w_out: bfloat16 [2048, 1024], replicated, may hold values from -0.125 to 0.125
- final_gain: float32 [1024], replicated, may hold values from 0.25 to 1.75
Outputs:
- layer_out: bfloat16 [16, 4096, 1024], P('cand', 'seq')
- loss: float32 [512], P(('seq', 'cand'))
Inputs may be any that keep to these rules, and one draw needn't show every extreme that they name: `lengths`: one history in every draw has all 4096 events valid. `target_pos`: each target lies before its history's length.
All inputs are finite; a program needn't handle non-finite values.
Results may differ from a plain program's by a relative error of at most 0.0085.
Values may be sent and summed in bfloat16 or wider, within the bound.
No kernel may reach another device: no remote copies, remote signals or barrier semaphores. Data moves between devices by JAX's collectives and lax.ppermute only.
A program may use at most 128 MiB of HBM per device.

v0:
```python
import jax
import jax.numpy as jnp
from jax import lax
from jax.sharding import PartitionSpec as P

GROUP = 128


EPS = 1e-05
HIGH = lax.Precision.HIGHEST


def shifted(block, axis, distance):
    devices = range(lax.axis_size(axis))
    route = [(i - distance, i) for i in devices if i - distance in devices]
    return lax.ppermute(block, axis, route)


def joined(shard, axis, combine):
    everything = jax.tree.map(lambda part: lax.all_gather(part, axis), shard)
    initial = jax.tree.map(lambda part: part[0], everything)

    def turn(k, so_far):
        return combine(so_far, jax.tree.map(lambda part: part[k], everything))

    return lax.fori_loop(1, lax.axis_size(axis), turn, initial)


def rms(v, gain):
    return v * lax.rsqrt(jnp.mean(v * v, axis=-1, keepdims=True) + EPS) * gain


def join_stats(first, second):
    top = jnp.maximum(first[0], second[0])
    total = first[1] * jnp.exp(first[0] - top) + second[1] * jnp.exp(second[0] - top)
    return (top, total, first[2] + second[2])


def local(
    events,
    lengths,
    target_pos,
    target_ids,
    items,
    item_block,
    temper,
    in_gain,
    w_xbc,
    w_z,
    w_dt,
    conv_w,
    conv_b,
    dt_bias,
    a_log,
    d_skip,
    norm_gain,
    w_out,
    final_gain,
):
    seq_len = events.shape[1]
    heads = a_log.shape[0]
    inner = w_z.shape[1]
    width = conv_w.shape[1]
    state_size = (width - inner) // 2
    head_size = inner // heads
    taps = conv_w.shape[0]
    blocks = seq_len // GROUP
    ev = events[0]
    normed = rms(ev.astype(jnp.float32), in_gain).astype(jnp.bfloat16)
    xbc_raw = jnp.dot(normed, w_xbc, preferred_element_type=jnp.float32).astype(jnp.bfloat16)
    gate_z = jnp.dot(normed, w_z, preferred_element_type=jnp.float32).astype(jnp.bfloat16)
    dt_raw = jnp.dot(normed, w_dt, preferred_element_type=jnp.float32)
    rim = shifted(xbc_raw[seq_len - (taps - 1) :], "seq", 1)
    padded = jnp.concatenate([rim, xbc_raw], axis=0).astype(jnp.float32)
    conv = conv_b
    for k in range(taps):
        conv = conv + conv_w[k] * padded[k : k + seq_len]
    xbc = jax.nn.silu(conv)
    xh = xbc[:, :inner].reshape(blocks, GROUP, heads, head_size)
    bmat = xbc[:, inner : inner + state_size].reshape(blocks, GROUP, state_size)
    cmat = xbc[:, inner + state_size :].reshape(blocks, GROUP, state_size)
    place = lax.axis_index("seq") * seq_len + jnp.arange(seq_len, dtype=jnp.int32)
    valid = (place < lengths[0]).astype(jnp.float32)
    step = jax.nn.softplus(dt_raw + dt_bias) * valid[:, None]
    logdec = (-step * jnp.exp(a_log)).reshape(blocks, GROUP, heads)
    step = step.reshape(blocks, GROUP, heads)
    cum = jnp.cumsum(logdec, axis=1)
    cum_t = jnp.transpose(cum, (0, 2, 1))
    diff = cum_t[:, :, :, None] - cum_t[:, :, None, :]
    rowi = jnp.arange(GROUP)[:, None]
    colj = jnp.arange(GROUP)[None, :]
    decay = jnp.exp(jnp.where((rowi >= colj)[None, None], diff, -jnp.inf))
    scores = jnp.einsum("cin,cjn->cij", cmat, bmat, precision=HIGH)
    weights = scores[:, None] * decay * jnp.transpose(step, (0, 2, 1))[:, :, None, :]
    y_in = jnp.einsum("chij,cjhp->cihp", weights, xh, precision=HIGH)
    tail = jnp.exp(cum[:, -1:, :] - cum) * step
    group_states = jnp.einsum("cjn,cjh,cjhp->chpn", bmat, tail, xh, precision=HIGH)
    group_decay = jnp.exp(cum[:, -1, :])

    def advance(state, inputs):
        g, s = inputs
        return (g[:, None, None] * state + s, state)

    zero_state = jnp.zeros((heads, head_size, state_size), jnp.float32)
    local_state, before = lax.scan(advance, zero_state, (group_decay, group_states))
    offsets = jnp.cumsum(cum[:, -1, :], axis=0) - cum[:, -1, :]
    local_decay = jnp.exp(jnp.sum(cum[:, -1, :], axis=0))
    entering = zero_state
    for turn in range(lax.axis_size("seq") - 1):
        entering = shifted(
            (local_decay[:, None, None] * entering + local_state).astype(jnp.bfloat16), "seq", 1
        ).astype(jnp.float32)
    y_st = jnp.einsum("cin,chpn->cihp", cmat, before, precision=HIGH) * jnp.exp(cum)[..., None]
    y_enter = (
        jnp.einsum("cin,hpn->cihp", cmat, entering, precision=HIGH)
        * jnp.exp(cum + offsets[:, None, :])[..., None]
    )
    y = (y_in + y_st + y_enter + d_skip[:, None] * xh).reshape(seq_len, inner)
    gated = y * jax.nn.silu(gate_z.astype(jnp.float32))
    mixed = rms(gated, norm_gain).astype(jnp.bfloat16)
    out = (
        ev.astype(jnp.float32) + jnp.dot(mixed, w_out, preferred_element_type=jnp.float32)
    ).astype(jnp.bfloat16)
    final = rms(out.astype(jnp.float32), final_gain).astype(jnp.bfloat16)
    wanted = target_pos[0]
    tgt_rows = target_ids.shape[1]
    onehot = (wanted[:, None] == place[None, :]).astype(jnp.bfloat16)
    rows = lax.psum_scatter(
        jnp.dot(onehot, final, preferred_element_type=jnp.float32).astype(jnp.bfloat16),
        "seq",
        scatter_dimension=0,
        tiled=True,
    )
    block_size = items.shape[0]
    item_ids = item_block[0] * block_size + jnp.arange(block_size, dtype=jnp.int32)
    cand_count = lax.axis_size("cand")
    hist_count = temper.shape[0]
    prow = lax.all_gather(rows, ("seq", "cand"), axis=0, tiled=True)
    pid = lax.all_gather(target_ids[0], ("seq", "cand"), axis=0, tiled=True)
    row_index = jnp.arange(prow.shape[0], dtype=jnp.int32)
    history = row_index // tgt_rows % cand_count
    match = history[:, None] == jnp.arange(hist_count, dtype=jnp.int32)[None, :]
    row_scale = jnp.sum(jnp.where(match, temper[None, :], 0.0), axis=1)
    logit = row_scale[:, None] * lax.dot_general(
        prow, items, (((1,), (1,)), ((), ())), preferred_element_type=jnp.float32
    )
    top = jnp.max(logit, axis=1)
    total = jnp.sum(jnp.exp(logit - top[:, None]), axis=1)
    hit = jnp.sum(jnp.where(pid[:, None] == item_ids[None, :], logit, 0.0), axis=1)
    top, total, hit = (top, total, hit)
    own = lax.axis_index(("seq", "cand")) * tgt_rows
    peak, whole, target = joined((top, total, hit), ("seq", "cand"), join_stats)
    loss = (
        lax.dynamic_slice_in_dim(peak, own, tgt_rows)
        + jnp.log(lax.dynamic_slice_in_dim(whole, own, tgt_rows))
        - lax.dynamic_slice_in_dim(target, own, tgt_rows)
    )
    return (out[None], loss)


def solution(mesh):
    placed = (
        P("cand", "seq", None),
        P("cand"),
        P("cand", None),
        P("cand", "seq"),
        P(("seq", "cand"), None),
        P(("seq", "cand")),
        P(),
        P(),
        P(),
        P(),
        P(),
        P(),
        P(),
        P(),
        P(),
        P(),
        P(),
        P(),
        P(),
    )
    return jax.shard_map(
        local,
        mesh=mesh,
        in_specs=placed,
        out_specs=(P("cand", "seq", None), P(("seq", "cand"))),
        check_vma=False,
    )
```

profile of v0, /device:TPU:1, one launch (start us, length us, event | category | flops | bytes accessed | tf_op | source)
XLA Modules:
  0.0 511.1 jit_solution(8737042329853987828)
XLA Ops:
  8.8 5.4 %convolution_convert_fusion = bf16[512,2304]{1,0:T(8,128)(2,1)S(1)} fusion(bf16[1024,2304]{1,0:T(8,128)(2,1)} %param.31, bf16[1,512,1024]{2,1,0:T(8,128)(2,1)} %param.23, f32[1024]{0:T(1024)} %param.30, f32[512]{0:T(512)S(1)} %add_rsqrt_fusion.2), kind=kOutput, calls=%fused_computation.28 | convolution fusion | flops 2419195904 | bytes 8132608 | tf_op jit(solution)/shard_map/dot_general | solution.py:70
  34.4 5.4 %copy.60 = f32[512,2048]{0,1:T(8,128)} copy(f32[512,2048]{1,0:T(8,128)} %slice.79) | data formatting | bytes 8388608 | tf_op jit(solution)/shard_map/slice | solution.py:79
  39.7 5.2 %reshape.131 = f32[4,128,32,64]{1,0,3,2:T(4,128)} reshape(f32[512,2048]{0,1:T(8,128)} %copy.60) | data formatting | bytes 8388608 | tf_op jit(solution)/shard_map/reshape | solution.py:79
  48.1 5.1 fusion.17
  53.2 12.5 %while.33 = (s32[]{:T(128)}, f32[32,64,128]{2,1,0:T(8,128)S(1)}, f32[4,32,64,128]{3,2,1,0:T(8,128)}, f32[4,32]{1,0:T(4,128)}, f32[4,32,64,128]{3,2,1,0:T(8,128)}, /*index=5*/s32[]{:T(128)}, s32[]{:T(128)}) while((s32[]{:T(128)}, f32[32,64,128]{2,1,0:T(8,128)S(1)}, f32[4,32,64,128]{3,2,1,0:T(8,128)}, f32[4,32]{1,0:T(4,128)}, ...), condition=%wide.region_3.4_spmd.clone, body=%wide.region_2.3_spmd.clone.sunk | while | flops 1048579 | bytes 5243872 | solution.py:105
  67.8 6.1 %collective-permute-done.1 = bf16[32,64,128]{2,1,0:T(8,128)(2,1)S(1)} collective-permute-done((bf16[32,64,128]{2,1,0:T(8,128)(2,1)S(1)}, bf16[32,64,128]{2,1,0:T(8,128)(2,1)S(1)}, u32[]{:S(2)}, u32[]{:S(2)}) %collective-permute-start.1) | collective-permute-done | bytes 524320 | tf_op jit(solution)/shard_map/ppermute | solution.py:16
  74.1 4.5 collective-permute-start.2
  78.6 6.1 %collective-permute-done.2 = bf16[32,64,128]{2,1,0:T(8,128)(2,1)S(1)} collective-permute-done((bf16[32,64,128]{2,1,0:T(8,128)(2,1)S(1)}, bf16[32,64,128]{2,1,0:T(8,128)(2,1)S(1)}, u32[]{:S(2)}, u32[]{:S(2)}) %collective-permute-start.2) | collective-permute-done | bytes 524320 | tf_op jit(solution)/shard_map/ppermute | solution.py:16
  89.3 6.1 %collective-permute-done.3 = bf16[32,64,128]{2,1,0:T(8,128)(2,1)S(1)} collective-permute-done((bf16[32,64,128]{2,1,0:T(8,128)(2,1)S(1)}, bf16[32,64,128]{2,1,0:T(8,128)(2,1)S(1)}, u32[]{:S(2)}, u32[]{:S(2)}) %collective-permute-start.3) | collective-permute-done | bytes 524320 | tf_op jit(solution)/shard_map/ppermute | solution.py:16
  100.1 6.1 %collective-permute-done.4 = bf16[32,64,128]{2,1,0:T(8,128)(2,1)S(1)} collective-permute-done((bf16[32,64,128]{2,1,0:T(8,128)(2,1)S(1)}, bf16[32,64,128]{2,1,0:T(8,128)(2,1)S(1)}, u32[]{:S(2)}, u32[]{:S(2)}) %collective-permute-start.4) | collective-permute-done | bytes 524320 | tf_op jit(solution)/shard_map/ppermute | solution.py:16
  106.4 15.0 %collective-permute-start.5 = (bf16[32,64,128]{2,1,0:T(8,128)(2,1)S(1)}, bf16[32,64,128]{2,1,0:T(8,128)(2,1)S(1)}, u32[]{:S(2)}, u32[]{:S(2)}) collective-permute-start(bf16[32,64,128]{2,1,0:T(8,128)(2,1)S(1)} %add_convert_fusion.2), channel_id=1, source_target_pairs={{0,16},{16,32},{32,48},{48,64},{64,80},{80,96},{96,112},{1,17},{17... | collective-permute-start | bytes 1572872 | tf_op jit(solution)/shard_map/ppermute | solution.py:16
  124.6 5.4 %fusion.58 = f32[4,128,32,64]{1,3,2,0:T(8,128)S(1)} fusion(f32[4,128,128,1]{2,1,3,0:T(8,128)S(1)} %bitcast.101, f32[4,32,64,128]{3,2,1,0:T(8,128)} %get-tuple-element.208), kind=kOutput, calls=%fused_computation.124 | convolution fusion | flops 1610612736 | bytes 8650752 | tf_op jit(solution)/shard_map/cin,chpn->cihp/dot_general | solution.py:113
  134.6 17.0 %fusion.1 = f32[4,32,64,128]{3,2,1,0:T(8,128)S(1)} fusion(f32[4,32,128]{2,1,0:T(8,128)S(1)} %copy.64, f32[4,32,128]{2,1,0:T(8,128)S(1)} %copy.62, f32[4,128,128]{2,1,0:T(8,128)S(1)} %fusion.57, pred[128,128]{1,0:T(8,128)(4,1)S(1)} %iota_compare_fusion, f32[4,128,32,64]{1,0,3,2:T(4,128)S(1)} %copy-done.2), kind=kOutput, calls=%fused_computation.10 | convolution fusion | flops 1619001344 | bytes 8798208 | tf_op jit(solution)/shard_map/chij,cjhp->cihp/dot_general | solution.py:95
  151.7 5.0 fusion.16
  156.7 9.1 %copy.77 = f32[4,128,32,64]{3,2,1,0:T(8,128)} copy(f32[4,128,32,64]{1,3,2,0:T(8,128)} %fusion.16) | data formatting | bytes 8388608 | tf_op jit(solution)/shard_map/reshape | solution.py:118
  165.8 7.9 %reshape.168 = f32[512,2048]{1,0:T(8,128)} reshape(f32[4,128,32,64]{3,2,1,0:T(8,128)} %copy.77) | data formatting | bytes 8388608 | tf_op jit(solution)/shard_map/reshape | solution.py:118
  173.7 6.5 %multiply_reduce_fusion.1 = (f32[512]{0:T(512)S(1)}, bf16[512,2048]{1,0:T(8,128)(2,1)S(1)}) fusion(f32[512,2048]{1,0:T(8,128)} %reshape.168, bf16[1024,2048]{1,0:T(8,128)(2,1)} %param.32, bf16[1,512,1024]{2,1,0:T(8,128)(2,1)S(1)} %copy-done.9, f32[1024]{0:T(1024)S(1)} %copy-done.22, f32[512]{0:T(512)S(1)} %copy-done.15), kind=kOutput, calls=%fused_computation.39 | convolution fusion | flops 2159017472 | bytes 11542528 | tf_op jit(solution)/shard_map/dot_general | solution.py:71
  185.8 56.9 %all-reduce.4.cloned.1.call-done = bf16[32,1024]{1,0:T(8,128)(2,1)} async-done(((bf16[32,1024]{1,0:T(8,128)(2,1)}), bf16[32,1024]{1,0:T(8,128)(2,1)}) %all-reduce.4.cloned.1.call-update) | async-done | bytes 65552
  244.8 68.0 %all-reduce = s32[512]{0:T(512)S(1)} all-reduce(s32[512]{0:T(512)S(1)} %bitcast_dynamic-update-slice_fusion.1), channel_id=4, replica_groups=mesh['seq'=8,'cand'=16] {'seq','cand'}, use_global_device_ids=true, to_apply=%add | all-reduce | flops 512 | bytes 4096
  314.2 7.1 %multiply_reduce_fusion = (f32[512]{0:T(512)S(1)}, f32[512,4096]{1,0:T(8,128)S(1)}) fusion(f32[512]{0:T(512)S(1)} %select_reduce_fusion.1, bf16[512,1024]{1,0:T(8,128)(2,1)S(1)} %reshape.151, bf16[4096,1024]{1,0:T(8,128)(2,1)} %param.27), kind=kOutput, calls=%fused_computation.16 | convolution fusion | flops 4299161088 | bytes 17829888 | tf_op jit(solution)/shard_map/dot_general | solution.py:144
  324.5 55.4 %all-gather.6 = f32[128,1,512]{2,1,0:T(1,128)S(1)} all-gather(f32[1,1,512]{2,1,0:T(1,128)S(1)} %bitcast.122), channel_id=3, replica_groups=mesh['seq'=8,'cand'=16] {'seq','cand'}, dimensions={0}, use_global_device_ids=true | all-gather | bytes 264192 | tf_op jit(solution)/shard_map/all_gather | solution.py:20
  379.9 55.7 %all-gather.7 = f32[128,1,512]{2,1,0:T(1,128)S(1)} all-gather(f32[1,1,512]{2,1,0:T(1,128)S(1)} %bitcast.121), channel_id=5, replica_groups=mesh['seq'=8,'cand'=16] {'seq','cand'}, dimensions={0}, use_global_device_ids=true | all-gather | bytes 264192 | tf_op jit(solution)/shard_map/all_gather | solution.py:20
  435.6 55.7 %all-gather.5 = f32[128,1,512]{2,1,0:T(1,128)S(1)} all-gather(f32[1,1,512]{2,1,0:T(1,128)S(1)} %bitcast.120), channel_id=2, replica_groups=mesh['seq'=8,'cand'=16] {'seq','cand'}, dimensions={0}, use_global_device_ids=true | all-gather | bytes 264192 | tf_op jit(solution)/shard_map/all_gather | solution.py:20
  491.4 11.8 %while.32 = (s32[]{:T(128)}, f32[512]{0:T(512)S(1)}, f32[512]{0:T(512)S(1)}, f32[512]{0:T(512)S(1)}, f32[128,512]{1,0:T(8,128)S(1)}, /*index=5*/f32[128,512]{1,0...) while((s32[]{:T(128)}, f32[512]{0:T(512)S(1)}, f32[512]{0:T(512)S(1)}, ...), condition=%wide.region_14.15_spmd, body=%wide.region_13.14_spmd.sunk | while | flops 3589 | bytes 30871 | solution.py:26
  (653 shorter events, 74.0 us)
Async XLA Ops:
  7.2 12.9 %copy-start = (bf16[1024,32]{0,1:T(8,128)(2,1)S(1)}, bf16[1024,32]{0,1:T(8,128)(2,1)}, u32[]{:S(2)}) copy-start(bf16[1024,32]{0,1:T(8,128)(2,1)} %param.33) | copy-start | bytes 196612
  7.2 235.5 %all-reduce.4.cloned.1.call-start = ((), (), s32[]{:S(2)}) async-start(), calls=%async_computation.1 | async-start | bytes 131072
  8.7 11.3 %copy-start.14 = (f32[512]{0:T(512)}, f32[512]{0:T(512)S(1)}, u32[]{:S(2)}) copy-start(f32[512]{0:T(512)S(1)} %add_rsqrt_fusion.2) | copy-start | bytes 6148
  8.8 11.3 %copy-start.8 = (bf16[1,512,1024]{2,1,0:T(8,128)(2,1)S(1)}, bf16[1,512,1024]{2,1,0:T(8,128)(2,1)}, u32[]{:S(2)}) copy-start(bf16[1,512,1024]{2,1,0:T(8,128)(2,1)} %param.23) | copy-start | bytes 3145732
  8.8 11.3 %copy-start.21 = (f32[1024]{0:T(1024)S(1)}, f32[1024]{0:T(1024)}, u32[]{:S(2)}) copy-start(f32[1024]{0:T(1024)} %param.30) | copy-start | bytes 12292
  8.8 11.3 %copy-start.25 = (f32[32]{0:T(128)S(1)}, f32[32]{0:T(128)}, u32[]{:S(2)}) copy-start(f32[32]{0:T(128)} %param.36) | copy-start | bytes 388
  14.8 12.7 %collective-permute-start = (bf16[3,2304]{1,0:T(4,128)(2,1)}, bf16[3,2304]{1,0:T(4,128)(2,1)}, u32[]{:S(2)}, u32[]{:S(2)}) collective-permute-start(bf16[3,2304]{1,0:T(4,128)(2,1)} %slice.74), channel_id=1, source_target_pairs={{0,16},{16,32},{32,48},{48,64},{64,80},{80,96},{96,112},{1,17},{17... | collective-permute-start | bytes 41480 | tf_op jit(solution)/shard_map/ppermute | solution.py:16
  53.2 12.5 %copy-start.17 = (f32[32]{0:T(128)S(1)}, f32[32]{0:T(128)}, u32[]{:S(2)}) copy-start(f32[32]{0:T(128)} %get-tuple-element.273) | copy-start | bytes 388
  65.9 8.0 %collective-permute-start.1 = (bf16[32,64,128]{2,1,0:T(8,128)(2,1)S(1)}, bf16[32,64,128]{2,1,0:T(8,128)(2,1)S(1)}, u32[]{:S(2)}, u32[]{:S(2)}) collective-permute-start(bf16[32,64,128]{2,1,0:T(8,128)(2,1)S(1)} %add_convert_fusion.6), channel_id=1, source_target_pairs={{0,16},{16,32},{32,48},{48,64},{64,80},{80,96},{96,112},{1,17},{17... | collective-permute-start | bytes 1572872 | tf_op jit(solution)/shard_map/ppermute | solution.py:16
  73.9 47.5 %copy-start.5 = (f32[4,128,32]{2,1,0:T(8,128)S(1)}, f32[4,128,32]{2,1,0:T(8,128)}, u32[]{:S(2)}) copy-start(f32[4,128,32]{2,1,0:T(8,128)} %copy-done.4) | copy-start | bytes 196612
  73.9 47.6 %copy-start.7 = (f32[4,128,32]{2,1,0:T(8,128)S(1)}, f32[4,128,32]{2,1,0:T(8,128)}, u32[]{:S(2)}) copy-start(f32[4,128,32]{2,1,0:T(8,128)} %get-tuple-element.269) | copy-start | bytes 196612
  73.9 47.7 %copy-start.6 = (f32[4,128,32]{2,1,0:T(8,128)S(1)}, f32[4,128,32]{2,1,0:T(8,128)}, u32[]{:S(2)}) copy-start(f32[4,128,32]{2,1,0:T(8,128)} %get-tuple-element.270) | copy-start | bytes 196612
  74.1 10.6 %collective-permute-start.2 = (bf16[32,64,128]{2,1,0:T(8,128)(2,1)S(1)}, bf16[32,64,128]{2,1,0:T(8,128)(2,1)S(1)}, u32[]{:S(2)}, u32[]{:S(2)}) collective-permute-start(bf16[32,64,128]{2,1,0:T(8,128)(2,1)S(1)} %add_convert_fusion.5), channel_id=1, source_target_pairs={{0,16},{16,32},{32,48},{48,64},{64,80},{80,96},{96,112},{1,17},{17... | collective-permute-start | bytes 1572872 | tf_op jit(solution)/shard_map/ppermute | solution.py:16
  85.0 10.5 %collective-permute-start.3 = (bf16[32,64,128]{2,1,0:T(8,128)(2,1)S(1)}, bf16[32,64,128]{2,1,0:T(8,128)(2,1)S(1)}, u32[]{:S(2)}, u32[]{:S(2)}) collective-permute-start(bf16[32,64,128]{2,1,0:T(8,128)(2,1)S(1)} %add_convert_fusion.4), channel_id=1, source_target_pairs={{0,16},{16,32},{32,48},{48,64},{64,80},{80,96},{96,112},{1,17},{17... | collective-permute-start | bytes 1572872 | tf_op jit(solution)/shard_map/ppermute | solution.py:16
  95.7 10.5 %collective-permute-start.4 = (bf16[32,64,128]{2,1,0:T(8,128)(2,1)S(1)}, bf16[32,64,128]{2,1,0:T(8,128)(2,1)S(1)}, u32[]{:S(2)}, u32[]{:S(2)}) collective-permute-start(bf16[32,64,128]{2,1,0:T(8,128)(2,1)S(1)} %add_convert_fusion.3), channel_id=1, source_target_pairs={{0,16},{16,32},{32,48},{48,64},{64,80},{80,96},{96,112},{1,17},{17... | collective-permute-start | bytes 1572872 | tf_op jit(solution)/shard_map/ppermute | solution.py:16
  106.4 15.4 %collective-permute-start.5 = (bf16[32,64,128]{2,1,0:T(8,128)(2,1)S(1)}, bf16[32,64,128]{2,1,0:T(8,128)(2,1)S(1)}, u32[]{:S(2)}, u32[]{:S(2)}) collective-permute-start(bf16[32,64,128]{2,1,0:T(8,128)(2,1)S(1)} %add_convert_fusion.2), channel_id=1, source_target_pairs={{0,16},{16,32},{32,48},{48,64},{64,80},{80,96},{96,112},{1,17},{17... | collective-permute-start | bytes 1572872 | tf_op jit(solution)/shard_map/ppermute | solution.py:16
  122.0 8.0 %collective-permute-start.6 = (bf16[32,64,128]{2,1,0:T(8,128)(2,1)S(1)}, bf16[32,64,128]{2,1,0:T(8,128)(2,1)S(1)}, u32[]{:S(2)}, u32[]{:S(2)}) collective-permute-start(bf16[32,64,128]{2,1,0:T(8,128)(2,1)S(1)} %add_convert_fusion.1), channel_id=1, source_target_pairs={{0,16},{16,32},{32,48},{48,64},{64,80},{80,96},{96,112},{1,17},{17... | collective-permute-start | bytes 1572872 | tf_op jit(solution)/shard_map/ppermute | solution.py:16
  130.2 21.4 %copy-start.16 = (f32[32]{0:T(128)S(1)}, f32[32]{0:T(128)}, u32[]{:S(2)}) copy-start(f32[32]{0:T(128)} %param.38) | copy-start | bytes 388
  130.3 21.4 %collective-permute-start.7 = (bf16[32,64,128]{2,1,0:T(8,128)(2,1)S(1)}, bf16[32,64,128]{2,1,0:T(8,128)(2,1)S(1)}, u32[]{:S(2)}, u32[]{:S(2)}) collective-permute-start(bf16[32,64,128]{2,1,0:T(8,128)(2,1)S(1)} %add_convert_fusion), channel_id=1, source_target_pairs={{0,16},{16,32},{32,48},{48,64},{64,80},{80,96},{96,112},{1,17},{17... | collective-permute-start | bytes 1572872 | tf_op jit(solution)/shard_map/ppermute | solution.py:16
  180.3 64.4 %copy-start.27 = (s32[1,4]{1,0:T(1,128)S(1)}, s32[1,4]{1,0:T(1,128)}, u32[]{:S(2)}) copy-start(s32[1,4]{1,0:T(1,128)} %param.26) | copy-start | bytes 52
  180.4 132.4 %copy-start.18 = (f32[16]{0:T(128)S(1)}, f32[16]{0:T(128)}, u32[]{:S(2)}) copy-start(f32[16]{0:T(128)} %param.29) | copy-start | bytes 196
  183.3 138.1 %copy-start.28 = (bf16[512,1024]{1,0:T(8,128)(2,1)}, bf16[512,1024]{1,0:T(8,128)(2,1)S(1)}, u32[]{:S(2)}) copy-start(bf16[512,1024]{1,0:T(8,128)(2,1)S(1)} %get-tuple-element.279) | copy-start | bytes 3145732
  184.5 128.4 %all-gather.10.cloned.1.call-start = ((), (), s32[]{:S(2)}) async-start(), calls=%async_computation | async-start | bytes 1056768 | tf_op jit(solution)/shard_map/all_gather | solution.py:138
  321.4 182.4 %copy-start.1 = (bf16[1024,32]{0,1:T(8,128)(2,1)S(1)}, bf16[1024,32]{0,1:T(8,128)(2,1)}, u32[]{:S(2)}) copy-start(bf16[1024,32]{0,1:T(8,128)(2,1)} %param.33) | copy-start | bytes 196612
  (16 other events, 84.9 us)
Sparse Core Ops, SparseCore 0:
  184.6 58.0 all-reduce.3
  245.9 65.2 all-gather.9
where the time goes:
time: 519 us; the launch traced here: 511 us
  blocking collectives  235 us (45%)
  waiting for transfers between devices  81.4 us (16%)
  matrix products  57.5 us (11%)
  local copies, waits for them, and re-layouts  44.8 us (9%)
  starting transfers between devices  41.1 us (8%)
  other arithmetic  29.3 us (6%)
  between operations  17.2 us (3%)
    all_gather x3, blocking collectives, joined(): everything = jax.tree.map(lambda part: lax.all_gather(part, axis), shard)  167 us
    unnamed x1, blocking collectives  68 us
    unnamed x3, waiting for transfers between devices  57 us
    ppermute x8, starting transfers between devices, shifted(): return lax.ppermute(block, axis, route)  41 us
    ppermute x8, waiting for transfers between devices, shifted(): return lax.ppermute(block, axis, route)  24.4 us
    reshape x2, local copies, waits for them, and re-layouts, local(): y = (y_in + y_st + y_enter + d_skip[:, None] * xh).reshape(seq_len, inner)  17 us
    dot_general x1, matrix products, local(): y_in = jnp.einsum('chij,cjhp->cihp', weights, xh, precision=HIGH)  17 us
  transfers between devices with their start and end apart: 10, of which 5 were waited for; matrix products, arithmetic and copies ran while one was open for 6% of the time, Pallas kernels for 0%

commit v1 on v0

v1 whole, which is shorter than its diff:
```python
import functools

import jax
import jax.numpy as jnp
from jax import lax
from jax.experimental import pallas as pl
from jax.experimental.pallas import tpu as pltpu
from jax.sharding import PartitionSpec as P

GROUP = 128
EPS = 1e-05
BLK = 256
HALO = 16
BF = jnp.bfloat16
F32 = jnp.float32
VMEM_LIMIT = 56 * 1024 * 1024


def rms(v, gain):
    return v * lax.rsqrt(jnp.mean(v * v, axis=-1, keepdims=True) + EPS) * gain


def silu(v):
    half = 0.5 * v
    return half + half * jnp.tanh(half)


def four(v):
    return jnp.concatenate([v, v, v, v], axis=1)


def lane_group(shape):
    return lax.broadcasted_iota(jnp.int32, shape, 1) // 32


def packed(v, parts):
    group = lane_group(v.shape)
    rest = v
    out = jnp.zeros_like(v)
    for part in range(parts):
        piece = rest.astype(BF).astype(F32)
        out = jnp.where(group == part, piece, out)
        rest = rest - piece
    return out.astype(BF)


def expander(first_head, heads, lanes, parts):
    shape = (128, heads * lanes)
    row = lax.broadcasted_iota(jnp.int32, shape, 0)
    col = lax.broadcasted_iota(jnp.int32, shape, 1)
    return ((row % 32 == first_head + col // lanes) & (row < 32 * parts)).astype(BF)


def dot(a, b):
    return jnp.dot(a, b, preferred_element_type=F32)


def dot_nt(a, b):
    return lax.dot_general(a, b, (((1,), (1,)), ((), ())), preferred_element_type=F32)


def gate_kernel(meta, ev, gain, w_z, w_dt, dt_bias, a_log, normed, z, cum_out, cum_t, packs):
    rows = ev.shape[0]

    @pl.when(pl.program_id(0) == 0)
    def _():
        normed[...] = rms(ev[...].astype(F32), gain[...]).astype(BF)
        raw = dot(normed[...], four(w_dt[...]))
        place = meta[0] * rows + lax.broadcasted_iota(jnp.int32, (rows, 128), 0)
        v = raw + four(dt_bias[...])
        soft = jnp.maximum(v, 0.0) + jnp.log1p(jnp.exp(-jnp.abs(v)))
        step = jnp.where(place < meta[1], soft, 0.0)
        logdec = -step * jnp.exp(four(a_log[...]))
        tri = (
            lax.broadcasted_iota(jnp.int32, (rows, rows), 0)
            >= lax.broadcasted_iota(jnp.int32, (rows, rows), 1)
        ).astype(BF)
        cum = dot(tri, packed(logdec, 3))
        cum = cum + pltpu.roll(cum, 32, 1)
        cum = cum + pltpu.roll(cum, 64, 1)
        cum_out[...] = packed(cum, 3)
        flipped = jnp.transpose(cum)
        for g in range(8):
            cum_t[g] = flipped[4 * g : 4 * g + 4]
        packs[0] = packed(step, 2)
        packs[1] = packed(jnp.exp(cum[rows - 1 :] - cum) * step, 2)
        packs[4] = packed(jnp.exp(cum), 2)
        for c in range(rows // GROUP):
            lo, hi = c * GROUP, (c + 1) * GROUP
            own = cum[lo:hi]
            packs[2, lo:hi] = packed(jnp.exp(cum[hi - 1 : hi] - own) * step[lo:hi], 2)
            start = cum[lo - 1 : lo] if c else 0.0
            packs[3, lo:hi] = packed(jnp.exp(own - start), 2)

    z[...] = dot(normed[...], w_z[...]).astype(BF)


def xbc_kernel(meta, normed, halo, gain, w, conv_w, conv_b, packs, x, bc, keep, send, full, raw, b_t):
    g = pl.program_id(0)
    rows = normed.shape[0]

    @pl.when(g == 0)
    def _():
        full[:HALO] = rms(halo[...].astype(F32), gain[...]).astype(BF)
        full[HALO:] = normed[...]

    raw[...] = dot(full[...], w[...]).astype(BF).astype(F32)
    conv = conv_b[...]
    for k in range(4):
        conv = conv + conv_w[k : k + 1] * raw[HALO - 3 + k : HALO - 3 + k + rows]
    act = silu(conv)

    @pl.when(g == 0)
    def _():
        bc[...] = act.astype(BF)
        b_t[...] = jnp.transpose(act[:, :128]).astype(BF)

    def state(out):
        blk = meta[3] ^ 4 if out is send else meta[3]
        first = (blk + (g - 1) % 4) * 4
        spread = expander(first, 4, 64, 2)
        weighted = (act * dot(packs[0], spread)).astype(BF)
        out[:128] = dot(b_t[...], weighted).astype(BF)
        whole = dot(packs[1, rows - 16 :], spread)
        out[128:] = jnp.broadcast_to(whole[15:], (16, BLK)).astype(BF)

    @pl.when(g > 0)
    def _():
        x[...] = act.astype(BF)

    @pl.when((g > 0) & (g < 5))
    def _():
        state(send)

    @pl.when(g >= 5)
    def _():
        state(keep)


def scan_kernel(x, bc, cum, cum_t, packs, d_skip, y, scores, b_t):
    g = pl.program_id(0)
    rows = x.shape[0]
    chunks = rows // GROUP

    @pl.when(g == 0)
    def _():
        lower = lax.broadcasted_iota(jnp.int32, (GROUP, GROUP), 0) >= lax.broadcasted_iota(
            jnp.int32, (GROUP, GROUP), 1
        )
        for c in range(chunks):
            part = slice(c * GROUP, (c + 1) * GROUP)
            scores[c] = jnp.where(lower, dot_nt(bc[part, 128:], bc[part, :128]), 0.0)
        b_t[...] = jnp.transpose(bc[:, :128].astype(F32)).astype(BF)

    spread = expander(4 * g, 4, 64, 2)
    wide = expander(4 * g, 4, GROUP, 3)
    skip = dot(packed(jnp.broadcast_to(four(d_skip[...]), (16, 128)), 2), spread)[:1]
    left = lax.broadcasted_iota(jnp.int32, (GROUP, 128), 1) < 64
    before = jnp.zeros((128, BLK), F32)
    for c in range(chunks):
        part = slice(c * GROUP, (c + 1) * GROUP)
        xc = x[part].astype(F32)
        stepped = xc * dot(packs[0, part], spread)
        tailed = (xc * dot(packs[2, part], spread)).astype(BF)
        inner = dot(packs[3, part], spread)
        own = dot(cum[part], wide)
        out = xc * skip
        if c:
            out = out + dot(bc[part, 128:], before.astype(BF)) * inner
        pairs = []
        for p in range(2):
            weights = []
            for h in (2 * p, 2 * p + 1):
                diff = own[:, h * GROUP : (h + 1) * GROUP] - cum_t[0, h : h + 1, part]
                weights.append((scores[c] * jnp.exp(jnp.minimum(diff, 0.0))).astype(BF))
            pair = stepped[:, p * 128 : (p + 1) * 128]
            stacked = jnp.concatenate(
                [jnp.where(left, pair, 0.0), jnp.where(left, 0.0, pair)], axis=0
            ).astype(BF)
            pairs.append(dot(jnp.concatenate(weights, axis=1), stacked))
        y[part] = (out + jnp.concatenate(pairs, axis=1)).astype(BF)
        if c < chunks - 1:
            before = before * inner[GROUP - 1 :] + dot(b_t[:, part], tailed)


def out_kernel(meta, y, bc, kept, got, packs, z, ev, norm_gain, w_out, final_gain, wanted, out, rows_out):
    i = pl.program_id(0)
    rows = y.shape[0]
    half = kept.shape[1]
    core = meta[2]
    mine, other = kept[...], got[...]
    entering = [jnp.where(core == 0, mine, other), jnp.where(core == 0, other, mine)]
    gated = []
    square = jnp.zeros((rows, 128), F32)
    for b in range(2 * half // BLK):
        cols = slice(b * BLK, (b + 1) * BLK)
        at = b * BLK % half
        e = entering[b * BLK // half][:128, at : at + BLK]
        add = dot(bc[:, 128:], e) * dot(packs[0], expander(4 * b, 4, 64, 2))
        v = (y[:, cols].astype(F32) + add) * silu(z[:, cols].astype(F32))
        sq = v * v
        square = square + sq[:, :128] + sq[:, 128:]
        gated.append(v)
    scale = lax.rsqrt(jnp.sum(square, axis=1, keepdims=True) * (1.0 / (2 * half)) + EPS)
    mixed = jnp.concatenate(
        [
            (gated[b] * scale * norm_gain[:, b * BLK : (b + 1) * BLK]).astype(BF)
            for b in range(2 * half // BLK)
        ],
        axis=1,
    )
    res = (ev[...].astype(F32) + dot(mixed, w_out[...])).astype(BF)
    out[...] = res
    final = rms(res.astype(F32), final_gain[...]).astype(BF)
    first = (meta[0] * pl.num_programs(0) + i) * rows
    place = first + lax.broadcasted_iota(jnp.int32, (32, rows), 1)
    pick = dot((place == wanted[...]).astype(BF), final)

    @pl.when(i == 0)
    def _():
        rows_out[...] = jnp.zeros_like(rows_out)

    for k in range(4):
        cols = slice(k * 1024, (k + 1) * 1024)
        rows_out[:, cols] = rows_out[:, cols] + pick[8 * k : 8 * k + 8]


def logit_kernel(meta, own, got, items, scale, stats, rows_all, ids, top, total, hit):
    step = pl.program_id(0)
    block = items.shape[0]
    count = own.shape[0]

    @pl.when(step == 0)
    def _():
        core = meta[2]
        for k in range(4):
            cols = slice(k * 1024, (k + 1) * 1024)
            mine, other = own[:, cols], got[:, cols]
            rows_all[2 * k * count : (2 * k + 1) * count] = jnp.where(core == 0, mine, other)
            rows_all[(2 * k + 1) * count : (2 * k + 2) * count] = jnp.where(core == 0, other, mine)
        mine, other = own[:, 4 * 1024 :].astype(F32), got[:, 4 * 1024 :].astype(F32)
        digits = jnp.concatenate(
            [jnp.where(core == 0, mine, other), jnp.where(core == 0, other, mine)], axis=0
        )
        digits = jnp.transpose(digits)
        lines = digits[:4] * 65536.0 + digits[4:8] * 256.0 + digits[8:12]
        for k in range(4):
            ids[:, k * 128 : (k + 1) * 128] = lines[k : k + 1].astype(jnp.int32)
        top[...] = jnp.full_like(top, -1e30)
        total[...] = jnp.zeros_like(total)
        hit[...] = jnp.zeros_like(hit)

    logit = dot_nt(items[...], rows_all[...]) * scale[...]
    place = lax.broadcasted_iota(jnp.int32, logit.shape, 0)
    at = ids[...] - (meta[4] * (pl.num_programs(0) * block) + step * block)
    hit[...] += jnp.sum(jnp.where(place == at, logit, 0.0), axis=0, keepdims=True)
    new = jnp.maximum(top[...], jnp.max(logit, axis=0, keepdims=True))
    total[...] = total[...] * jnp.exp(top[...] - new) + jnp.sum(
        jnp.exp(logit - new), axis=0, keepdims=True
    )
    top[...] = new

    @pl.when(step == pl.num_programs(0) - 1)
    def _():
        lines = [
            ref[:, k * 128 : (k + 1) * 128] for ref in (top, total, hit) for k in range(4)
        ]
        lines = jnp.concatenate(lines + [jnp.zeros((116, 128), F32)], axis=0)
        stats[...] = jnp.transpose(lines)[:, :16]


def call(kernel, grid, in_specs, out_specs, out_shape, scratch, flops, nbytes):
    return pl.pallas_call(
        kernel,
        grid_spec=pltpu.PrefetchScalarGridSpec(
            num_scalar_prefetch=1,
            grid=(grid,),
            in_specs=in_specs,
            out_specs=out_specs,
            scratch_shapes=scratch,
        ),
        out_shape=out_shape,
        compiler_params=pltpu.CompilerParams(vmem_limit_bytes=VMEM_LIMIT),
        cost_estimate=pl.CostEstimate(flops=flops, bytes_accessed=nbytes, transcendentals=0),
    )


def whole(*shape):
    return pl.BlockSpec(shape, lambda *_: (0,) * len(shape))


def joined(first, second):
    decay = second[128:129]
    return jnp.concatenate([first[:128] * decay + second[:128], first[128:] * second[128:]], axis=0)


def local(
    events, lengths, target_pos, target_ids, items, item_block, temper, in_gain, w_xbc, w_z, w_dt,
    conv_w, conv_b, dt_bias, a_log, d_skip, norm_gain, w_out, final_gain,
):
    rows, width = events.shape[1:]
    inner = w_z.shape[1]
    ev = events[0]
    x_at, core, seq = lax.axis_index("x"), lax.axis_index("core"), lax.axis_index(("x", "core"))
    meta = jnp.stack([seq, lengths[0], core, core * 4, item_block[0]]).astype(jnp.int32)
    order = ("core", "x", "cand")

    with jax.named_scope("halo"):
        halo = lax.ppermute(ev[rows - HALO :], ("x", "core"), [(i, i + 1) for i in range(7)])
    with jax.named_scope("ids"):
        digits = jnp.concatenate([target_ids // 65536, target_ids // 256 % 256, target_ids % 256], axis=1)
        digits = jnp.pad(digits, ((0, 0), (0, 116))).astype(BF)
        scale = jnp.broadcast_to(temper[None, :], (32, 16)).reshape(1, 512)

    with jax.named_scope("gate"):
        normed, z, cum, cum_t, packs = call(
            gate_kernel, 4,
            [
                whole(rows, width), whole(1, width),
                pl.BlockSpec((width, inner // 4), lambda g, m: (0, g)),
                whole(width, 32), whole(1, 32), whole(1, 32),
            ],
            [
                whole(rows, width), pl.BlockSpec((rows, inner // 4), lambda g, m: (0, g)),
                whole(rows, 128), whole(8, 4, rows), whole(5, rows, 128),
            ],
            [
                jax.ShapeDtypeStruct((rows, width), BF), jax.ShapeDtypeStruct((rows, inner), BF),
                jax.ShapeDtypeStruct((rows, 128), BF), jax.ShapeDtypeStruct((8, 4, rows), F32),
                jax.ShapeDtypeStruct((5, rows, 128), BF),
            ],
            [], 2 * rows * width * inner, 2 * width * inner + 8 * rows * inner,
        )(meta, ev, in_gain[None], w_z, w_dt, dt_bias[None], a_log[None])

    def column(g, m):
        return jnp.where(g == 0, 8, jnp.where(g < 5, (m[3] ^ 4) + g - 1, m[3] + g - 5))

    with jax.named_scope("xbc"):
        x, bc, keep, send = call(
            xbc_kernel, 9,
            [
                whole(rows, width), whole(HALO, width), whole(1, width),
                pl.BlockSpec((width, BLK), lambda g, m: (0, column(g, m))),
                pl.BlockSpec((4, BLK), lambda g, m: (0, column(g, m))),
                pl.BlockSpec((1, BLK), lambda g, m: (0, column(g, m))),
                whole(2, rows, 128),
            ],
            [
                pl.BlockSpec((rows, BLK), lambda g, m: (0, column(jnp.maximum(g, 1), m))),
                whole(rows, 256),
                pl.BlockSpec((144, BLK), lambda g, m: (0, jnp.maximum(g - 5, 0))),
                pl.BlockSpec((144, BLK), lambda g, m: (0, jnp.clip(g - 1, 0, 3))),
            ],
            [
                jax.ShapeDtypeStruct((rows, inner), BF), jax.ShapeDtypeStruct((rows, 256), BF),
                jax.ShapeDtypeStruct((144, inner // 2), BF), jax.ShapeDtypeStruct((144, inner // 2), BF),
            ],
            [
                pltpu.VMEM((rows + HALO, width), BF), pltpu.VMEM((rows + HALO, BLK), F32),
                pltpu.VMEM((128, rows), BF),
            ],
            2 * rows * width * 2304, 2 * width * 2304 + 4 * rows * inner,
        )(meta, normed, halo, in_gain[None], w_xbc, conv_w, conv_b[None], packs[jnp.array([1, 4])])

    swap = [(0, 1), (1, 0)]
    with jax.named_scope("states"):
        got = lax.ppermute(send, "core", swap).astype(F32)
        own = keep.astype(F32)
        first = jnp.where(core == 0, own, got)
        chip = joined(first, jnp.where(core == 0, got, own))
        near = lax.ppermute(chip.astype(BF), "x", [(0, 1), (1, 0), (2, 3), (3, 2)]).astype(F32)
        odd = x_at % 2 == 1
        pair = joined(jnp.where(odd, near, chip), jnp.where(odd, chip, near))
        far = lax.ppermute(pair.astype(BF), "x", [(1, 2), (0, 3)]).astype(F32)[:128]
        enter = jnp.where(odd, near[:128] + near[128:129] * far, far)
        later = first[:128] + first[128:129] * enter
        here = jnp.where(core == 0, enter, later).astype(BF)
        there = lax.ppermute(jnp.where(core == 0, later, enter).astype(BF), "core", swap)

    with jax.named_scope("scan"):
        y = call(
            scan_kernel_meta, inner // BLK,
            [
                pl.BlockSpec((rows, BLK), lambda g, m: (0, g)), whole(rows, 256), whole(rows, 128),
                pl.BlockSpec((1, 4, rows), lambda g, m: (g, 0, 0)), whole(5, rows, 128), whole(1, 32),
            ],
            pl.BlockSpec((rows, BLK), lambda g, m: (0, g)),
            jax.ShapeDtypeStruct((rows, inner), BF),
            [pltpu.VMEM((rows // GROUP, GROUP, GROUP), F32), pltpu.VMEM((128, rows), BF)],
            8 * rows * 128 * inner, 4 * rows * inner,
        )(meta, x, bc, cum, cum_t, packs, d_skip[None])

    part = 128
    with jax.named_scope("out"):
        out, picked = call(
            out_kernel, rows // part,
            [
                pl.BlockSpec((part, inner), lambda i, m: (i, 0)),
                pl.BlockSpec((part, 256), lambda i, m: (i, 0)),
                whole(128, inner // 2), whole(128, inner // 2),
                pl.BlockSpec((1, part, 128), lambda i, m: (4, i, 0)),
                pl.BlockSpec((part, inner), lambda i, m: (i, 0)),
                pl.BlockSpec((part, width), lambda i, m: (i, 0)),
                whole(1, inner), whole(inner, width), whole(1, width), whole(32, 1),
            ],
            [pl.BlockSpec((part, width), lambda i, m: (i, 0)), whole(8, 4 * width)],
            [jax.ShapeDtypeStruct((rows, width), BF), jax.ShapeDtypeStruct((8, 4 * width), F32)],
            [], 2 * rows * inner * (width + 128), 2 * inner * width + 6 * rows * inner,
        )(
            meta, y, bc, here, there, packs, z, ev, norm_gain[None], w_out, final_gain[None],
            jnp.transpose(target_pos.reshape(8, 4)).reshape(32, 1),
        )

    with jax.named_scope("rows"):
        mine = lax.all_to_all(picked.astype(BF), ("x", "core"), 0, 0, tiled=True)
        mine = jnp.sum(mine.astype(F32), axis=0, keepdims=True).astype(BF)
        mine = jnp.concatenate([mine, digits], axis=1)
        own_rows = lax.all_to_all(
            jnp.broadcast_to(mine, (64, mine.shape[1])), ("x", "cand"), 0, 0, tiled=True
        )
        got_rows = lax.ppermute(own_rows, "core", swap)

    steps = 8
    block = items.shape[0] // steps
    with jax.named_scope("logits"):
        stats = call(
            logit_kernel, steps,
            [
                whole(64, 4 * width + 128), whole(64, 4 * width + 128),
                pl.BlockSpec((block, width), lambda g, m: (g, 0)), whole(1, 512),
            ],
            whole(128, 16),
            jax.ShapeDtypeStruct((128, 16), F32),
            [pltpu.VMEM((512, width), BF), pltpu.VMEM((1, 512), jnp.int32)]
            + [pltpu.VMEM((1, 512), F32)] * 3,
            2 * 512 * items.shape[0] * width, 2 * items.shape[0] * width,
        )(meta, own_rows, got_rows, items, scale)

    with jax.named_scope("loss"):
        seen = lax.all_to_all(stats, order, 0, 0, tiled=True)
        top, total, hit = seen[:, 0:4], seen[:, 4:8], seen[:, 8:12]
        peak = jnp.max(top, axis=0)
        loss = peak + jnp.log(jnp.sum(total * jnp.exp(top - peak), axis=0)) - jnp.sum(hit, axis=0)
    return (out[None], loss)


def scan_kernel_meta(meta, *refs):
    scan_kernel(*refs)


def solution(mesh):
    fine = jax.sharding.Mesh(
        mesh.devices.reshape(mesh.shape["seq"] // 2, 2, mesh.shape["cand"]), ("x", "core", "cand")
    )
    seq = ("x", "core")
    each = ("x", "core", "cand")
    placed = (
        P("cand", seq, None),
        P("cand"),
        P("cand", None),
        P("cand", seq),
        P(each, None),
        P(each),
    ) + (P(),) * 13
    return jax.shard_map(
        local,
        mesh=fine,
        in_specs=placed,
        out_specs=(P("cand", seq, None), P(each)),
        check_vma=False,
    )
```

time: 519 us -> 155 us (0.30); the launches traced: 511 us -> 154 us
  blocking collectives: 235 us -> 34.3 us
  waiting for transfers between devices: 81.4 us -> 17.9 us
  Pallas kernels: 0 us -> 58.8 us
  matrix products: 57.5 us -> 0 us
  local copies, waits for them, and re-layouts: 44.8 us -> 13.2 us
  starting transfers between devices: 41.1 us -> 18.7 us
  other arithmetic: 29.3 us -> 9.49 us
  between operations: 17.2 us -> 2.18 us
    all_gather x3 -> x0, blocking collectives: 167 us -> none  [joined(): everything = jax.tree.map(lambda part: lax.all_gather(part, axis), shard)]
    unnamed x1 -> x0, blocking collectives: 68 us -> none
    pallas_call x0 -> x5, Pallas kernels: none -> 58.8 us  [the longest x1 15.1 us: local(): call(xbc_kernel, 9, [whole(rows, width), whole(HALO, width), whole(1, wid...]
    dot_general x11 -> x0, matrix products: 57.5 us -> none  [the longest x1 17 us: local(): y_in = jnp.einsum('chij,cjhp->cihp', weights, xh, precision=HIGH)]
    unnamed x3 -> x0, waiting for transfers between devices: 57 us -> none
    all_to_all x0 -> x2, blocking collectives: none -> 34.3 us  [the longest x1 20.9 us: local(): lax.all_to_all(jnp.broadcast_to(mine, (64, mine.shape[1])), ('x', 'cand')...]
    ppermute x8 -> x6, starting transfers between devices: 41 us -> 13.6 us  [the longest x1 4.5 us: local(): lax.ppermute(ev[rows - HALO:], ('x', 'core'), [(i, i + 1) for i in range(...]
    reshape x6 -> x3, local copies, waits for them, and re-layouts: 23.5 us -> 1.42 us  [the longest x1 0.69 us: local(): jnp.transpose(target_pos.reshape(8, 4)).reshape(32, 1)]
  transfers between devices with their start and end apart: 10 -> 7, of which waited for: 5 -> 5; matrix products, arithmetic and copies ran while one was open for 6% -> 5% of each run, Pallas kernels for 0% -> 14%
where the time goes in v1:
time: 155 us; the launch traced here: 154 us
  Pallas kernels  58.8 us (38%)
  blocking collectives  34.3 us (22%)
  starting transfers between devices  18.7 us (12%)
  waiting for transfers between devices  17.9 us (12%)
  local copies, waits for them, and re-layouts  13.2 us (9%)
  other arithmetic  9.49 us (6%)
  between operations  2.18 us (1%)
    all_to_all x1, blocking collectives, local(): lax.all_to_all(jnp.broadcast_to(mine, (64, mine.shape[1])), ('x', 'cand')...  20.9 us
    pallas_call x1, Pallas kernels, local(): call(xbc_kernel, 9, [whole(rows, width), whole(HALO, width), whole(1, wid...  15.1 us
    all_to_all x1, blocking collectives, local(): seen = lax.all_to_all(stats, order, 0, 0, tiled=True)  13.4 us
    pallas_call x1, Pallas kernels, local(): call(scan_kernel_meta, inner // BLK, [pl.BlockSpec((rows, BLK), lambda g,...  12.4 us
    pallas_call x1, Pallas kernels, local(): call(logit_kernel, steps, [whole(64, 4 * width + 128), whole(64, 4 * widt...  11.8 us
    pallas_call x1, Pallas kernels, local(): call(out_kernel, rows // part, [pl.BlockSpec((part, inner), lambda i, m:...  10.7 us
    pallas_call x1, Pallas kernels, local(): call(gate_kernel, 4, [whole(rows, width), whole(1, width), pl.BlockSpec((...  8.77 us
    ppermute x1, waiting for transfers between devices, local(): lax.ppermute(chip.astype(BF), 'x', [(0, 1), (1, 0), (2, 3), (3, 2)])  7.25 us
  transfers between devices with their start and end apart: 7, of which 5 were waited for; matrix products, arithmetic and copies ran while one was open for 5% of the time, Pallas kernels for 14%

profile of v1, /device:TPU:1, one launch (start us, length us, event | category | flops | bytes accessed | tf_op | source)
XLA Modules:
  0.0 154.5 jit_solution(17345374857189682736)
XLA Ops:
  1.4 4.5 %collective-permute-start = (bf16[16,1024]{1,0:T(8,128)(2,1)S(1)}, bf16[16,1024]{1,0:T(8,128)(2,1)S(1)}, u32[]{:S(2)}, u32[]{:S(2)}) collective-permute-start(bf16[16,1024]{1,0:T(8,128)(2,1)S(1)} %slice_bitcast_fusion), channel_id=1, source_target_pairs={{0,16},{16,32},{32,48},{48,64},{64,80},{80,96},{96,112},{1,17},{17... | collective-permute-start | bytes 98312 | tf_op jit(solution)/shard_map/halo/ppermute | solution.py:309
  7.2 1.7 %copy.33.w_dt = bf16[1024,32]{1,0:T(8,128)(2,1)} copy(bf16[1024,32]{0,1:T(8,128)(2,1)} %param.30) | data formatting | bytes 131072 | tf_op args[10]
  9.6 8.8 %gate.1 = (bf16[512,1024]{1,0:T(8,128)(2,1)}, bf16[512,2048]{1,0:T(8,128)(2,1)}, bf16[512,128]{1,0:T(8,128)(2,1)}, f32[8,4,512]{2,1,0:T(4,128)}, bf16[5,512,128]{2,1,0:T(8,128)(2,1)}) custom-call(s32[5]{0:T(128)} %stack.15.meta, bf16[512,1024]{1,0:T(8,128)(2,1)} %bitcast.29, f32[1,1024]{1,0:T(1,128)} %bitcast.43, bf16[1024,2048]{1,0:T(8,128)(2,1)} %w_z.1, ...), custom_call_target="tpu_custom_call" | custom-call | flops 2147483648 | bytes 12582912 | tf_op jit(solution)/shard_map/gate/pallas_call | solution.py:316
  19.0 2.4 %gather_fusion = bf16[2,512,128]{2,1,0:T(8,128)(2,1)} fusion(bf16[5,512,128]{2,1,0:T(8,128)(2,1)} %get-tuple-element.14.refs_4_.packs, s32[1024]{0:T(1024)S(1)} %pad_clamp_fusion), kind=kCustom, calls=%fused_computation | custom fusion | bytes 524296 | tf_op jit(solution)/shard_map/xbc/gather | solution.py:363
  22.0 15.1 %xbc.1 = (bf16[512,2048]{1,0:T(8,128)(2,1)}, bf16[512,256]{1,0:T(8,128)(2,1)}, bf16[144,1024]{1,0:T(8,128)(2,1)}, bf16[144,1024]{1,0:T(8,128)(2,1)}) custom-call(s32[5]{0:T(128)} %stack.15.meta, bf16[512,1024]{1,0:T(8,128)(2,1)} %get-tuple-element.13.normed, bf16[16,1024]{1,0:T(8,128)(2,1)} %copy-done.7, f32[1,1024]{1,0:T(1,128)} %bitcast.44, ...), custom_call_target="tpu_custom_call" | custom-call | flops 2415919104 | bytes 8912896 | tf_op jit(solution)/shard_map/xbc/pallas_call | solution.py:339
  37.1 1.8 %collective-permute-done.1 = bf16[144,1024]{1,0:T(8,128)(2,1)S(1)} collective-permute-done((bf16[144,1024]{1,0:T(8,128)(2,1)}, bf16[144,1024]{1,0:T(8,128)(2,1)S(1)}, u32[]{:S(2)}, u32[]{:S(2)}) %collective-permute-start.1) | collective-permute-done | bytes 294944 | tf_op jit(solution)/shard_map/states/ppermute | solution.py:367
  38.9 1.1 convert_select_fusion
  40.2 1.3 collective-permute-start.2
  41.5 7.3 %collective-permute-done.2 = bf16[144,1024]{1,0:T(8,128)(2,1)S(1)} collective-permute-done((bf16[144,1024]{1,0:T(8,128)(2,1)S(1)}, bf16[144,1024]{1,0:T(8,128)(2,1)S(1)}, u32[]{:S(2)}, u32[]{:S(2)}) %collective-permute-start.2) | collective-permute-done | bytes 294944 | tf_op jit(solution)/shard_map/states/ppermute | solution.py:371
  49.0 3.2 %collective-permute-start.3 = (bf16[144,1024]{1,0:T(8,128)(2,1)S(1)}, bf16[144,1024]{1,0:T(8,128)(2,1)S(1)}, u32[]{:S(2)}, u32[]{:S(2)}) collective-permute-start(bf16[144,1024]{1,0:T(8,128)(2,1)S(1)} %pad_maximum_fusion.1), channel_id=1, source_target_pairs={{32,64},{0,96},{33,65},{1,97},{34,66},{2,98},{35,67},{3,99},{36,68... | collective-permute-start | bytes 884744 | tf_op jit(solution)/shard_map/states/ppermute | solution.py:374
  54.3 3.2 %collective-permute-done.3 = bf16[144,1024]{1,0:T(8,128)(2,1)S(1)} collective-permute-done((bf16[144,1024]{1,0:T(8,128)(2,1)S(1)}, bf16[144,1024]{1,0:T(8,128)(2,1)S(1)}, u32[]{:S(2)}, u32[]{:S(2)}) %collective-permute-start.3) | collective-permute-done | bytes 294944 | tf_op jit(solution)/shard_map/states/ppermute | solution.py:374
  57.5 0.9 select_convert_fusion
  58.4 1.9 %collective-permute-start.4 = (bf16[128,1024]{1,0:T(8,128)(2,1)S(1)}, bf16[128,1024]{1,0:T(8,128)(2,1)S(1)}, u32[]{:S(2)}, u32[]{:S(2)}) collective-permute-start(bf16[128,1024]{1,0:T(8,128)(2,1)S(1)} %get-tuple-element.26), channel_id=1, source_target_pairs={{0,16},{16,0},{1,17},{17,1},{2,18},{18,2},{3,19},{19,3},{4,20},{20... | collective-permute-start | bytes 786440 | tf_op jit(solution)/shard_map/states/ppermute | solution.py:378
  60.3 12.4 %scan.1.y = bf16[512,2048]{1,0:T(8,128)(2,1)} custom-call(s32[5]{0:T(128)} %stack.15.meta, bf16[512,2048]{1,0:T(8,128)(2,1)} %get-tuple-element.15.refs_0_, bf16[512,256]{1,0:T(8,128)(2,1)} %get-tuple-element.16.refs_1_.bc, bf16[512,128]{1,0:T(8,128)(2,1)} %get-tuple-element.17.refs_2_, f32[8,4,512]{2,1,0:T(4,128)} %get-tuple-element.18.refs_3_, ...), custom_call_target="tpu_custom_call" | custom-call | flops 1073741824 | bytes 4194304 | tf_op jit(solution)/shard_map/scan/pallas_call | solution.py:381
  73.4 10.7 %out.1 = (bf16[512,1024]{1,0:T(8,128)(2,1)}, f32[8,4096]{1,0:T(8,128)}) custom-call(s32[5]{0:T(128)} %stack.15.meta, bf16[512,2048]{1,0:T(8,128)(2,1)} %scan.1.y, bf16[512,256]{1,0:T(8,128)(2,1)} %get-tuple-element.16.refs_1_.bc, bf16[128,1024]{1,0:T(8,128)(2,1)} %get-tuple-element.27.kept, bf16[128,1024]{1,0:T(8,128)(2,1)} %copy-done.1, ...), custom_call_target="tpu_custom_call" | custom-call | flops 2415919104 | bytes 10485760 | tf_op jit(solution)/shard_map/out/pallas_call | solution.py:395
  84.2 0.9 convert_bitcast_fusion
  86.9 5.1 %all-to-all-start = ((bf16[8,2,2048]{2,1,0:T(2,128)(2,1)}), bf16[8,2,2048]{2,1,0:T(2,128)(2,1)S(1)}, u32[]{:S(2)}, u32[]{:S(2)}) async-start(bf16[8,2,2048]{2,1,0:T(2,128)(2,1)} %reshape.58), calls=%async_computation | async-start | bytes 131072 | tf_op jit(solution)/shard_map/rows/all_to_all | solution.py:415
  92.0 4.8 %all-to-all-done = bf16[8,2,2048]{2,1,0:T(2,128)(2,1)S(1)} async-done(((bf16[8,2,2048]{2,1,0:T(2,128)(2,1)}), bf16[8,2,2048]{2,1,0:T(2,128)(2,1)S(1)}, u32[]{:S(2)}, u32[]{:S(2)}) %all-to-all-start) | async-done | bytes 65568 | tf_op jit(solution)/shard_map/rows/all_to_all | solution.py:415
  97.7 3.9 %reduce.9 = bf16[64,4224]{1,0:T(8,128)(2,1)S(1)} reduce(bf16[64,1,4224]{2,1,0:T(2,128)(2,1)S(1)} %broadcast_in_dim.50, bf16[]{:T(256)} %broadcast.87), dimensions={1}, to_apply=%broadcast_in_dim.50.reduce_sub_computation | reduce | bytes 1081346 | tf_op jit(solution)/shard_map/rows/broadcast_in_dim | solution.py:419
  102.0 20.9 %all_to_all.29 = bf16[64,2,2112]{2,1,0:T(2,128)(2,1)S(1)} all-to-all(bf16[64,2,2112]{2,1,0:T(2,128)(2,1)S(1)} %reshape.60), channel_id=1, replica_groups=mesh['x'=4,'core'=2,'cand'=16] {'x','cand'}, dimensions={0} | all-to-all | bytes 1081344 | tf_op jit(solution)/shard_map/rows/all_to_all | solution.py:418
  123.6 2.6 %collective-permute-start.5 = (bf16[64,4224]{1,0:T(8,128)(2,1)S(1)}, bf16[64,4224]{1,0:T(8,128)(2,1)S(1)}, u32[]{:S(2)}, u32[]{:S(2)}) collective-permute-start(bf16[64,4224]{1,0:T(8,128)(2,1)S(1)} %bitcast.31), channel_id=1, source_target_pairs={{0,16},{16,0},{1,17},{17,1},{2,18},{18,2},{3,19},{19,3},{4,20},{20... | collective-permute-start | bytes 1622024 | tf_op jit(solution)/shard_map/rows/ppermute | solution.py:421
  126.9 0.9 collective-permute-done.5.got
  128.6 11.8 %logits.1 = f32[128,16]{1,0:T(8,128)} custom-call(s32[5]{0:T(128)} %stack.15.meta, bf16[64,4224]{1,0:T(8,128)(2,1)} %bitcast.32, bf16[64,4224]{1,0:T(8,128)(2,1)} %copy-done.6, bf16[4096,1024]{1,0:T(8,128)(2,1)} %items.1, f32[1,512]{1,0:T(1,128)} %reshape.38.scale), custom_call_target="tpu_custom_call" | custom-call | flops 4294967296 | bytes 8388608 | tf_op jit(solution)/shard_map/logits/pallas_call | solution.py:426
  140.4 13.4 %all_to_all.30 = f32[128,1,16]{2,1,0:T(1,128)S(1)} all-to-all(f32[128,1,16]{2,1,0:T(1,128)} %bitcast.33), channel_id=1, replica_groups=mesh['x'=4,'core'=2,'cand'=16] {'core','x','cand'}, dimensions={0} | all-to-all | bytes 16384 | tf_op jit(solution)/shard_map/loss/all_to_all | solution.py:440
  (60 shorter events, 11.9 us)
Async XLA Ops:
  1.4 20.0 %collective-permute-start = (bf16[16,1024]{1,0:T(8,128)(2,1)S(1)}, bf16[16,1024]{1,0:T(8,128)(2,1)S(1)}, u32[]{:S(2)}, u32[]{:S(2)}) collective-permute-start(bf16[16,1024]{1,0:T(8,128)(2,1)S(1)} %slice_bitcast_fusion), channel_id=1, source_target_pairs={{0,16},{16,32},{32,48},{48,64},{64,80},{80,96},{96,112},{1,17},{17... | collective-permute-start | bytes 98312 | tf_op jit(solution)/shard_map/halo/ppermute | solution.py:309
  9.6 8.8 %copy-start.4 = (s32[2]{0:T(128)S(1)}, s32[2]{0:T(128)}, u32[]{:S(2)}) copy-start(s32[2]{0:T(128)} %constant.95) | copy-start | bytes 28
  9.6 8.8 %copy-start.2 = (f32[2304]{0:T(1024)S(1)}, f32[2304]{0:T(1024)}, u32[]{:S(2)}) copy-start(f32[2304]{0:T(1024)} %param.32) | copy-start | bytes 27652
  21.4 0.6 copy-start.7
  37.0 1.9 %collective-permute-start.1 = (bf16[144,1024]{1,0:T(8,128)(2,1)}, bf16[144,1024]{1,0:T(8,128)(2,1)S(1)}, u32[]{:S(2)}, u32[]{:S(2)}) collective-permute-start(bf16[144,1024]{1,0:T(8,128)(2,1)} %get-tuple-element.20), channel_id=1, source_target_pairs={{0,16},{16,0},{1,17},{17,1},{2,18},{18,2},{3,19},{19,3},{4,20},{20... | collective-permute-start | bytes 884744 | tf_op jit(solution)/shard_map/states/ppermute | solution.py:367
  40.1 12.6 %copy-start.8 = (s32[1,32]{1,0:T(1,128)S(1)}, s32[1,32]{1,0:T(1,128)}, u32[]{:S(2)}) copy-start(s32[1,32]{1,0:T(1,128)} %param.22) | copy-start | bytes 388
  40.2 8.5 %collective-permute-start.2 = (bf16[144,1024]{1,0:T(8,128)(2,1)S(1)}, bf16[144,1024]{1,0:T(8,128)(2,1)S(1)}, u32[]{:S(2)}, u32[]{:S(2)}) collective-permute-start(bf16[144,1024]{1,0:T(8,128)(2,1)S(1)} %fusion.4), channel_id=1, source_target_pairs={{0,32},{32,0},{64,96},{96,64},{1,33},{33,1},{65,97},{97,65},{2,34}... | collective-permute-start | bytes 884744 | tf_op jit(solution)/shard_map/states/ppermute | solution.py:371
  48.9 11.4 %copy-start.5 = (s32[1,4]{1,0:T(1,128)S(1)}, s32[1,4]{1,0:T(1,128)}, u32[]{:S(2)}) copy-start(s32[1,4]{1,0:T(1,128)} %param.23) | copy-start | bytes 52
  49.0 8.5 %collective-permute-start.3 = (bf16[144,1024]{1,0:T(8,128)(2,1)S(1)}, bf16[144,1024]{1,0:T(8,128)(2,1)S(1)}, u32[]{:S(2)}, u32[]{:S(2)}) collective-permute-start(bf16[144,1024]{1,0:T(8,128)(2,1)S(1)} %pad_maximum_fusion.1), channel_id=1, source_target_pairs={{32,64},{0,96},{33,65},{1,97},{34,66},{2,98},{35,67},{3,99},{36,68... | collective-permute-start | bytes 884744 | tf_op jit(solution)/shard_map/states/ppermute | solution.py:374
  58.4 14.3 %collective-permute-start.4 = (bf16[128,1024]{1,0:T(8,128)(2,1)S(1)}, bf16[128,1024]{1,0:T(8,128)(2,1)S(1)}, u32[]{:S(2)}, u32[]{:S(2)}) collective-permute-start(bf16[128,1024]{1,0:T(8,128)(2,1)S(1)} %get-tuple-element.26), channel_id=1, source_target_pairs={{0,16},{16,0},{1,17},{17,1},{2,18},{18,2},{3,19},{19,3},{4,20},{20... | collective-permute-start | bytes 786440 | tf_op jit(solution)/shard_map/states/ppermute | solution.py:378
  72.7 0.7 copy-start.1
  86.9 9.9 %all-to-all-start = ((bf16[8,2,2048]{2,1,0:T(2,128)(2,1)}), bf16[8,2,2048]{2,1,0:T(2,128)(2,1)S(1)}, u32[]{:S(2)}, u32[]{:S(2)}) async-start(bf16[8,2,2048]{2,1,0:T(2,128)(2,1)} %reshape.58), calls=%async_computation | async-start | bytes 131072 | tf_op jit(solution)/shard_map/rows/all_to_all | solution.py:415
  102.0 24.3 %copy-start.3 = (f32[16]{0:T(128)S(1)}, f32[16]{0:T(128)}, u32[]{:S(2)}) copy-start(f32[16]{0:T(128)} %param.26) | copy-start | bytes 196
  123.6 4.2 %copy-start = (bf16[64,1,4224]{2,0,1:T(8,128)(2,1)}, bf16[64,1,4224]{2,0,1:T(8,128)(2,1)S(1)}, u32[]{:S(2)}) copy-start(bf16[64,1,4224]{2,0,1:T(8,128)(2,1)S(1)} %copy.40) | copy-start | bytes 1622020
  123.6 4.2 %collective-permute-start.5 = (bf16[64,4224]{1,0:T(8,128)(2,1)S(1)}, bf16[64,4224]{1,0:T(8,128)(2,1)S(1)}, u32[]{:S(2)}, u32[]{:S(2)}) collective-permute-start(bf16[64,4224]{1,0:T(8,128)(2,1)S(1)} %bitcast.31), channel_id=1, source_target_pairs={{0,16},{16,0},{1,17},{17,1},{2,18},{18,2},{3,19},{19,3},{4,20},{20... | collective-permute-start | bytes 1622024 | tf_op jit(solution)/shard_map/rows/ppermute | solution.py:421
  127.8 0.8 copy-start.6

commit v2 on v0

v2 whole, which is shorter than its diff:
```python
import jax
import jax.numpy as jnp
import numpy as np
from jax import lax
from jax.experimental import pallas as pl
from jax.experimental.pallas import tpu as pltpu
from jax.sharding import PartitionSpec as P

GROUP = 128
EPS = 1e-05
BLK = 256
HALO = 16
PART = 64
BF = jnp.bfloat16
F32 = jnp.float32
SEQ = ("x", "core")
EACH = ("core", "x", "cand")
VMEM = pl.BlockSpec(memory_space=pltpu.VMEM)
HBM = pl.BlockSpec(memory_space=pl.ANY)
SMEM = pl.BlockSpec(memory_space=pltpu.SMEM)


def rms(v, gain):
    return v * lax.rsqrt(jnp.mean(v * v, axis=-1, keepdims=True) + EPS) * gain


def silu(v):
    half = 0.5 * v
    return half + half * jnp.tanh(half)


def four(v, axis=1):
    return jnp.concatenate([v, v, v, v], axis=axis)


def packed(v, parts):
    group = lax.broadcasted_iota(jnp.int32, v.shape, 1) // 32
    rest = v
    out = jnp.zeros_like(v)
    for part in range(parts):
        piece = rest.astype(BF).astype(F32)
        out = jnp.where(group == part, piece, out)
        rest = rest - piece
    return out.astype(BF)


def expander(heads, lanes, parts):
    row = np.arange(128)[:, None]
    col = np.arange(heads * lanes)[None, :]
    return jnp.asarray((row % 32 == col // lanes) & (row < 32 * parts), BF)


def dot(a, b):
    return jnp.dot(a, b, preferred_element_type=F32)


def dot_nt(a, b):
    return lax.dot_general(a, b, (((1,), (1,)), ((), ())), preferred_element_type=F32)


def blocks(total, size):
    return [slice(i, i + size) for i in range(0, total, size)]


def call(kernel, out_shape, specs, scratch=(), flops=0, limit=12, outs=None):
    many = isinstance(out_shape, (list, tuple))
    return pl.pallas_call(
        kernel,
        in_specs=specs,
        out_specs=outs or ([VMEM] * len(out_shape) if many else VMEM),
        out_shape=out_shape,
        scratch_shapes=list(scratch),
        compiler_params=pltpu.CompilerParams(vmem_limit_bytes=limit * 1024 * 1024),
        cost_estimate=pl.CostEstimate(flops=flops, bytes_accessed=0, transcendentals=0),
    )


def shape(*dims, dtype=BF):
    return jax.ShapeDtypeStruct(dims, dtype)


def fetches(pairs, sems, started=None):
    copies = [pltpu.make_async_copy(src, dst, sems.at[i]) for i, (src, dst) in enumerate(pairs)]
    for copy in copies[:started]:
        copy.start()
    return copies


def mix_kernel(
    length, ev_h, gain_h, w_dt_h, dt_bias_h, a_log_h, halo_h, w_h, conv_w_h, conv_b_h, spread_h,
    normed_h, cum_out, cum_t, shard, chunk, x_h, bc, keep, send,
    ev, gain, w_dt, dt_bias, a_log, halo, w, conv_w, conv_b, spread,
    full, x, raw, tail, weighted, b_t, states, sems, out_sems,
):
    rows, inner = x.shape
    order = [slice(inner, inner + BLK)] + blocks(inner, BLK)
    copies = fetches(
        [
            (ev_h, ev), (gain_h, gain), (w_dt_h, w_dt), (dt_bias_h, dt_bias), (a_log_h, a_log),
            (halo_h, halo), (conv_w_h, conv_w), (conv_b_h, conv_b), (spread_h, spread), (w_h, w),
        ],
        sems,
    )
    for copy in copies[:6]:
        copy.wait()
    full[:HALO] = rms(halo[...].astype(F32), gain[...]).astype(BF)
    for part in blocks(rows, PART):
        full[HALO + part.start : HALO + part.stop] = rms(ev[part].astype(F32), gain[...]).astype(BF)
    pre = dot_nt(full[HALO:], four(w_dt[...], 0))
    place = lax.axis_index(SEQ) * rows + lax.broadcasted_iota(jnp.int32, (rows, 128), 0)
    v = pre + four(dt_bias[...])
    soft = jnp.maximum(v, 0.0) + jnp.log1p(jnp.exp(-jnp.abs(v)))
    step = jnp.where(place < length[0], soft, 0.0)
    logdec = -step * jnp.exp(four(a_log[...]))
    lower = (
        lax.broadcasted_iota(jnp.int32, (rows, rows), 0)
        >= lax.broadcasted_iota(jnp.int32, (rows, rows), 1)
    ).astype(BF)
    cum = dot(lower, packed(logdec, 3))
    cum = cum + pltpu.roll(cum, 32, 1)
    cum = cum + pltpu.roll(cum, 64, 1)
    cum_out[...] = packed(cum, 3)
    flipped = jnp.transpose(cum)
    for g in range(8):
        cum_t[g] = flipped[4 * g : 4 * g + 4]
    shard[0] = packed(jnp.exp(cum[rows - 1 :] - cum) * step, 2)
    shard[1] = packed(jnp.exp(cum), 2)
    chunk[0] = packed(step, 2)
    for c, part in enumerate(blocks(rows, GROUP)):
        own = cum[part]
        chunk[1, part] = packed(jnp.exp(own[GROUP - 1 :] - own) * step[part], 2)
        chunk[2, part] = packed(jnp.exp(own - (cum[part.start - 1 : part.start] if c else 0.0)), 2)
    for copy in copies[6:]:
        copy.wait()
    stores = [pltpu.make_async_copy(full.at[HALO:], normed_h, out_sems.at[8])]
    stores[0].start()
    for n, cols in enumerate(order):
        slot = n % 2
        both = dot(full[...], w[:, cols])
        raw[slot, 0] = both[:, :128]
        raw[slot, 1] = both[:, 128:]
        if n:
            tail[slot] = dot(shard[0], spread[:, cols])
        for j in range(2):
            at = cols.start // 128 + j
            lanes = slice(at * 128, (at + 1) * 128)
            local_lanes = slice(j * 128, (j + 1) * 128)
            for part in blocks(rows, PART):
                conv = conv_b[at : at + 1]
                for k in range(4):
                    first = HALO - 3 + k + part.start
                    conv = conv + conv_w[k : k + 1, lanes] * raw[slot, j, first : first + PART]
                act = silu(conv)
                if n:
                    x[part, lanes] = act.astype(BF)
                    weighted[slot, part, local_lanes] = (act * tail[slot, part, local_lanes]).astype(BF)
                else:
                    bc[part, local_lanes] = act.astype(BF)
        if n:
            stores += fetches([(x.at[:, cols], x_h.at[:, cols])], out_sems.at[n - 1 : n])
            states[:128, cols] = dot(b_t[...], weighted[slot]).astype(BF)
            decay = dot(shard[1, rows - 16 :], spread[:, cols])
            states[128:, cols] = jnp.broadcast_to(decay[15:], (16, BLK)).astype(BF)
        else:
            b_t[...] = jnp.transpose(bc[:, :128].astype(F32)).astype(BF)
    first = lax.axis_index("core") == 0
    half = inner // 2
    for part in blocks(144, 48):
        low, high = states[part, :half], states[part, half:]
        keep[part] = jnp.where(first, low, high)
        send[part] = jnp.where(first, high, low)
    for store in stores:
        store.wait()


def join(first, second, out):
    decay = second[128:129].astype(F32)
    for part in blocks(128, PART):
        out[part] = (first[part].astype(F32) * decay + second[part].astype(F32)).astype(BF)
    out[128:] = (first[128:].astype(F32) * second[128:].astype(F32)).astype(BF)


def chip_kernel(keep, got, chip):
    @pl.when(lax.axis_index("core") == 0)
    def _():
        join(keep, got, chip)

    @pl.when(lax.axis_index("core") == 1)
    def _():
        join(got, keep, chip)


def pair_kernel(chip, near, pair):
    odd = lax.axis_index("x") % 2

    @pl.when(odd == 1)
    def _():
        join(near, chip, pair)

    @pl.when(odd == 0)
    def _():
        join(chip, near, pair)


def enter_kernel(keep, got, near, far, here, away):
    odd = (lax.axis_index("x") % 2 == 1).astype(F32)
    front = lax.axis_index("core") == 0
    near_decay = near[128:129].astype(F32) * odd + (1.0 - odd)
    decay = jnp.where(front, keep[128:129].astype(F32), got[128:129].astype(F32))
    for part in blocks(128, PART):
        enter = near[part].astype(F32) * odd + near_decay * far[part].astype(F32)
        first = jnp.where(front, keep[part].astype(F32), got[part].astype(F32))
        later = first + decay * enter
        here[part] = jnp.where(front, enter, later).astype(BF)
        away[part] = jnp.where(front, later, enter).astype(BF)


def scan_kernel(lo, hi, x, bc, cum, cum_t, chunk, spread, wide, d_skip, y, scores, b_t, lines):
    rows = x.shape[0]
    lower = lax.broadcasted_iota(jnp.int32, (GROUP, GROUP), 0) >= lax.broadcasted_iota(
        jnp.int32, (GROUP, GROUP), 1
    )
    for c, part in enumerate(blocks(rows, GROUP)):
        scores[c] = jnp.where(lower, dot_nt(bc[part, 128:], bc[part, :128]), 0.0)
    b_t[...] = jnp.transpose(bc[:, :128].astype(F32)).astype(BF)
    lines[...] = packed(jnp.broadcast_to(four(d_skip[...]), (16, 128)), 2)
    left = lax.broadcasted_iota(jnp.int32, (GROUP, 128), 1) < 64

    def group(g, _):
        cols = pl.ds(pl.multiple_of(g * BLK, BLK), BLK)
        to = pl.ds(pl.multiple_of((g - lo) * BLK, BLK), BLK)
        sp = spread[:, cols]
        wd = wide[:, pl.ds(pl.multiple_of(g * 4 * GROUP, 4 * GROUP), 4 * GROUP)]
        skip = dot(lines[...], sp)[:1]
        before = jnp.zeros((128, BLK), F32)
        for c, part in enumerate(blocks(rows, GROUP)):
            xc = x[part, cols].astype(F32)
            stepped = xc * dot(chunk[0, part], sp)
            inside = dot(chunk[2, part], sp)
            own = dot(cum[part], wd)
            out = xc * skip
            if c:
                out = out + dot(bc[part, 128:], before.astype(BF)) * inside
            pairs = []
            for p in range(2):
                weights = []
                for h in (2 * p, 2 * p + 1):
                    diff = own[:, h * GROUP : (h + 1) * GROUP] - cum_t[g, h : h + 1, part]
                    weights.append((scores[c] * jnp.exp(jnp.minimum(diff, 0.0))).astype(BF))
                pair = stepped[:, p * 128 : (p + 1) * 128]
                stacked = jnp.concatenate(
                    [jnp.where(left, pair, 0.0), jnp.where(left, 0.0, pair)], axis=0
                ).astype(BF)
                pairs.append(dot(jnp.concatenate(weights, axis=1), stacked))
            y[part, to] = (out + jnp.concatenate(pairs, axis=1)).astype(BF)
            if c < rows // GROUP - 1:
                tailed = (xc * dot(chunk[1, part], sp)).astype(BF)
                before = before * inside[GROUP - 1 :] + dot(b_t[:, part], tailed)
        return 0

    lax.fori_loop(lo, hi, group, 0)


def out_kernel(
    y_a, y_b, bc, kept, got, shard, z, ev, norm_gain, w_out, final_gain, wanted, spread,
    out, picked, mixed, square, enter, total, final,
):
    rows, inner = z.shape
    split = y_a.shape[1]
    width = ev.shape[1]
    half = inner // 2
    first = lax.axis_index("core") == 0
    enter[:, :half] = jnp.where(first, kept[...], got[...])
    enter[:, half:] = jnp.where(first, got[...], kept[...])
    for n, cols in enumerate(blocks(inner, BLK)):
        state = dot(bc[:, 128:], enter[:, cols])
        decay = dot(shard[1], spread[:, cols])
        for part in blocks(rows, PART):
            y = y_a[part, cols] if cols.stop <= split else y_b[part, cols.start - split : cols.stop - split]
            v = y.astype(F32) + state[part] * decay[part]
            v = v * silu(z[part, cols].astype(F32))
            sq = v * v
            sq = sq[:, :128] + sq[:, 128:]
            square[part] = square[part] + sq if n else sq
            mixed[part, cols] = (v * norm_gain[:, cols]).astype(BF)
    for cols in blocks(width, BLK):
        total[:, cols] = dot(mixed[...], w_out[:, cols])
    for part in blocks(rows, PART):
        mean = jnp.sum(square[part], axis=1, keepdims=True) * (1.0 / inner)
        res = (ev[part].astype(F32) + total[part] * lax.rsqrt(mean + EPS)).astype(BF)
        out[part] = res
        final[part] = rms(res.astype(F32), final_gain[...]).astype(BF)
    place = lax.axis_index(SEQ) * rows + lax.broadcasted_iota(jnp.int32, (32, rows), 1)
    column = jnp.transpose(jnp.broadcast_to(wanted[...].astype(F32), (128, 32)))[:, :1]
    pick = dot((place.astype(F32) == column).astype(BF), final[...]).astype(BF)
    for s in range(8):
        picked[s] = pick[4 * s : 4 * s + 4]


def rows_kernel(ids, got, sent):
    width = got.shape[2]
    mine = got[0].astype(F32)
    for s in range(1, got.shape[0]):
        mine = mine + got[s].astype(F32)
    row = lax.broadcasted_iota(jnp.int32, (4, 128), 0)
    lane = lax.broadcasted_iota(jnp.int32, (4, 128), 1)
    own = jnp.zeros((4, 128), jnp.int32)
    for k in range(4):
        own = jnp.where(row == k, ids[0, k], own)
    digits = jnp.where(lane == 0, own >> 16, jnp.where(lane == 1, (own >> 8) & 255, own & 255))
    digits = jnp.where(lane < 3, digits, 0).astype(F32)
    both = jnp.concatenate([mine, digits], axis=1).astype(BF)
    count = sent.shape[0] // 2
    for d in range(count):
        sent[d] = both[:2]
        sent[count + d] = both[2:]


def logit_kernel(block_id, temper, own, got, items, stats, rows, ids, scale):
    count, width = own.shape[0], items.shape[1]
    first = lax.axis_index("core") == 0
    for part in blocks(count, PART):
        mine, other = own[part], got[part]
        low = jnp.where(first, mine, other)
        high = jnp.where(first, other, mine)
        rows[part] = low[:, :width]
        rows[count + part.start : count + part.stop] = high[:, :width]
    for n in range(2):
        digits = jnp.where(first == (n == 0), own[:, width:], got[:, width:]).astype(F32)
        digits = jnp.transpose(digits)
        value = digits[0:1] * 65536.0 + digits[1:2] * 256.0 + digits[2:3]
        ids[:, n * count : (n + 1) * count] = value.astype(jnp.int32)
    history = lax.broadcasted_iota(jnp.int32, scale.shape, 1) // 2 % 16
    factor = jnp.zeros(scale.shape, F32)
    for c in range(16):
        factor = jnp.where(history == c, temper[c], factor)
    scale[...] = factor
    top = jnp.full(scale.shape, -1e30, F32)
    total = jnp.zeros(scale.shape, F32)
    hit = jnp.zeros(scale.shape, F32)
    base = ids[...] - block_id[0] * items.shape[0]
    for part in blocks(items.shape[0], 512):
        logit = dot_nt(items[part], rows[...]) * scale[...]
        place = lax.broadcasted_iota(jnp.int32, logit.shape, 0)
        hit = hit + jnp.sum(jnp.where(place == base - part.start, logit, 0.0), axis=0, keepdims=True)
        new = jnp.maximum(top, jnp.max(logit, axis=0, keepdims=True))
        total = total * jnp.exp(top - new) + jnp.sum(jnp.exp(logit - new), axis=0, keepdims=True)
        top = new
    gap = jnp.zeros((5, count), F32)
    lines = []
    for n in range(2):
        lines += [v[:, n * count : (n + 1) * count] for v in (top, total, hit)] + [gap]
    lines = jnp.concatenate(lines + [jnp.zeros((112, count), F32)], axis=0)
    stats[...] = jnp.transpose(lines)[:, :16]


def local(
    events, lengths, target_pos, target_ids, items, item_block, temper, in_gain, w_xbc, w_z, w_dt,
    conv_w, conv_b, dt_bias, a_log, d_skip, norm_gain, w_out, final_gain,
):
    rows, width = events.shape[1:]
    inner = w_z.shape[1]
    ev = events[0]
    spread = expander(32, 64, 2)
    wide = expander(32, GROUP, 3)
    chunks = rows // GROUP

    with jax.named_scope("halo"):
        halo = lax.ppermute(ev[rows - HALO :], SEQ, [(i, i + 1) for i in range(7)])

    with jax.named_scope("mix"):
        normed, cum, cum_t, shard, chunk, x, bc, keep, send = call(
            mix_kernel,
            [
                shape(rows, width), shape(rows, 128), shape(8, 4, rows, dtype=F32),
                shape(2, rows, 128), shape(3, rows, 128), shape(rows, inner), shape(rows, 256),
                shape(144, inner // 2), shape(144, inner // 2),
            ],
            [SMEM] + [HBM] * 10,
            [
                pltpu.VMEM((rows, width), BF), pltpu.VMEM((1, width), F32), pltpu.VMEM((32, width), BF),
                pltpu.VMEM((1, 32), F32), pltpu.VMEM((1, 32), F32), pltpu.VMEM((HALO, width), BF),
                pltpu.VMEM(w_xbc.shape, BF), pltpu.VMEM(conv_w.shape, F32),
                pltpu.VMEM((conv_b.shape[0] // 128, 128), F32), pltpu.VMEM(spread.shape, BF),
                pltpu.VMEM((rows + HALO, width), BF), pltpu.VMEM((rows, inner), BF),
                pltpu.VMEM((2, 2, rows + HALO, 128), F32),
                pltpu.VMEM((2, rows, BLK), F32), pltpu.VMEM((2, rows, BLK), BF),
                pltpu.VMEM((128, rows), BF), pltpu.VMEM((144, inner), BF),
                pltpu.SemaphoreType.DMA((10,)), pltpu.SemaphoreType.DMA((9,)),
            ],
            2 * rows * width * 2304,
            limit=56,
            outs=[HBM] + [VMEM] * 4 + [HBM] + [VMEM] * 3,
        )(
            lengths, ev, in_gain[None], w_dt.T, dt_bias[None], a_log[None], halo, w_xbc, conv_w,
            conv_b.reshape(-1, 128), spread,
        )

    def scan(lo, hi, x):
        return call(
            lambda *refs: scan_kernel(lo, hi, *refs),
            shape(rows, (hi - lo) * BLK),
            [VMEM] * 8,
            [
                pltpu.VMEM((chunks, GROUP, GROUP), F32), pltpu.VMEM((128, rows), BF),
                pltpu.VMEM((16, 128), BF),
            ],
            16 * rows * 128 * (hi - lo) * BLK,
        )(x, bc, cum, cum_t, chunk, spread, wide, d_skip[None])

    swap = [(0, 1), (1, 0)]
    payload = shape(144, inner // 2)
    entry = shape(128, inner // 2)
    with jax.named_scope("chip"):
        got = lax.ppermute(send, "core", swap)
        chip = call(chip_kernel, payload, [VMEM] * 2)(keep, got)
        sent, x = lax.optimization_barrier((chip, x))
        near = lax.ppermute(sent, "x", [(0, 1), (1, 0), (2, 3), (3, 2)])
    with jax.named_scope("scan"):
        y_a = scan(0, 5, x)
    with jax.named_scope("pair"):
        pair = call(pair_kernel, payload, [VMEM] * 2)(chip, near)
        sent, y_a, x, source = lax.optimization_barrier((pair, y_a, x, normed))
        far = lax.ppermute(sent, "x", [(1, 2), (0, 3)])
    with jax.named_scope("gate"):
        z = dot(source, w_z).astype(BF)
    with jax.named_scope("scan"):
        y_b = scan(5, 8, x)
    with jax.named_scope("enter"):
        here, away = call(enter_kernel, [entry, entry], [VMEM] * 4)(keep, got, near, far)
        away, z, y_b = lax.optimization_barrier((away, z, y_b))
        there = lax.ppermute(away, "core", swap)

    with jax.named_scope("out"):
        out, picked = call(
            out_kernel,
            [shape(rows, width), shape(8, 4, width)],
            [VMEM] * 13,
            [
                pltpu.VMEM((rows, inner), BF), pltpu.VMEM((rows, 128), F32), pltpu.VMEM((128, inner), BF),
                pltpu.VMEM((rows, width), F32), pltpu.VMEM((rows, width), BF),
            ],
            2 * rows * inner * (width + 256),
            limit=14,
        )(
            y_a, y_b, bc, here, there, shard, z, ev, norm_gain[None], w_out, final_gain[None], target_pos,
            spread,
        )

    with jax.named_scope("rows"):
        mine = lax.all_to_all(picked, SEQ, 0, 0, tiled=True)
        sent = call(rows_kernel, shape(128, 2, width + 128), [SMEM, VMEM], flops=10**10)(target_ids, mine)
        own_rows = lax.all_to_all(sent, EACH, 0, 0, tiled=True).reshape(256, width + 128)
        got_rows = lax.ppermute(own_rows, "core", swap)

    with jax.named_scope("logits"):
        stats = call(
            logit_kernel,
            shape(256, 16, dtype=F32),
            [SMEM, SMEM, VMEM, VMEM, VMEM],
            [
                pltpu.VMEM((512, width), BF), pltpu.VMEM((1, 512), jnp.int32), pltpu.VMEM((1, 512), F32),
            ],
            2 * 512 * items.shape[0] * width,
        )(item_block, temper, own_rows, got_rows, items)

    with jax.named_scope("loss"):
        seen = lax.all_to_all(stats.reshape(128, 2, 16), EACH, 0, 0, tiled=True)
        top, total, hit = [
            jnp.concatenate([seen[:, :, n], seen[:, :, n + 8]], axis=1) for n in range(3)
        ]
        peak = jnp.max(top, axis=0)
        loss = peak + jnp.log(jnp.sum(total * jnp.exp(top - peak), axis=0)) - jnp.sum(hit, axis=0)
    return (out[None], loss)


def solution(mesh):
    fine = jax.sharding.Mesh(
        mesh.devices.reshape(mesh.shape["seq"] // 2, 2, mesh.shape["cand"]), ("x", "core", "cand")
    )
    each = ("x", "core", "cand")
    placed = (
        P("cand", SEQ, None),
        P("cand"),
        P("cand", None),
        P("cand", SEQ),
        P(each, None),
        P(each),
    ) + (P(),) * 13
    return jax.shard_map(
        local,
        mesh=fine,
        in_specs=placed,
        out_specs=(P("cand", SEQ, None), P(each)),
        check_vma=False,
    )
```

time: 519 us -> 120 us (0.23); the launches traced: 511 us -> 119 us
  blocking collectives: 235 us -> 45.9 us
  waiting for transfers between devices: 81.4 us -> 4.28 us
  matrix products: 57.5 us -> 2.36 us
  Pallas kernels: 0 us -> 37.8 us
  local copies, waits for them, and re-layouts: 44.8 us -> 12.6 us
  other arithmetic: 29.3 us -> 0.85 us
  starting transfers between devices: 41.1 us -> 13.1 us
  between operations: 17.2 us -> 2.25 us
    all_gather x3 -> x0, blocking collectives: 167 us -> none  [joined(): everything = jax.tree.map(lambda part: lax.all_gather(part, axis), shard)]
    unnamed x1 -> x0, blocking collectives: 68 us -> none
    unnamed x3 -> x0, waiting for transfers between devices: 57 us -> none
    dot_general x11 -> x1, matrix products: 57.5 us -> 2.36 us  [dot(): return jnp.dot(a, b, preferred_element_type=F32)]
    all_to_all x0 -> x3, blocking collectives: none -> 45.9 us  [the longest x1 22.4 us: local(): lax.all_to_all(sent, EACH, 0, 0, tiled=True).reshape(256, width + 128)]
    pallas_call x0 -> x9, Pallas kernels: none -> 37.8 us  [the longest x1 13.4 us: local(): call(mix_kernel, [shape(rows, width), shape(rows, 128), shape(8, 4, rows,...]
    ppermute x8 -> x6, starting transfers between devices: 41 us -> 13.1 us  [the longest x1 4.5 us: local(): halo = lax.ppermute(ev[rows - HALO:], SEQ, [(i, i + 1) for i in range(7)])]
    reshape x6 -> x1, local copies, waits for them, and re-layouts: 23.5 us -> 0.22 us  [local(): lax.all_to_all(sent, EACH, 0, 0, tiled=True).reshape(256, width + 128)]
  transfers between devices with their start and end apart: 10 -> 6, of which waited for: 5 -> 4; matrix products, arithmetic and copies ran while one was open for 6% -> 2% of each run, Pallas kernels for 0% -> 9%
where the time goes in v2:
time: 120 us; the launch traced here: 119 us
  blocking collectives  45.9 us (38%)
  Pallas kernels  37.8 us (31%)
  starting transfers between devices  13.1 us (11%)
  local copies, waits for them, and re-layouts  12.6 us (10%)
  waiting for transfers between devices  4.28 us (4%)
  matrix products  2.36 us (2%)
  between operations  2.25 us (2%)
    all_to_all x1, blocking collectives, local(): lax.all_to_all(sent, EACH, 0, 0, tiled=True).reshape(256, width + 128)  22.4 us
    all_to_all x1, blocking collectives, local(): seen = lax.all_to_all(stats.reshape(128, 2, 16), EACH, 0, 0, tiled=True)  14.2 us
    pallas_call x1, Pallas kernels, local(): call(mix_kernel, [shape(rows, width), shape(rows, 128), shape(8, 4, rows,...  13.4 us
    pallas_call x2, Pallas kernels, scan(): call(lambda *refs: scan_kernel(lo, hi, *refs), shape(rows, (hi - lo) * BL...  11 us
    unnamed x58, local copies, waits for them, and re-layouts  10.7 us
    all_to_all x1, blocking collectives, local(): mine = lax.all_to_all(picked, SEQ, 0, 0, tiled=True)  9.29 us
    pallas_call x1, Pallas kernels, local(): call(logit_kernel, shape(256, 16, dtype=F32), [SMEM, SMEM, VMEM, VMEM, VM...  6.8 us
    pallas_call x1, Pallas kernels, local(): call(out_kernel, [shape(rows, width), shape(8, 4, width)], [VMEM] * 13, [...  5.48 us
  transfers between devices with their start and end apart: 6, of which 4 were waited for; matrix products, arithmetic and copies ran while one was open for 2% of the time, Pallas kernels for 9%

profile of v2, /device:TPU:1, one launch (start us, length us, event | category | flops | bytes accessed | tf_op | source)
XLA Modules:
  0.0 119.0 jit_solution(1768618016615237715)
XLA Ops:
  1.4 4.5 %collective-permute-start = (bf16[16,1024]{1,0:T(8,128)(2,1)S(1)}, bf16[16,1024]{1,0:T(8,128)(2,1)S(1)}, u32[]{:S(2)}, u32[]{:S(2)}) collective-permute-start(bf16[16,1024]{1,0:T(8,128)(2,1)S(1)} %slice_bitcast_fusion), channel_id=1, source_target_pairs={{0,16},{16,32},{32,48},{48,64},{64,80},{80,96},{96,112},{1,17},{17... | collective-permute-start | bytes 98312 | tf_op jit(solution)/shard_map/halo/ppermute | solution.py:369
  7.5 13.4 %mix.1 = (bf16[512,1024]{1,0:T(8,128)(2,1)}, bf16[512,128]{1,0:T(8,128)(2,1)}, f32[8,4,512]{2,1,0:T(4,128)}, bf16[2,512,128]{2,1,0:T(8,128)(2,1)}, bf16[3,512,12...) custom-call(s32[1]{0:T(128)S(6)} %copy.45.length, ...), custom_call_target="tpu_custom_call" | custom-call | flops 2415919104 | tf_op jit(solution)/shard_map/mix/pallas_call | solution.py:372
  21.0 1.8 %collective-permute-done.1.got = bf16[144,1024]{1,0:T(8,128)(2,1)S(1)} collective-permute-done((bf16[144,1024]{1,0:T(8,128)(2,1)}, bf16[144,1024]{1,0:T(8,128)(2,1)S(1)}, u32[]{:S(2)}, u32[]{:S(2)}) %collective-permute-start.1) | collective-permute-done | bytes 294944 | tf_op jit(solution)/shard_map/chip/ppermute | solution.py:415
  22.8 1.0 copy-done.9
  23.8 2.1 %collective-permute-start.2 = (bf16[144,1024]{1,0:T(8,128)(2,1)S(1)}, bf16[144,1024]{1,0:T(8,128)(2,1)S(1)}, u32[]{:S(2)}, u32[]{:S(2)}) collective-permute-start(bf16[144,1024]{1,0:T(8,128)(2,1)S(1)} %chip.1), channel_id=1, source_target_pairs={{0,32},{32,0},{64,96},{96,64},{1,33},{33,1},{65,97},{97,65},{2,34}... | collective-permute-start | bytes 884744 | tf_op jit(solution)/shard_map/chip/ppermute | solution.py:418
  26.0 1.6 %copy-done = bf16[512,2048]{1,0:T(8,128)(2,1)S(1)} copy-done((bf16[512,2048]{1,0:T(8,128)(2,1)S(1)}, bf16[512,2048]{1,0:T(8,128)(2,1)}, u32[]{:S(2)}) %copy-start) | copy-done | bytes 2097176
  27.6 0.9 copy-done.5
  28.5 1.0 copy-done.7
  29.5 0.9 copy-done.12
  30.4 0.8 copy-done.14
  31.3 6.8 %scan.2.y_a = bf16[512,1280]{1,0:T(8,128)(2,1)S(1)} custom-call(bf16[512,2048]{1,0:T(8,128)(2,1)S(1)} %copy-done, bf16[512,256]{1,0:T(8,128)(2,1)S(1)} %copy-done.5, bf16[512,128]{1,0:T(8,128)(2,1)S(1)} %copy-done.12, f32[8,4,512]{2,1,0:T(4,128)S(1)} %copy-done.14, bf16[3,512,128]{2,1,0:T(8,128)(2,1)S(1)} %copy-done.7, bf16[128,2048]{1,0:T(8,128)(2,1)S(1)} %copy-done.2, ...), custom_call_target="tpu_custom_call" | custom-call | flops 1342177280 | tf_op jit(solution)/shard_map/scan/pallas_call | solution.py:400
  38.3 4.2 %collective-permute-start.3 = (bf16[144,1024]{1,0:T(8,128)(2,1)S(1)}, bf16[144,1024]{1,0:T(8,128)(2,1)S(1)}, u32[]{:S(2)}, u32[]{:S(2)}) collective-permute-start(bf16[144,1024]{1,0:T(8,128)(2,1)S(1)} %pair.1), channel_id=1, source_target_pairs={{32,64},{0,96},{33,65},{1,97},{34,66},{2,98},{35,67},{3,99},{36,68... | collective-permute-start | bytes 884744 | tf_op jit(solution)/shard_map/pair/ppermute | solution.py:424
  42.5 2.4 %convolution_convert_fusion.z = bf16[512,2048]{1,0:T(8,128)(2,1)S(1)} fusion(bf16[512,1024]{1,0:T(8,128)(2,1)S(1)} %copy-done.26, bf16[1024,2048]{1,0:T(8,128)(2,1)S(1)} %copy-done.24), kind=kOutput, calls=%fused_computation | convolution fusion | flops 2148532224 | bytes 7340032 | tf_op jit(solution)/shard_map/gate/dot_general | solution.py:54
  45.0 4.2 %scan.3.y_b = bf16[512,768]{1,0:T(8,128)(2,1)S(1)} custom-call(bf16[512,2048]{1,0:T(8,128)(2,1)S(1)} %copy-done.1, bf16[512,256]{1,0:T(8,128)(2,1)S(1)} %copy-done.6, bf16[512,128]{1,0:T(8,128)(2,1)S(1)} %copy-done.13, f32[8,4,512]{2,1,0:T(4,128)S(1)} %copy-done.15, bf16[3,512,128]{2,1,0:T(8,128)(2,1)S(1)} %copy-done.8, bf16[128,2048]{1,0:T(8,128)(2,1)S(1)} %copy-done.2, ...), custom_call_target="tpu_custom_call" | custom-call | flops 805306368 | tf_op jit(solution)/shard_map/scan/pallas_call | solution.py:400
  49.5 1.0 collective-permute-start.4
  50.5 1.2 collective-permute-done.4.got
  51.7 5.5 %out.1 = (bf16[512,1024]{1,0:T(8,128)(2,1)}, bf16[8,4,1024]{2,1,0:T(4,128)(2,1)S(1)}) custom-call(bf16[512,1280]{1,0:T(8,128)(2,1)S(1)} %scan.2.y_a, bf16[512,768]{1,0:T(8,128)(2,1)S(1)} %scan.3.y_b, bf16[512,256]{1,0:T(8,128)(2,1)S(1)} %copy-done.6, bf16[128,1024]{1,0:T(8,128)(2,1)S(1)} %get-tuple-element.40.kept, ...), custom_call_target="tpu_custom_call" | custom-call | flops 2684354560 | tf_op jit(solution)/shard_map/out/pallas_call | solution.py:435
  57.2 9.3 %all_to_all.15.got = bf16[8,4,1024]{2,1,0:T(4,128)(2,1)S(1)} all-to-all(bf16[8,4,1024]{2,1,0:T(4,128)(2,1)S(1)} %get-tuple-element.45), channel_id=1, replica_groups=mesh['x'=4,'core'=2,'cand'=16] {'x','core'}, dimensions={0} | all-to-all | bytes 131072 | tf_op jit(solution)/shard_map/rows/all_to_all | solution.py:451
  67.1 22.4 %all_to_all.16 = bf16[128,2,1152]{2,1,0:T(2,128)(2,1)S(1)} all-to-all(bf16[128,2,1152]{2,1,0:T(2,128)(2,1)S(1)} %rows.1), channel_id=1, replica_groups=mesh['x'=4,'core'=2,'cand'=16] {'core','x','cand'}, dimensions={0} | all-to-all | bytes 1179648 | tf_op jit(solution)/shard_map/rows/all_to_all | solution.py:453
  89.8 1.2 collective-permute-start.5
  91.6 1.0 collective-permute-done.5.got
  92.6 3.4 %copy-done.21 = bf16[4096,1024]{1,0:T(8,128)(2,1)S(1)} copy-done((bf16[4096,1024]{1,0:T(8,128)(2,1)S(1)}, bf16[4096,1024]{1,0:T(8,128)(2,1)}, u32[]{:S(2)}) %copy-start.21) | copy-done | bytes 8388632
  96.0 6.8 %logits.1 = f32[256,16]{1,0:T(8,128)S(1)} custom-call(s32[1]{0:T(128)S(6)} %copy.46.block_id, f32[16]{0:T(128)S(1)} %copy-done.23, bf16[256,1152]{1,0:T(8,128)(2,1)S(1)} %reshape.16.own, bf16[256,1152]{1,0:T(8,128)(2,1)S(1)} %collective-permute-done.5.got, bf16[4096,1024]{1,0:T(8,128)(2,1)S(1)} %copy-done.21), custom_call_target="tpu_custom_call" | custom-call | flops 4294967296 | tf_op jit(solution)/shard_map/logits/pallas_call | solution.py:457
  102.8 14.2 %all_to_all.17 = f32[128,2,16]{2,1,0:T(2,128)S(1)} all-to-all(f32[128,2,16]{2,1,0:T(2,128)S(1)} %bitcast.23), channel_id=1, replica_groups=mesh['x'=4,'core'=2,'cand'=16] {'core','x','cand'}, dimensions={0} | all-to-all | bytes 32768 | tf_op jit(solution)/shard_map/loss/all_to_all | solution.py:468
  (67 shorter events, 5.3 us)
Async XLA Ops:
  1.4 5.5 %collective-permute-start = (bf16[16,1024]{1,0:T(8,128)(2,1)S(1)}, bf16[16,1024]{1,0:T(8,128)(2,1)S(1)}, u32[]{:S(2)}, u32[]{:S(2)}) collective-permute-start(bf16[16,1024]{1,0:T(8,128)(2,1)S(1)} %slice_bitcast_fusion), channel_id=1, source_target_pairs={{0,16},{16,32},{32,48},{48,64},{64,80},{80,96},{96,112},{1,17},{17... | collective-permute-start | bytes 98312 | tf_op jit(solution)/shard_map/halo/ppermute | solution.py:369
  7.5 18.5 %copy-start.2 = (bf16[128,2048]{1,0:T(8,128)(2,1)S(1)}, bf16[128,2048]{1,0:T(8,128)(2,1)}, u32[]{:S(2)}) copy-start(bf16[128,2048]{1,0:T(8,128)(2,1)} %constant.8.clone.spread_h.refs_5_.spread) | copy-start | bytes 1572868
  7.5 18.5 %copy-start.4 = (bf16[128,4096]{1,0:T(8,128)(2,1)S(1)}, bf16[128,4096]{1,0:T(8,128)(2,1)}, u32[]{:S(2)}) copy-start(bf16[128,4096]{1,0:T(8,128)(2,1)} %constant.9.clone.refs_6_) | copy-start | bytes 3145732
  7.5 18.5 %copy-start.19 = (f32[32]{0:T(128)S(1)}, f32[32]{0:T(128)}, u32[]{:S(2)}) copy-start(f32[32]{0:T(128)} %param.36) | copy-start | bytes 388
  7.5 35.0 %copy-start.24 = (bf16[1024,2048]{1,0:T(8,128)(2,1)S(1)}, bf16[1024,2048]{1,0:T(8,128)(2,1)}, u32[]{:S(2)}) copy-start(bf16[1024,2048]{1,0:T(8,128)(2,1)} %param.30) | copy-start | bytes 12582916
  20.9 1.9 %collective-permute-start.1 = (bf16[144,1024]{1,0:T(8,128)(2,1)}, bf16[144,1024]{1,0:T(8,128)(2,1)S(1)}, u32[]{:S(2)}, u32[]{:S(2)}) collective-permute-start(bf16[144,1024]{1,0:T(8,128)(2,1)} %get-tuple-element.25), channel_id=1, source_target_pairs={{0,16},{16,0},{1,17},{17,1},{2,18},{18,2},{3,19},{19,3},{4,20},{20... | collective-permute-start | bytes 884744 | tf_op jit(solution)/shard_map/chip/ppermute | solution.py:415
  23.8 14.3 %collective-permute-start.2 = (bf16[144,1024]{1,0:T(8,128)(2,1)S(1)}, bf16[144,1024]{1,0:T(8,128)(2,1)S(1)}, u32[]{:S(2)}, u32[]{:S(2)}) collective-permute-start(bf16[144,1024]{1,0:T(8,128)(2,1)S(1)} %chip.1), channel_id=1, source_target_pairs={{0,32},{32,0},{64,96},{96,64},{1,33},{33,1},{65,97},{97,65},{2,34}... | collective-permute-start | bytes 884744 | tf_op jit(solution)/shard_map/chip/ppermute | solution.py:418
  31.3 11.2 %copy-start.26 = (bf16[512,1024]{1,0:T(8,128)(2,1)S(1)}, bf16[512,1024]{1,0:T(8,128)(2,1)}, u32[]{:S(2)}) copy-start(bf16[512,1024]{1,0:T(8,128)(2,1)} %get-tuple-element.37) | copy-start | bytes 3145732
  38.2 6.6 %copy-start.1 = (bf16[512,2048]{1,0:T(8,128)(2,1)S(1)}, bf16[512,2048]{1,0:T(8,128)(2,1)}, u32[]{:S(2)}) copy-start(bf16[512,2048]{1,0:T(8,128)(2,1)} %get-tuple-element.38.refs_0_) | copy-start | bytes 6291460
  38.3 6.6 %copy-start.6 = (bf16[512,256]{1,0:T(8,128)(2,1)S(1)}, bf16[512,256]{1,0:T(8,128)(2,1)}, u32[]{:S(2)}) copy-start(bf16[512,256]{1,0:T(8,128)(2,1)} %get-tuple-element.29.refs_1_.bc) | copy-start | bytes 786436
  38.3 6.6 %copy-start.8 = (bf16[3,512,128]{2,1,0:T(8,128)(2,1)S(1)}, bf16[3,512,128]{2,1,0:T(8,128)(2,1)}, u32[]{:S(2)}) copy-start(bf16[3,512,128]{2,1,0:T(8,128)(2,1)} %get-tuple-element.32.refs_4_) | copy-start | bytes 1179652
  38.3 6.6 %copy-start.13 = (bf16[512,128]{1,0:T(8,128)(2,1)S(1)}, bf16[512,128]{1,0:T(8,128)(2,1)}, u32[]{:S(2)}) copy-start(bf16[512,128]{1,0:T(8,128)(2,1)} %get-tuple-element.30.refs_2_) | copy-start | bytes 393220
  38.3 6.6 %copy-start.15 = (f32[8,4,512]{2,1,0:T(4,128)S(1)}, f32[8,4,512]{2,1,0:T(4,128)}, u32[]{:S(2)}) copy-start(f32[8,4,512]{2,1,0:T(4,128)} %get-tuple-element.31.refs_3_) | copy-start | bytes 196612
  38.3 10.9 %collective-permute-start.3 = (bf16[144,1024]{1,0:T(8,128)(2,1)S(1)}, bf16[144,1024]{1,0:T(8,128)(2,1)S(1)}, u32[]{:S(2)}, u32[]{:S(2)}) collective-permute-start(bf16[144,1024]{1,0:T(8,128)(2,1)S(1)} %pair.1), channel_id=1, source_target_pairs={{32,64},{0,96},{33,65},{1,97},{34,66},{2,98},{35,67},{3,99},{36,68... | collective-permute-start | bytes 884744 | tf_op jit(solution)/shard_map/pair/ppermute | solution.py:424
  44.9 6.8 %copy-start.3 = (bf16[2048,1024]{1,0:T(8,128)(2,1)S(1)}, bf16[2048,1024]{1,0:T(8,128)(2,1)}, u32[]{:S(2)}) copy-start(bf16[2048,1024]{1,0:T(8,128)(2,1)} %w_out.1) | copy-start | bytes 12582916
  44.9 6.7 %copy-start.11 = (bf16[1,512,1024]{2,1,0:T(8,128)(2,1)S(1)}, bf16[1,512,1024]{2,1,0:T(8,128)(2,1)}, u32[]{:S(2)}) copy-start(bf16[1,512,1024]{2,1,0:T(8,128)(2,1)} %param.21) | copy-start | bytes 3145732
  44.9 6.7 %copy-start.16 = (bf16[2,512,128]{2,1,0:T(8,128)(2,1)S(1)}, bf16[2,512,128]{2,1,0:T(8,128)(2,1)}, u32[]{:S(2)}) copy-start(bf16[2,512,128]{2,1,0:T(8,128)(2,1)} %get-tuple-element.42.shard) | copy-start | bytes 786436
  45.0 6.7 %copy-start.17 = (f32[2048]{0:T(1024)S(1)}, f32[2048]{0:T(1024)}, u32[]{:S(2)}) copy-start(f32[2048]{0:T(1024)} %param.37) | copy-start | bytes 24580
  45.0 6.7 %copy-start.18 = (f32[1024]{0:T(1024)S(1)}, f32[1024]{0:T(1024)}, u32[]{:S(2)}) copy-start(f32[1024]{0:T(1024)} %param.39) | copy-start | bytes 12292
  45.0 6.7 %copy-start.20 = (s32[1,32]{1,0:T(1,128)S(1)}, s32[1,32]{1,0:T(1,128)}, u32[]{:S(2)}) copy-start(s32[1,32]{1,0:T(1,128)} %wanted.1) | copy-start | bytes 388
  49.5 2.2 %collective-permute-start.4 = (bf16[128,1024]{1,0:T(8,128)(2,1)S(1)}, bf16[128,1024]{1,0:T(8,128)(2,1)S(1)}, u32[]{:S(2)}, u32[]{:S(2)}) collective-permute-start(bf16[128,1024]{1,0:T(8,128)(2,1)S(1)} %get-tuple-element.41), channel_id=1, source_target_pairs={{0,16},{16,0},{1,17},{17,1},{2,18},{18,2},{3,19},{19,3},{4,20},{20... | collective-permute-start | bytes 786440 | tf_op jit(solution)/shard_map/enter/ppermute | solution.py:432
  51.7 14.8 %copy-start.22 = (s32[1,4]{1,0:T(1,128)S(1)}, s32[1,4]{1,0:T(1,128)}, u32[]{:S(2)}) copy-start(s32[1,4]{1,0:T(1,128)} %ids.1) | copy-start | bytes 52
  66.5 26.1 %copy-start.23 = (f32[16]{0:T(128)S(1)}, f32[16]{0:T(128)}, u32[]{:S(2)}) copy-start(f32[16]{0:T(128)} %temper.1) | copy-start | bytes 196
  89.8 2.8 %collective-permute-start.5 = (bf16[256,1152]{1,0:T(8,128)(2,1)S(1)}, bf16[256,1152]{1,0:T(8,128)(2,1)S(1)}, u32[]{:S(2)}, u32[]{:S(2)}) collective-permute-start(bf16[256,1152]{1,0:T(8,128)(2,1)S(1)} %reshape.16.own), channel_id=1, source_target_pairs={{0,16},{16,0},{1,17},{17,1},{2,18},{18,2},{3,19},{19,3},{4,20},{20... | collective-permute-start | bytes 1769480 | tf_op jit(solution)/shard_map/rows/ppermute | solution.py:454
  (9 other events, 14.5 us)

commit v3 on v2

--- a/solution.py
+++ b/solution.py
@@ -90,7 +90,7 @@
     length, ev_h, gain_h, w_dt_h, dt_bias_h, a_log_h, halo_h, w_h, conv_w_h, conv_b_h, spread_h,
     normed_h, cum_out, cum_t, shard, chunk, x_h, bc, keep, send,
     ev, gain, w_dt, dt_bias, a_log, halo, w, conv_w, conv_b, spread,
-    full, x, raw, tail, weighted, b_t, states, sems, out_sems,
+    full, x, raw, tail, weighted, b_t, states, fades, sems, out_sems,
 ):
     rows, inner = x.shape
     order = [slice(inner, inner + BLK)] + blocks(inner, BLK)
@@ -132,15 +132,30 @@
         chunk[2, part] = packed(jnp.exp(own - (cum[part.start - 1 : part.start] if c else 0.0)), 2)
     for copy in copies[6:]:
         copy.wait()
-    stores = [pltpu.make_async_copy(full.at[HALO:], normed_h, out_sems.at[8])]
+    stores = [pltpu.make_async_copy(full.at[HALO:], normed_h, out_sems.at[2])]
     stores[0].start()
+    fades[:rows] = shard[0]
+    fades[rows:] = shard[1, rows - 16 :]
+
+    def project(n):
+        both = dot(full[...], w[:, order[n]])
+        raw[n % 2, 0] = both[:, :128]
+        raw[n % 2, 1] = both[:, 128:]
+        if n:
+            tail[n % 2] = dot(fades[...], spread[:, order[n]])
+
+    def end_state(n):
+        cols = order[n]
+        states[:128, cols] = dot(b_t[...], weighted[n % 2]).astype(BF)
+        states[128:, cols] = jnp.broadcast_to(tail[n % 2, rows + 15 :], (16, BLK)).astype(BF)
+
+    project(0)
     for n, cols in enumerate(order):
         slot = n % 2
-        both = dot(full[...], w[:, cols])
-        raw[slot, 0] = both[:, :128]
-        raw[slot, 1] = both[:, 128:]
-        if n:
-            tail[slot] = dot(shard[0], spread[:, cols])
+        if n + 1 < len(order):
+            if n > 1:
+                end_state(n - 1)
+            project(n + 1)
         for j in range(2):
             at = cols.start // 128 + j
             lanes = slice(at * 128, (at + 1) * 128)
@@ -156,13 +171,15 @@
                     weighted[slot, part, local_lanes] = (act * tail[slot, part, local_lanes]).astype(BF)
                 else:
                     bc[part, local_lanes] = act.astype(BF)
-        if n:
-            stores += fetches([(x.at[:, cols], x_h.at[:, cols])], out_sems.at[n - 1 : n])
-            states[:128, cols] = dot(b_t[...], weighted[slot]).astype(BF)
-            decay = dot(shard[1, rows - 16 :], spread[:, cols])
-            states[128:, cols] = jnp.broadcast_to(decay[15:], (16, BLK)).astype(BF)
-        else:
+        if n == 0:
             b_t[...] = jnp.transpose(bc[:, :128].astype(F32)).astype(BF)
+        if n == 6:
+            done = slice(0, cols.stop)
+            stores += fetches([(x.at[:, done], x_h.at[:, done])], out_sems.at[0:1])
+    rest = slice(order[6].stop, inner)
+    stores += fetches([(x.at[:, rest], x_h.at[:, rest])], out_sems.at[1:2])
+    end_state(len(order) - 2)
+    end_state(len(order) - 1)
     first = lax.axis_index("core") == 0
     half = inner // 2
     for part in blocks(144, 48):
@@ -190,33 +207,31 @@
         join(got, keep, chip)
 
 
-def pair_kernel(chip, near, pair):
-    odd = lax.axis_index("x") % 2
-
-    @pl.when(odd == 1)
-    def _():
-        join(near, chip, pair)
-
-    @pl.when(odd == 0)
-    def _():
-        join(chip, near, pair)
-
-
-def enter_kernel(keep, got, near, far, here, away):
-    odd = (lax.axis_index("x") % 2 == 1).astype(F32)
+def enter_kernel(keep, got, near, mid, far, here, away):
     front = lax.axis_index("core") == 0
-    near_decay = near[128:129].astype(F32) * odd + (1.0 - odd)
+    near_decay, mid_decay = near[128:129].astype(F32), mid[128:129].astype(F32)
     decay = jnp.where(front, keep[128:129].astype(F32), got[128:129].astype(F32))
     for part in blocks(128, PART):
-        enter = near[part].astype(F32) * odd + near_decay * far[part].astype(F32)
+        enter = mid[part].astype(F32) + mid_decay * far[part].astype(F32)
+        enter = near[part].astype(F32) + near_decay * enter
         first = jnp.where(front, keep[part].astype(F32), got[part].astype(F32))
         later = first + decay * enter
         here[part] = jnp.where(front, enter, later).astype(BF)
         away[part] = jnp.where(front, later, enter).astype(BF)
 
 
-def scan_kernel(lo, hi, x, bc, cum, cum_t, chunk, spread, wide, d_skip, y, scores, b_t, lines):
-    rows = x.shape[0]
+def head_offsets(lanes, heads, parts):
+    row = lax.broadcasted_iota(jnp.int32, (128, heads * lanes), 0)
+    col = lax.broadcasted_iota(jnp.int32, (128, heads * lanes), 1)
+    return jnp.where(row < 32 * parts, (row & 31) - col // lanes, -1000)
+
+
+def scan_kernel(
+    x, bc, cum, cum_t, chunk, d_skip, y, scores, b_t, lines, narrow, wide, steps, tails, insides, times
+):
+    rows, inner = x.shape
+    narrow[...] = head_offsets(64, 4, 2)
+    wide[...] = head_offsets(GROUP, 4, 3)
     lower = lax.broadcasted_iota(jnp.int32, (GROUP, GROUP), 0) >= lax.broadcasted_iota(
         jnp.int32, (GROUP, GROUP), 1
     )
@@ -228,16 +243,19 @@
 
     def group(g, _):
         cols = pl.ds(pl.multiple_of(g * BLK, BLK), BLK)
-        to = pl.ds(pl.multiple_of((g - lo) * BLK, BLK), BLK)
-        sp = spread[:, cols]
-        wd = wide[:, pl.ds(pl.multiple_of(g * 4 * GROUP, 4 * GROUP), 4 * GROUP)]
+        sp = (narrow[...] == 4 * g).astype(F32).astype(BF)
+        wd = (wide[...] == 4 * g).astype(F32).astype(BF)
         skip = dot(lines[...], sp)[:1]
         before = jnp.zeros((128, BLK), F32)
+        steps[...] = dot(chunk[0], sp)
+        tails[...] = dot(chunk[1], sp)
+        insides[...] = dot(chunk[2], sp)
+        times[...] = dot(cum[...], wd)
         for c, part in enumerate(blocks(rows, GROUP)):
             xc = x[part, cols].astype(F32)
-            stepped = xc * dot(chunk[0, part], sp)
-            inside = dot(chunk[2, part], sp)
-            own = dot(cum[part], wd)
+            stepped = xc * steps[part]
+            inside = insides[part]
+            own = times[part]
             out = xc * skip
             if c:
                 out = out + dot(bc[part, 128:], before.astype(BF)) * inside
@@ -252,32 +270,37 @@
                     [jnp.where(left, pair, 0.0), jnp.where(left, 0.0, pair)], axis=0
                 ).astype(BF)
                 pairs.append(dot(jnp.concatenate(weights, axis=1), stacked))
-            y[part, to] = (out + jnp.concatenate(pairs, axis=1)).astype(BF)
+            y[part, cols] = (out + jnp.concatenate(pairs, axis=1)).astype(BF)
             if c < rows // GROUP - 1:
-                tailed = (xc * dot(chunk[1, part], sp)).astype(BF)
+                tailed = (xc * tails[part]).astype(BF)
                 before = before * inside[GROUP - 1 :] + dot(b_t[:, part], tailed)
         return 0
 
-    lax.fori_loop(lo, hi, group, 0)
+    lax.fori_loop(0, inner // BLK, group, 0)
 
 
 def out_kernel(
-    y_a, y_b, bc, kept, got, shard, z, ev, norm_gain, w_out, final_gain, wanted, spread,
+    y, bc, kept, got, shard, z, ev, norm_gain, w_out, final_gain, wanted, spread,
     out, picked, mixed, square, enter, total, final,
 ):
     rows, inner = z.shape
-    split = y_a.shape[1]
     width = ev.shape[1]
     half = inner // 2
     first = lax.axis_index("core") == 0
     enter[:, :half] = jnp.where(first, kept[...], got[...])
     enter[:, half:] = jnp.where(first, got[...], kept[...])
-    for n, cols in enumerate(blocks(inner, BLK)):
-        state = dot(bc[:, 128:], enter[:, cols])
-        decay = dot(shard[1], spread[:, cols])
+    tiles = blocks(inner, BLK)
+
+    def spread_state(n):
+        return dot(bc[:, 128:], enter[:, tiles[n]]), dot(shard[1], spread[:, tiles[n]])
+
+    ahead = spread_state(0)
+    for n, cols in enumerate(tiles):
+        state, decay = ahead
+        if n + 1 < len(tiles):
+            ahead = spread_state(n + 1)
         for part in blocks(rows, PART):
-            y = y_a[part, cols] if cols.stop <= split else y_b[part, cols.start - split : cols.stop - split]
-            v = y.astype(F32) + state[part] * decay[part]
+            v = y[part, cols].astype(F32) + state[part] * decay[part]
             v = v * silu(z[part, cols].astype(F32))
             sq = v * v
             sq = sq[:, :128] + sq[:, 128:]
@@ -318,6 +341,7 @@
 
 def logit_kernel(block_id, temper, own, got, items, stats, rows, ids, scale):
     count, width = own.shape[0], items.shape[1]
+    tiles = blocks(items.shape[0], 512)
     first = lax.axis_index("core") == 0
     for part in blocks(count, PART):
         mine, other = own[part], got[part]
@@ -339,7 +363,7 @@
     total = jnp.zeros(scale.shape, F32)
     hit = jnp.zeros(scale.shape, F32)
     base = ids[...] - block_id[0] * items.shape[0]
-    for part in blocks(items.shape[0], 512):
+    for part in tiles:
         logit = dot_nt(items[part], rows[...]) * scale[...]
         place = lax.broadcasted_iota(jnp.int32, logit.shape, 0)
         hit = hit + jnp.sum(jnp.where(place == base - part.start, logit, 0.0), axis=0, keepdims=True)
@@ -354,6 +378,16 @@
     stats[...] = jnp.transpose(lines)[:, :16]
 
 
+def loss_kernel(seen, loss):
+    parts = []
+    for n in (0, 8):
+        top, total, hit = [seen[:, :, n + i : n + i + 1] for i in range(3)]
+        peak = jnp.max(top, axis=0)
+        whole = jnp.sum(total * jnp.exp(top - peak[None]), axis=0)
+        parts.append(peak + jnp.log(whole) - jnp.sum(hit, axis=0))
+    loss[...] = jnp.concatenate(parts, axis=0)
+
+
 def local(
     events, lengths, target_pos, target_ids, items, item_block, temper, in_gain, w_xbc, w_z, w_dt,
     conv_w, conv_b, dt_bias, a_log, d_skip, norm_gain, w_out, final_gain,
@@ -362,7 +396,6 @@
     inner = w_z.shape[1]
     ev = events[0]
     spread = expander(32, 64, 2)
-    wide = expander(32, GROUP, 3)
     chunks = rows // GROUP
 
     with jax.named_scope("halo"):
@@ -384,8 +417,8 @@
                 pltpu.VMEM((conv_b.shape[0] // 128, 128), F32), pltpu.VMEM(spread.shape, BF),
                 pltpu.VMEM((rows + HALO, width), BF), pltpu.VMEM((rows, inner), BF),
                 pltpu.VMEM((2, 2, rows + HALO, 128), F32),
-                pltpu.VMEM((2, rows, BLK), F32), pltpu.VMEM((2, rows, BLK), BF),
-                pltpu.VMEM((128, rows), BF), pltpu.VMEM((144, inner), BF),
+                pltpu.VMEM((2, rows + 16, BLK), F32), pltpu.VMEM((2, rows, BLK), BF),
+                pltpu.VMEM((128, rows), BF), pltpu.VMEM((144, inner), BF), pltpu.VMEM((rows + 16, 128), BF),
                 pltpu.SemaphoreType.DMA((10,)), pltpu.SemaphoreType.DMA((9,)),
             ],
             2 * rows * width * 2304,
@@ -396,46 +429,43 @@
             conv_b.reshape(-1, 128), spread,
         )
 
-    def scan(lo, hi, x):
-        return call(
-            lambda *refs: scan_kernel(lo, hi, *refs),
-            shape(rows, (hi - lo) * BLK),
-            [VMEM] * 8,
-            [
-                pltpu.VMEM((chunks, GROUP, GROUP), F32), pltpu.VMEM((128, rows), BF),
-                pltpu.VMEM((16, 128), BF),
-            ],
-            16 * rows * 128 * (hi - lo) * BLK,
-        )(x, bc, cum, cum_t, chunk, spread, wide, d_skip[None])
-
     swap = [(0, 1), (1, 0)]
     payload = shape(144, inner // 2)
     entry = shape(128, inner // 2)
     with jax.named_scope("chip"):
         got = lax.ppermute(send, "core", swap)
         chip = call(chip_kernel, payload, [VMEM] * 2)(keep, got)
-        sent, x = lax.optimization_barrier((chip, x))
-        near = lax.ppermute(sent, "x", [(0, 1), (1, 0), (2, 3), (3, 2)])
+        before = [
+            lax.ppermute(chip, "x", [(i, i + n) for i in range(4 - n)]) for n in (1, 2, 3)
+        ]
+        x, chip = lax.optimization_barrier((x, chip))
     with jax.named_scope("scan"):
-        y_a = scan(0, 5, x)
-    with jax.named_scope("pair"):
-        pair = call(pair_kernel, payload, [VMEM] * 2)(chip, near)
-        sent, y_a, x, source = lax.optimization_barrier((pair, y_a, x, normed))
-        far = lax.ppermute(sent, "x", [(1, 2), (0, 3)])
+        y = call(
+            scan_kernel,
+            shape(rows, inner),
+            [VMEM] * 6,
+            [
+                pltpu.VMEM((chunks, GROUP, GROUP), F32), pltpu.VMEM((128, rows), BF),
+                pltpu.VMEM((16, 128), BF), pltpu.VMEM((128, BLK), jnp.int32),
+                pltpu.VMEM((128, 4 * GROUP), jnp.int32), pltpu.VMEM((rows, BLK), F32),
+                pltpu.VMEM((rows, BLK), F32), pltpu.VMEM((rows, BLK), F32), pltpu.VMEM((rows, 4 * GROUP), F32),
+            ],
+            16 * rows * 128 * inner,
+            limit=56,
+        )(x, bc, cum, cum_t, chunk, d_skip[None])
+        y, source = lax.optimization_barrier((y, normed))
     with jax.named_scope("gate"):
         z = dot(source, w_z).astype(BF)
-    with jax.named_scope("scan"):
-        y_b = scan(5, 8, x)
+        before, z = lax.optimization_barrier((before, z))
     with jax.named_scope("enter"):
-        here, away = call(enter_kernel, [entry, entry], [VMEM] * 4)(keep, got, near, far)
-        away, z, y_b = lax.optimization_barrier((away, z, y_b))
+        here, away = call(enter_kernel, [entry, entry], [VMEM] * 5)(keep, got, *before)
         there = lax.ppermute(away, "core", swap)
 
     with jax.named_scope("out"):
         out, picked = call(
             out_kernel,
             [shape(rows, width), shape(8, 4, width)],
-            [VMEM] * 13,
+            [VMEM] * 12,
             [
                 pltpu.VMEM((rows, inner), BF), pltpu.VMEM((rows, 128), F32), pltpu.VMEM((128, inner), BF),
                 pltpu.VMEM((rows, width), F32), pltpu.VMEM((rows, width), BF),
@@ -443,7 +473,7 @@
             2 * rows * inner * (width + 256),
             limit=14,
         )(
-            y_a, y_b, bc, here, there, shard, z, ev, norm_gain[None], w_out, final_gain[None], target_pos,
+            y, bc, here, there, shard, z, ev, norm_gain[None], w_out, final_gain[None], target_pos,
             spread,
         )
 
@@ -466,11 +496,7 @@
 
     with jax.named_scope("loss"):
         seen = lax.all_to_all(stats.reshape(128, 2, 16), EACH, 0, 0, tiled=True)
-        top, total, hit = [
-            jnp.concatenate([seen[:, :, n], seen[:, :, n + 8]], axis=1) for n in range(3)
-        ]
-        peak = jnp.max(top, axis=0)
-        loss = peak + jnp.log(jnp.sum(total * jnp.exp(top - peak), axis=0)) - jnp.sum(hit, axis=0)
+        loss = call(loss_kernel, shape(4, 1, dtype=F32), [VMEM])(seen).reshape(4)
     return (out[None], loss)
 
 

time: 120 us -> 112 us (0.933)
  local copies, waits for them, and re-layouts: 12.6 us -> 6.02 us
  starting transfers between devices: 13.1 us -> 16.6 us
  Pallas kernels: 37.8 us -> 35.1 us
  blocking collectives: 45.9 us -> 44.2 us
    unnamed x58 -> x34, local copies, waits for them, and re-layouts: 10.7 us -> 5.03 us
    ppermute x2 -> x3, starting transfers between devices: 6.31 us -> 9.91 us  [local(): lax.ppermute(chip, 'x', [(i, i + n) for i in range(4 - n)])]
    pallas_call x1, Pallas kernels: 13.4 us -> 10.7 us  [local(): call(mix_kernel, [shape(rows, width), shape(rows, 128), shape(8, 4, rows,...]
    all_to_all x1, blocking collectives: 9.29 us -> 7.59 us  [local(): mine = lax.all_to_all(picked, SEQ, 0, 0, tiled=True)]
    pallas_call x5 -> x4, Pallas kernels: 16.9 us -> 16.9 us  [the longest x1 10.8 us: local(): call(scan_kernel, shape(rows, inner), [VMEM] * 6, [pltpu.VMEM((chunks, GR...]
  transfers between devices with their start and end apart: 6 -> 7, of which waited for: 4 -> 4; matrix products, arithmetic and copies ran while one was open for 2% -> 2% of each run, Pallas kernels for 9% -> 10%
where the time goes in v3:
time: 112 us; the launch traced here: 111 us
  blocking collectives  44.2 us (39%)
  Pallas kernels  35.1 us (31%)
  starting transfers between devices  16.6 us (15%)
  local copies, waits for them, and re-layouts  6.02 us (5%)
  waiting for transfers between devices  4.28 us (4%)
  matrix products  2.34 us (2%)
  between operations  2.19 us (2%)
    all_to_all x1, blocking collectives, local(): lax.all_to_all(sent, EACH, 0, 0, tiled=True).reshape(256, width + 128)  22.4 us
    all_to_all x1, blocking collectives, local(): seen = lax.all_to_all(stats.reshape(128, 2, 16), EACH, 0, 0, tiled=True)  14.2 us
    pallas_call x1, Pallas kernels, local(): call(scan_kernel, shape(rows, inner), [VMEM] * 6, [pltpu.VMEM((chunks, GR...  10.8 us
    pallas_call x1, Pallas kernels, local(): call(mix_kernel, [shape(rows, width), shape(rows, 128), shape(8, 4, rows,...  10.7 us
    ppermute x3, starting transfers between devices, local(): lax.ppermute(chip, 'x', [(i, i + n) for i in range(4 - n)])  9.91 us
    all_to_all x1, blocking collectives, local(): mine = lax.all_to_all(picked, SEQ, 0, 0, tiled=True)  7.59 us
    pallas_call x1, Pallas kernels, local(): call(logit_kernel, shape(256, 16, dtype=F32), [SMEM, SMEM, VMEM, VMEM, VM...  6.77 us
    pallas_call x1, Pallas kernels, local(): call(out_kernel, [shape(rows, width), shape(8, 4, width)], [VMEM] * 12, [...  5.29 us
  transfers between devices with their start and end apart: 7, of which 4 were waited for; matrix products, arithmetic and copies ran while one was open for 2% of the time, Pallas kernels for 10%

profile of v3, /device:TPU:1, one launch (start us, length us, event | category | flops | bytes accessed | tf_op | source)
XLA Modules:
  0.0 111.3 jit_solution(14639511210275470601)
XLA Ops:
  0.6 0.8 slice_bitcast_fusion
  1.4 4.5 %collective-permute-start = (bf16[16,1024]{1,0:T(8,128)(2,1)S(1)}, bf16[16,1024]{1,0:T(8,128)(2,1)S(1)}, u32[]{:S(2)}, u32[]{:S(2)}) collective-permute-start(bf16[16,1024]{1,0:T(8,128)(2,1)S(1)} %slice_bitcast_fusion), channel_id=1, source_target_pairs={{0,16},{16,32},{32,48},{48,64},{64,80},{80,96},{96,112},{1,17},{17... | collective-permute-start | bytes 98312 | tf_op jit(solution)/shard_map/halo/ppermute | solution.py:402
  6.9 0.6 copy-done.15
  7.5 10.7 %mix.1 = (bf16[512,1024]{1,0:T(8,128)(2,1)}, bf16[512,128]{1,0:T(8,128)(2,1)}, f32[8,4,512]{2,1,0:T(4,128)}, bf16[2,512,128]{2,1,0:T(8,128)(2,1)}, bf16[3,512,12...) custom-call(s32[1]{0:T(128)S(6)} %copy.22.length, ...), custom_call_target="tpu_custom_call" | custom-call | flops 2415919104 | tf_op jit(solution)/shard_map/mix/pallas_call | solution.py:405
  18.3 1.8 %collective-permute-done.1.got = bf16[144,1024]{1,0:T(8,128)(2,1)S(1)} collective-permute-done((bf16[144,1024]{1,0:T(8,128)(2,1)}, bf16[144,1024]{1,0:T(8,128)(2,1)S(1)}, u32[]{:S(2)}, u32[]{:S(2)}) %collective-permute-start.1) | collective-permute-done | bytes 294944 | tf_op jit(solution)/shard_map/chip/ppermute | solution.py:436
  20.1 1.0 copy-done.2
  21.2 4.2 %collective-permute-start.2 = (bf16[144,1024]{1,0:T(8,128)(2,1)S(1)}, bf16[144,1024]{1,0:T(8,128)(2,1)S(1)}, u32[]{:S(2)}, u32[]{:S(2)}) collective-permute-start(bf16[144,1024]{1,0:T(8,128)(2,1)S(1)} %chip.1), channel_id=1, source_target_pairs={{0,32},{32,64},{64,96},{1,33},{33,65},{65,97},{2,34},{34,66},{66,9... | collective-permute-start | bytes 884744 | tf_op jit(solution)/shard_map/chip/ppermute | solution.py:439
  25.5 4.4 %collective-permute-start.3 = (bf16[144,1024]{1,0:T(8,128)(2,1)S(1)}, bf16[144,1024]{1,0:T(8,128)(2,1)S(1)}, u32[]{:S(2)}, u32[]{:S(2)}) collective-permute-start(bf16[144,1024]{1,0:T(8,128)(2,1)S(1)} %chip.1), channel_id=1, source_target_pairs={{0,64},{32,96},{1,65},{33,97},{2,66},{34,98},{3,67},{35,99},{4,68}... | collective-permute-start | bytes 884744 | tf_op jit(solution)/shard_map/chip/ppermute | solution.py:439
  29.8 1.3 %collective-permute-start.4 = (bf16[144,1024]{1,0:T(8,128)(2,1)S(1)}, bf16[144,1024]{1,0:T(8,128)(2,1)S(1)}, u32[]{:S(2)}, u32[]{:S(2)}) collective-permute-start(bf16[144,1024]{1,0:T(8,128)(2,1)S(1)} %chip.1), channel_id=1, source_target_pairs={{0,96},{1,97},{2,98},{3,99},{4,100},{5,101},{6,102},{7,103},{8,104... | collective-permute-start | bytes 884744 | tf_op jit(solution)/shard_map/chip/ppermute | solution.py:439
  31.1 10.8 %scan.1.y = bf16[512,2048]{1,0:T(8,128)(2,1)} custom-call(bf16[512,2048]{1,0:T(8,128)(2,1)} %get-tuple-element.25.x, bf16[512,256]{1,0:T(8,128)(2,1)} %get-tuple-element.26.bc, bf16[512,128]{1,0:T(8,128)(2,1)} %get-tuple-element.27.cum, f32[8,4,512]{2,1,0:T(4,128)} %get-tuple-element.28.cum_t, bf16[3,512,128]{2,1,0:T(8,128)(2,1)} %get-tuple-element.29.chunk, ...), custom_call_target="tpu_custom_call" | custom-call | flops 2147483648 | tf_op jit(solution)/shard_map/scan/pallas_call | solution.py:443
  42.0 2.3 %convolution_convert_fusion.z = bf16[512,2048]{1,0:T(8,128)(2,1)S(1)} fusion(bf16[512,1024]{1,0:T(8,128)(2,1)S(1)} %copy-done.16, bf16[1024,2048]{1,0:T(8,128)(2,1)S(1)} %copy-done.14), kind=kOutput, calls=%fused_computation | convolution fusion | flops 2148532224 | bytes 7340032 | tf_op jit(solution)/shard_map/gate/dot_general | solution.py:54
  44.7 1.2 %collective-permute-start.5 = (bf16[128,1024]{1,0:T(8,128)(2,1)S(1)}, bf16[128,1024]{1,0:T(8,128)(2,1)S(1)}, u32[]{:S(2)}, u32[]{:S(2)}) collective-permute-start(bf16[128,1024]{1,0:T(8,128)(2,1)S(1)} %get-tuple-element.37), channel_id=1, source_target_pairs={{0,16},{16,0},{1,17},{17,1},{2,18},{18,2},{3,19},{19,3},{4,20},{20... | collective-permute-start | bytes 786440 | tf_op jit(solution)/shard_map/enter/ppermute | solution.py:462
  45.9 1.2 %collective-permute-done.5.got = bf16[128,1024]{1,0:T(8,128)(2,1)S(1)} collective-permute-done((bf16[128,1024]{1,0:T(8,128)(2,1)S(1)}, bf16[128,1024]{1,0:T(8,128)(2,1)S(1)}, u32[]{:S(2)}, u32[]{:S(2)}) %collective-permute-start.5) | collective-permute-done | bytes 262176 | tf_op jit(solution)/shard_map/enter/ppermute | solution.py:462
  47.1 5.3 %out.1 = (bf16[512,1024]{1,0:T(8,128)(2,1)}, bf16[8,4,1024]{2,1,0:T(4,128)(2,1)S(1)}) custom-call(bf16[512,2048]{1,0:T(8,128)(2,1)S(1)} %copy-done.1, bf16[512,256]{1,0:T(8,128)(2,1)S(1)} %copy-done.7, bf16[128,1024]{1,0:T(8,128)(2,1)S(1)} %get-tuple-element.36.kept, bf16[128,1024]{1,0:T(8,128)(2,1)S(1)} %collective-permute-done.5.got, ...), custom_call_target="tpu_custom_call" | custom-call | flops 2684354560 | tf_op jit(solution)/shard_map/out/pallas_call | solution.py:465
  52.4 7.6 %all_to_all.15.got = bf16[8,4,1024]{2,1,0:T(4,128)(2,1)S(1)} all-to-all(bf16[8,4,1024]{2,1,0:T(4,128)(2,1)S(1)} %get-tuple-element.41), channel_id=1, replica_groups=mesh['x'=4,'core'=2,'cand'=16] {'x','core'}, dimensions={0} | all-to-all | bytes 131072 | tf_op jit(solution)/shard_map/rows/all_to_all | solution.py:481
  60.0 0.6 rows.1
  60.7 22.4 %all_to_all.16 = bf16[128,2,1152]{2,1,0:T(2,128)(2,1)S(1)} all-to-all(bf16[128,2,1152]{2,1,0:T(2,128)(2,1)S(1)} %rows.1), channel_id=1, replica_groups=mesh['x'=4,'core'=2,'cand'=16] {'core','x','cand'}, dimensions={0} | all-to-all | bytes 1179648 | tf_op jit(solution)/shard_map/rows/all_to_all | solution.py:483
  83.3 0.9 collective-permute-start.6
  84.9 1.0 collective-permute-done.6.got
  85.9 3.4 %copy-done.11 = bf16[4096,1024]{1,0:T(8,128)(2,1)S(1)} copy-done((bf16[4096,1024]{1,0:T(8,128)(2,1)S(1)}, bf16[4096,1024]{1,0:T(8,128)(2,1)}, u32[]{:S(2)}) %copy-start.11) | copy-done | bytes 8388632
  89.3 6.8 %logits.1 = f32[256,16]{1,0:T(8,128)S(1)} custom-call(s32[1]{0:T(128)S(6)} %copy.23.block_id, f32[16]{0:T(128)S(1)} %copy-done.13, bf16[256,1152]{1,0:T(8,128)(2,1)S(1)} %reshape.18.own, bf16[256,1152]{1,0:T(8,128)(2,1)S(1)} %collective-permute-done.6.got, bf16[4096,1024]{1,0:T(8,128)(2,1)S(1)} %copy-done.11), custom_call_target="tpu_custom_call" | custom-call | flops 4294967296 | tf_op jit(solution)/shard_map/logits/pallas_call | solution.py:487
  96.0 14.2 %all_to_all.17.seen = f32[128,2,16]{2,1,0:T(2,128)S(1)} all-to-all(f32[128,2,16]{2,1,0:T(2,128)S(1)} %bitcast.17), channel_id=1, replica_groups=mesh['x'=4,'core'=2,'cand'=16] {'core','x','cand'}, dimensions={0} | all-to-all | bytes 32768 | tf_op jit(solution)/shard_map/loss/all_to_all | solution.py:498
  110.2 0.5 loss.1
  110.7 0.6 reduce
  (39 shorter events, 1.1 us)
Async XLA Ops:
  1.4 5.5 %collective-permute-start = (bf16[16,1024]{1,0:T(8,128)(2,1)S(1)}, bf16[16,1024]{1,0:T(8,128)(2,1)S(1)}, u32[]{:S(2)}, u32[]{:S(2)}) collective-permute-start(bf16[16,1024]{1,0:T(8,128)(2,1)S(1)} %slice_bitcast_fusion), channel_id=1, source_target_pairs={{0,16},{16,32},{32,48},{48,64},{64,80},{80,96},{96,112},{1,17},{17... | collective-permute-start | bytes 98312 | tf_op jit(solution)/shard_map/halo/ppermute | solution.py:402
  6.9 0.6 copy-start.15
  18.2 1.9 %collective-permute-start.1 = (bf16[144,1024]{1,0:T(8,128)(2,1)}, bf16[144,1024]{1,0:T(8,128)(2,1)S(1)}, u32[]{:S(2)}, u32[]{:S(2)}) collective-permute-start(bf16[144,1024]{1,0:T(8,128)(2,1)} %get-tuple-element.24), channel_id=1, source_target_pairs={{0,16},{16,0},{1,17},{17,1},{2,18},{18,2},{3,19},{19,3},{4,20},{20... | collective-permute-start | bytes 884744 | tf_op jit(solution)/shard_map/chip/ppermute | solution.py:436
  20.1 1.0 copy-start.2
  21.2 20.7 %copy-start.14 = (bf16[1024,2048]{1,0:T(8,128)(2,1)S(1)}, bf16[1024,2048]{1,0:T(8,128)(2,1)}, u32[]{:S(2)}) copy-start(bf16[1024,2048]{1,0:T(8,128)(2,1)} %param.29) | copy-start | bytes 12582916
  21.2 20.7 %copy-start.16 = (bf16[512,1024]{1,0:T(8,128)(2,1)S(1)}, bf16[512,1024]{1,0:T(8,128)(2,1)}, u32[]{:S(2)}) copy-start(bf16[512,1024]{1,0:T(8,128)(2,1)} %get-tuple-element.32) | copy-start | bytes 3145732
  21.2 23.2 %collective-permute-start.2 = (bf16[144,1024]{1,0:T(8,128)(2,1)S(1)}, bf16[144,1024]{1,0:T(8,128)(2,1)S(1)}, u32[]{:S(2)}, u32[]{:S(2)}) collective-permute-start(bf16[144,1024]{1,0:T(8,128)(2,1)S(1)} %chip.1), channel_id=1, source_target_pairs={{0,32},{32,64},{64,96},{1,33},{33,65},{65,97},{2,34},{34,66},{66,9... | collective-permute-start | bytes 884744 | tf_op jit(solution)/shard_map/chip/ppermute | solution.py:439
  25.5 18.9 %collective-permute-start.3 = (bf16[144,1024]{1,0:T(8,128)(2,1)S(1)}, bf16[144,1024]{1,0:T(8,128)(2,1)S(1)}, u32[]{:S(2)}, u32[]{:S(2)}) collective-permute-start(bf16[144,1024]{1,0:T(8,128)(2,1)S(1)} %chip.1), channel_id=1, source_target_pairs={{0,64},{32,96},{1,65},{33,97},{2,66},{34,98},{3,67},{35,99},{4,68}... | collective-permute-start | bytes 884744 | tf_op jit(solution)/shard_map/chip/ppermute | solution.py:439
  29.8 14.6 %collective-permute-start.4 = (bf16[144,1024]{1,0:T(8,128)(2,1)S(1)}, bf16[144,1024]{1,0:T(8,128)(2,1)S(1)}, u32[]{:S(2)}, u32[]{:S(2)}) collective-permute-start(bf16[144,1024]{1,0:T(8,128)(2,1)S(1)} %chip.1), channel_id=1, source_target_pairs={{0,96},{1,97},{2,98},{3,99},{4,100},{5,101},{6,102},{7,103},{8,104... | collective-permute-start | bytes 884744 | tf_op jit(solution)/shard_map/chip/ppermute | solution.py:439
  41.9 2.5 %copy-start.3 = (bf16[144,1024]{1,0:T(8,128)(2,1)S(1)}, bf16[144,1024]{1,0:T(8,128)(2,1)}, u32[]{:S(2)}) copy-start(bf16[144,1024]{1,0:T(8,128)(2,1)} %get-tuple-element.23.keep) | copy-start | bytes 884740
  41.9 5.1 %copy-start = (bf16[2048,1024]{1,0:T(8,128)(2,1)S(1)}, bf16[2048,1024]{1,0:T(8,128)(2,1)}, u32[]{:S(2)}) copy-start(bf16[2048,1024]{1,0:T(8,128)(2,1)} %w_out.1) | copy-start | bytes 12582916
  41.9 5.1 %copy-start.1 = (bf16[512,2048]{1,0:T(8,128)(2,1)S(1)}, bf16[512,2048]{1,0:T(8,128)(2,1)}, u32[]{:S(2)}) copy-start(bf16[512,2048]{1,0:T(8,128)(2,1)} %scan.1.y) | copy-start | bytes 6291460
  42.0 5.1 %copy-start.4 = (bf16[1,512,1024]{2,1,0:T(8,128)(2,1)S(1)}, bf16[1,512,1024]{2,1,0:T(8,128)(2,1)}, u32[]{:S(2)}) copy-start(bf16[1,512,1024]{2,1,0:T(8,128)(2,1)} %param.20) | copy-start | bytes 3145732
  42.0 5.1 %copy-start.5 = (bf16[128,2048]{1,0:T(8,128)(2,1)S(1)}, bf16[128,2048]{1,0:T(8,128)(2,1)}, u32[]{:S(2)}) copy-start(bf16[128,2048]{1,0:T(8,128)(2,1)} %constant.2.clone.spread_h.spread) | copy-start | bytes 1572868
  42.0 5.1 %copy-start.6 = (bf16[2,512,128]{2,1,0:T(8,128)(2,1)S(1)}, bf16[2,512,128]{2,1,0:T(8,128)(2,1)}, u32[]{:S(2)}) copy-start(bf16[2,512,128]{2,1,0:T(8,128)(2,1)} %get-tuple-element.38.shard) | copy-start | bytes 786436
  42.0 5.1 %copy-start.7 = (bf16[512,256]{1,0:T(8,128)(2,1)S(1)}, bf16[512,256]{1,0:T(8,128)(2,1)}, u32[]{:S(2)}) copy-start(bf16[512,256]{1,0:T(8,128)(2,1)} %get-tuple-element.26.bc) | copy-start | bytes 786436
  42.0 5.1 %copy-start.8 = (f32[2048]{0:T(1024)S(1)}, f32[2048]{0:T(1024)}, u32[]{:S(2)}) copy-start(f32[2048]{0:T(1024)} %param.36) | copy-start | bytes 24580
  42.0 5.1 %copy-start.9 = (f32[1024]{0:T(1024)S(1)}, f32[1024]{0:T(1024)}, u32[]{:S(2)}) copy-start(f32[1024]{0:T(1024)} %param.38) | copy-start | bytes 12292
  42.0 5.1 %copy-start.10 = (s32[1,32]{1,0:T(1,128)S(1)}, s32[1,32]{1,0:T(1,128)}, u32[]{:S(2)}) copy-start(s32[1,32]{1,0:T(1,128)} %wanted.1) | copy-start | bytes 388
  44.7 2.4 %collective-permute-start.5 = (bf16[128,1024]{1,0:T(8,128)(2,1)S(1)}, bf16[128,1024]{1,0:T(8,128)(2,1)S(1)}, u32[]{:S(2)}, u32[]{:S(2)}) collective-permute-start(bf16[128,1024]{1,0:T(8,128)(2,1)S(1)} %get-tuple-element.37), channel_id=1, source_target_pairs={{0,16},{16,0},{1,17},{17,1},{2,18},{18,2},{3,19},{19,3},{4,20},{20... | collective-permute-start | bytes 786440 | tf_op jit(solution)/shard_map/enter/ppermute | solution.py:462
  47.1 12.9 %copy-start.12 = (s32[1,4]{1,0:T(1,128)S(1)}, s32[1,4]{1,0:T(1,128)}, u32[]{:S(2)}) copy-start(s32[1,4]{1,0:T(1,128)} %ids.1) | copy-start | bytes 52
  60.0 25.9 %copy-start.13 = (f32[16]{0:T(128)S(1)}, f32[16]{0:T(128)}, u32[]{:S(2)}) copy-start(f32[16]{0:T(128)} %temper.1) | copy-start | bytes 196
  83.3 2.6 %collective-permute-start.6 = (bf16[256,1152]{1,0:T(8,128)(2,1)S(1)}, bf16[256,1152]{1,0:T(8,128)(2,1)S(1)}, u32[]{:S(2)}, u32[]{:S(2)}) collective-permute-start(bf16[256,1152]{1,0:T(8,128)(2,1)S(1)} %reshape.18.own), channel_id=1, source_target_pairs={{0,16},{16,0},{1,17},{17,1},{2,18},{18,2},{3,19},{19,3},{4,20},{20... | collective-permute-start | bytes 1769480 | tf_op jit(solution)/shard_map/rows/ppermute | solution.py:484
  85.9 3.4 %copy-start.11 = (bf16[4096,1024]{1,0:T(8,128)(2,1)S(1)}, bf16[4096,1024]{1,0:T(8,128)(2,1)}, u32[]{:S(2)}) copy-start(bf16[4096,1024]{1,0:T(8,128)(2,1)} %items.1) | copy-start | bytes 25165828

commit v4 on v3

--- a/solution.py
+++ b/solution.py
@@ -11,6 +11,7 @@
 BLK = 256
 HALO = 16
 PART = 64
+LOG2E = 1.4426950408889634
 BF = jnp.bfloat16
 F32 = jnp.float32
 SEQ = ("x", "core")
@@ -119,8 +120,9 @@
     cum = dot(lower, packed(logdec, 3))
     cum = cum + pltpu.roll(cum, 32, 1)
     cum = cum + pltpu.roll(cum, 64, 1)
-    cum_out[...] = packed(cum, 3)
-    flipped = jnp.transpose(cum)
+    scaled = cum * LOG2E
+    cum_out[...] = packed(scaled, 3)
+    flipped = jnp.transpose(scaled)
     for g in range(8):
         cum_t[g] = flipped[4 * g : 4 * g + 4]
     shard[0] = packed(jnp.exp(cum[rows - 1 :] - cum) * step, 2)
@@ -227,7 +229,7 @@
 
 
 def scan_kernel(
-    x, bc, cum, cum_t, chunk, d_skip, y, scores, b_t, lines, narrow, wide, steps, tails, insides, times
+    x, bc, cum, cum_t, chunk, d_skip, y, scores, b_t, firsts, narrow, wide, steps, tails, insides, times
 ):
     rows, inner = x.shape
     narrow[...] = head_offsets(64, 4, 2)
@@ -235,48 +237,57 @@
     lower = lax.broadcasted_iota(jnp.int32, (GROUP, GROUP), 0) >= lax.broadcasted_iota(
         jnp.int32, (GROUP, GROUP), 1
     )
-    for c, part in enumerate(blocks(rows, GROUP)):
-        scores[c] = jnp.where(lower, dot_nt(bc[part, 128:], bc[part, :128]), 0.0)
+    parts = blocks(rows, GROUP)
+    for c, part in enumerate(parts):
+        scores[c] = jnp.where(lower, dot_nt(bc[part, 128:], bc[part, :128]), 0.0).astype(BF)
     b_t[...] = jnp.transpose(bc[:, :128].astype(F32)).astype(BF)
-    lines[...] = packed(jnp.broadcast_to(four(d_skip[...]), (16, 128)), 2)
-    left = lax.broadcasted_iota(jnp.int32, (GROUP, 128), 1) < 64
-
-    def group(g, _):
-        cols = pl.ds(pl.multiple_of(g * BLK, BLK), BLK)
+    firsts[:rows] = chunk[0]
+    firsts[rows:] = packed(jnp.broadcast_to(four(d_skip[...]), (16, 128)), 2)
+    left = (lax.broadcasted_iota(jnp.int32, (GROUP, 128), 1) < 64).astype(F32).astype(BF)
+    right = (lax.broadcasted_iota(jnp.int32, (GROUP, 128), 1) >= 64).astype(F32).astype(BF)
+
+    def widen(g):
+        slot = g % 2
         sp = (narrow[...] == 4 * g).astype(F32).astype(BF)
         wd = (wide[...] == 4 * g).astype(F32).astype(BF)
-        skip = dot(lines[...], sp)[:1]
-        before = jnp.zeros((128, BLK), F32)
-        steps[...] = dot(chunk[0], sp)
-        tails[...] = dot(chunk[1], sp)
-        insides[...] = dot(chunk[2], sp)
-        times[...] = dot(cum[...], wd)
-        for c, part in enumerate(blocks(rows, GROUP)):
+        steps[slot] = dot(firsts[...], sp)
+        tails[slot] = dot(chunk[1], sp)
+        insides[slot] = dot(chunk[2], sp)
+        times[slot] = dot(cum[...], wd)
+
+    def group(g):
+        slot = g % 2
+        cols = slice(g * BLK, (g + 1) * BLK)
+        skip = steps[slot, rows : rows + 1]
+        before = None
+        entering = [None]
+        for part in parts[:-1]:
+            tailed = (x[part, cols].astype(F32) * tails[slot, part]).astype(BF)
+            new = dot(b_t[:, part], tailed)
+            before = new if before is None else before * insides[slot, part.stop - 1 : part.stop] + new
+            entering.append(before.astype(BF))
+        for c, part in enumerate(parts):
             xc = x[part, cols].astype(F32)
-            stepped = xc * steps[part]
-            inside = insides[part]
-            own = times[part]
+            stepped = (xc * steps[slot, part]).astype(BF)
             out = xc * skip
             if c:
-                out = out + dot(bc[part, 128:], before.astype(BF)) * inside
+                out = out + dot(bc[part, 128:], entering[c]) * insides[slot, part]
             pairs = []
             for p in range(2):
                 weights = []
                 for h in (2 * p, 2 * p + 1):
-                    diff = own[:, h * GROUP : (h + 1) * GROUP] - cum_t[g, h : h + 1, part]
-                    weights.append((scores[c] * jnp.exp(jnp.minimum(diff, 0.0))).astype(BF))
+                    diff = times[slot, part, h * GROUP : (h + 1) * GROUP] - cum_t[g, h : h + 1, part]
+                    weights.append(jnp.exp2(jnp.minimum(diff, 0.0)).astype(BF) * scores[c])
                 pair = stepped[:, p * 128 : (p + 1) * 128]
-                stacked = jnp.concatenate(
-                    [jnp.where(left, pair, 0.0), jnp.where(left, 0.0, pair)], axis=0
-                ).astype(BF)
+                stacked = jnp.concatenate([pair * left, pair * right], axis=0)
                 pairs.append(dot(jnp.concatenate(weights, axis=1), stacked))
             y[part, cols] = (out + jnp.concatenate(pairs, axis=1)).astype(BF)
-            if c < rows // GROUP - 1:
-                tailed = (xc * tails[part]).astype(BF)
-                before = before * inside[GROUP - 1 :] + dot(b_t[:, part], tailed)
-        return 0
-
-    lax.fori_loop(0, inner // BLK, group, 0)
+
+    widen(0)
+    for g in range(inner // BLK):
+        if g + 1 < inner // BLK:
+            widen(g + 1)
+        group(g)
 
 
 def out_kernel(
@@ -385,7 +396,7 @@
         peak = jnp.max(top, axis=0)
         whole = jnp.sum(total * jnp.exp(top - peak[None]), axis=0)
         parts.append(peak + jnp.log(whole) - jnp.sum(hit, axis=0))
-    loss[...] = jnp.concatenate(parts, axis=0)
+    loss[...] = jnp.concatenate([p[k : k + 1] for p in parts for k in range(2)], axis=1)
 
 
 def local(
@@ -445,10 +456,11 @@
             shape(rows, inner),
             [VMEM] * 6,
             [
-                pltpu.VMEM((chunks, GROUP, GROUP), F32), pltpu.VMEM((128, rows), BF),
-                pltpu.VMEM((16, 128), BF), pltpu.VMEM((128, BLK), jnp.int32),
-                pltpu.VMEM((128, 4 * GROUP), jnp.int32), pltpu.VMEM((rows, BLK), F32),
-                pltpu.VMEM((rows, BLK), F32), pltpu.VMEM((rows, BLK), F32), pltpu.VMEM((rows, 4 * GROUP), F32),
+                pltpu.VMEM((chunks, GROUP, GROUP), BF), pltpu.VMEM((128, rows), BF),
+                pltpu.VMEM((rows + 16, 128), BF), pltpu.VMEM((128, BLK), jnp.int32),
+                pltpu.VMEM((128, 4 * GROUP), jnp.int32), pltpu.VMEM((2, rows + 16, BLK), F32),
+                pltpu.VMEM((2, rows, BLK), F32), pltpu.VMEM((2, rows, BLK), F32),
+                pltpu.VMEM((2, rows, 4 * GROUP), F32),
             ],
             16 * rows * 128 * inner,
             limit=56,
@@ -479,7 +491,7 @@
 
     with jax.named_scope("rows"):
         mine = lax.all_to_all(picked, SEQ, 0, 0, tiled=True)
-        sent = call(rows_kernel, shape(128, 2, width + 128), [SMEM, VMEM], flops=10**10)(target_ids, mine)
+        sent = call(rows_kernel, shape(128, 2, width + 128), [SMEM, VMEM])(target_ids, mine)
         own_rows = lax.all_to_all(sent, EACH, 0, 0, tiled=True).reshape(256, width + 128)
         got_rows = lax.ppermute(own_rows, "core", swap)
 
@@ -496,7 +508,7 @@
 
     with jax.named_scope("loss"):
         seen = lax.all_to_all(stats.reshape(128, 2, 16), EACH, 0, 0, tiled=True)
-        loss = call(loss_kernel, shape(4, 1, dtype=F32), [VMEM])(seen).reshape(4)
+        loss = call(loss_kernel, shape(1, 4, dtype=F32), [VMEM])(seen).reshape(4)
     return (out[None], loss)
 
 

time: 112 us -> 110 us (0.982)
  Pallas kernels: 35.1 us -> 33.2 us
    pallas_call x1, Pallas kernels: 10.8 us -> 8.38 us  [local(): call(scan_kernel, shape(rows, inner), [VMEM] * 6, [pltpu.VMEM((chunks, GR...]
  transfers between devices with their start and end apart: 7 -> 7, of which waited for: 4 -> 4; matrix products, arithmetic and copies ran while one was open for 2% -> 2% of each run, Pallas kernels for 10% -> 8%
where the time goes in v4:
time: 110 us
  blocking collectives  45.2 us (41%)
  Pallas kernels  33.2 us (30%)
  starting transfers between devices  16.6 us (15%)
  local copies, waits for them, and re-layouts  6.03 us (5%)
  waiting for transfers between devices  4.28 us (4%)
  matrix products  2.34 us (2%)
  between operations  2.2 us (2%)
    all_to_all x1, blocking collectives, local(): lax.all_to_all(sent, EACH, 0, 0, tiled=True).reshape(256, width + 128)  22.4 us
    all_to_all x1, blocking collectives, local(): seen = lax.all_to_all(stats.reshape(128, 2, 16), EACH, 0, 0, tiled=True)  14.2 us
    pallas_call x1, Pallas kernels, local(): call(mix_kernel, [shape(rows, width), shape(rows, 128), shape(8, 4, rows,...  10.7 us
    ppermute x3, starting transfers between devices, local(): lax.ppermute(chip, 'x', [(i, i + n) for i in range(4 - n)])  10.1 us
    all_to_all x1, blocking collectives, local(): mine = lax.all_to_all(picked, SEQ, 0, 0, tiled=True)  8.67 us
    pallas_call x1, Pallas kernels, local(): call(scan_kernel, shape(rows, inner), [VMEM] * 6, [pltpu.VMEM((chunks, GR...  8.38 us
    pallas_call x1, Pallas kernels, local(): call(logit_kernel, shape(256, 16, dtype=F32), [SMEM, SMEM, VMEM, VMEM, VM...  6.78 us
    pallas_call x1, Pallas kernels, local(): call(out_kernel, [shape(rows, width), shape(8, 4, width)], [VMEM] * 12, [...  5.29 us
  transfers between devices with their start and end apart: 7, of which 4 were waited for; matrix products, arithmetic and copies ran while one was open for 2% of the time, Pallas kernels for 8%

profile of v4, /device:TPU:1, one launch (start us, length us, event | category | flops | bytes accessed | tf_op | source)
XLA Modules:
  0.0 110.0 jit_solution(8894651668383911099)
XLA Ops:
  0.6 0.8 slice_bitcast_fusion
  1.4 4.5 %collective-permute-start = (bf16[16,1024]{1,0:T(8,128)(2,1)S(1)}, bf16[16,1024]{1,0:T(8,128)(2,1)S(1)}, u32[]{:S(2)}, u32[]{:S(2)}) collective-permute-start(bf16[16,1024]{1,0:T(8,128)(2,1)S(1)} %slice_bitcast_fusion), channel_id=1, source_target_pairs={{0,16},{16,32},{32,48},{48,64},{64,80},{80,96},{96,112},{1,17},{17... | collective-permute-start | bytes 98312 | tf_op jit(solution)/shard_map/halo/ppermute | solution.py:413
  6.5 0.4 collective-permute-done.halo_h
  6.9 0.6 copy-done.15
  7.5 10.7 %mix.1 = (bf16[512,1024]{1,0:T(8,128)(2,1)}, bf16[512,128]{1,0:T(8,128)(2,1)}, f32[8,4,512]{2,1,0:T(4,128)}, bf16[2,512,128]{2,1,0:T(8,128)(2,1)}, bf16[3,512,12...) custom-call(s32[1]{0:T(128)S(6)} %copy.22.length, ...), custom_call_target="tpu_custom_call" | custom-call | flops 2415919104 | tf_op jit(solution)/shard_map/mix/pallas_call | solution.py:416
  18.3 1.8 %collective-permute-done.1.got = bf16[144,1024]{1,0:T(8,128)(2,1)S(1)} collective-permute-done((bf16[144,1024]{1,0:T(8,128)(2,1)}, bf16[144,1024]{1,0:T(8,128)(2,1)S(1)}, u32[]{:S(2)}, u32[]{:S(2)}) %collective-permute-start.1) | collective-permute-done | bytes 294944 | tf_op jit(solution)/shard_map/chip/ppermute | solution.py:447
  20.1 1.0 copy-done.2
  21.2 4.2 %collective-permute-start.2 = (bf16[144,1024]{1,0:T(8,128)(2,1)S(1)}, bf16[144,1024]{1,0:T(8,128)(2,1)S(1)}, u32[]{:S(2)}, u32[]{:S(2)}) collective-permute-start(bf16[144,1024]{1,0:T(8,128)(2,1)S(1)} %chip.1), channel_id=1, source_target_pairs={{0,32},{32,64},{64,96},{1,33},{33,65},{65,97},{2,34},{34,66},{66,9... | collective-permute-start | bytes 884744 | tf_op jit(solution)/shard_map/chip/ppermute | solution.py:450
  25.4 4.4 %collective-permute-start.3 = (bf16[144,1024]{1,0:T(8,128)(2,1)S(1)}, bf16[144,1024]{1,0:T(8,128)(2,1)S(1)}, u32[]{:S(2)}, u32[]{:S(2)}) collective-permute-start(bf16[144,1024]{1,0:T(8,128)(2,1)S(1)} %chip.1), channel_id=1, source_target_pairs={{0,64},{32,96},{1,65},{33,97},{2,66},{34,98},{3,67},{35,99},{4,68}... | collective-permute-start | bytes 884744 | tf_op jit(solution)/shard_map/chip/ppermute | solution.py:450
  29.8 1.5 %collective-permute-start.4 = (bf16[144,1024]{1,0:T(8,128)(2,1)S(1)}, bf16[144,1024]{1,0:T(8,128)(2,1)S(1)}, u32[]{:S(2)}, u32[]{:S(2)}) collective-permute-start(bf16[144,1024]{1,0:T(8,128)(2,1)S(1)} %chip.1), channel_id=1, source_target_pairs={{0,96},{1,97},{2,98},{3,99},{4,100},{5,101},{6,102},{7,103},{8,104... | collective-permute-start | bytes 884744 | tf_op jit(solution)/shard_map/chip/ppermute | solution.py:450
  31.3 8.4 %scan.1.y = bf16[512,2048]{1,0:T(8,128)(2,1)} custom-call(bf16[512,2048]{1,0:T(8,128)(2,1)} %get-tuple-element.25.x, bf16[512,256]{1,0:T(8,128)(2,1)} %get-tuple-element.26.bc, bf16[512,128]{1,0:T(8,128)(2,1)} %get-tuple-element.27.cum, f32[8,4,512]{2,1,0:T(4,128)} %get-tuple-element.28.cum_t, bf16[3,512,128]{2,1,0:T(8,128)(2,1)} %get-tuple-element.29.chunk, ...), custom_call_target="tpu_custom_call" | custom-call | flops 2147483648 | tf_op jit(solution)/shard_map/scan/pallas_call | solution.py:454
  39.8 2.3 %convolution_convert_fusion.z = bf16[512,2048]{1,0:T(8,128)(2,1)S(1)} fusion(bf16[512,1024]{1,0:T(8,128)(2,1)S(1)} %copy-done.16, bf16[1024,2048]{1,0:T(8,128)(2,1)S(1)} %copy-done.14), kind=kOutput, calls=%fused_computation | convolution fusion | flops 2148532224 | bytes 7340032 | tf_op jit(solution)/shard_map/gate/dot_general | solution.py:55
  42.5 1.0 collective-permute-start.5
  43.5 1.2 %collective-permute-done.5.got = bf16[128,1024]{1,0:T(8,128)(2,1)S(1)} collective-permute-done((bf16[128,1024]{1,0:T(8,128)(2,1)S(1)}, bf16[128,1024]{1,0:T(8,128)(2,1)S(1)}, u32[]{:S(2)}, u32[]{:S(2)}) %collective-permute-start.5) | collective-permute-done | bytes 262176 | tf_op jit(solution)/shard_map/enter/ppermute | solution.py:474
  44.7 5.3 %out.1 = (bf16[512,1024]{1,0:T(8,128)(2,1)}, bf16[8,4,1024]{2,1,0:T(4,128)(2,1)S(1)}) custom-call(bf16[512,2048]{1,0:T(8,128)(2,1)S(1)} %copy-done.1, bf16[512,256]{1,0:T(8,128)(2,1)S(1)} %copy-done.7, bf16[128,1024]{1,0:T(8,128)(2,1)S(1)} %get-tuple-element.36.kept, bf16[128,1024]{1,0:T(8,128)(2,1)S(1)} %collective-permute-done.5.got, ...), custom_call_target="tpu_custom_call" | custom-call | flops 2684354560 | tf_op jit(solution)/shard_map/out/pallas_call | solution.py:477
  50.0 8.7 %all_to_all.15.got = bf16[8,4,1024]{2,1,0:T(4,128)(2,1)S(1)} all-to-all(bf16[8,4,1024]{2,1,0:T(4,128)(2,1)S(1)} %get-tuple-element.41), channel_id=1, replica_groups=mesh['x'=4,'core'=2,'cand'=16] {'x','core'}, dimensions={0} | all-to-all | bytes 131072 | tf_op jit(solution)/shard_map/rows/all_to_all | solution.py:493
  58.7 0.6 rows.1
  59.3 22.4 %all_to_all.16 = bf16[128,2,1152]{2,1,0:T(2,128)(2,1)S(1)} all-to-all(bf16[128,2,1152]{2,1,0:T(2,128)(2,1)S(1)} %rows.1), channel_id=1, replica_groups=mesh['x'=4,'core'=2,'cand'=16] {'core','x','cand'}, dimensions={0} | all-to-all | bytes 1179648 | tf_op jit(solution)/shard_map/rows/all_to_all | solution.py:495
  82.0 0.9 collective-permute-start.6
  83.6 1.0 collective-permute-done.6.got
  84.6 3.4 %copy-done.12 = bf16[4096,1024]{1,0:T(8,128)(2,1)S(1)} copy-done((bf16[4096,1024]{1,0:T(8,128)(2,1)S(1)}, bf16[4096,1024]{1,0:T(8,128)(2,1)}, u32[]{:S(2)}) %copy-start.12) | copy-done | bytes 8388632
  87.9 6.8 %logits.1 = f32[256,16]{1,0:T(8,128)S(1)} custom-call(s32[1]{0:T(128)S(6)} %copy.23.block_id, f32[16]{0:T(128)S(1)} %copy-done.13, bf16[256,1152]{1,0:T(8,128)(2,1)S(1)} %reshape.18.own, bf16[256,1152]{1,0:T(8,128)(2,1)S(1)} %collective-permute-done.6.got, bf16[4096,1024]{1,0:T(8,128)(2,1)S(1)} %copy-done.12), custom_call_target="tpu_custom_call" | custom-call | flops 4294967296 | tf_op jit(solution)/shard_map/logits/pallas_call | solution.py:499
  94.7 14.2 %all_to_all.17.seen = f32[128,2,16]{2,1,0:T(2,128)S(1)} all-to-all(f32[128,2,16]{2,1,0:T(2,128)S(1)} %bitcast.18), channel_id=1, replica_groups=mesh['x'=4,'core'=2,'cand'=16] {'core','x','cand'}, dimensions={0} | all-to-all | bytes 32768 | tf_op jit(solution)/shard_map/loss/all_to_all | solution.py:510
  108.9 1.1 loss.1
  (38 shorter events, 0.8 us)
Async XLA Ops:
  1.4 5.5 %collective-permute-start = (bf16[16,1024]{1,0:T(8,128)(2,1)S(1)}, bf16[16,1024]{1,0:T(8,128)(2,1)S(1)}, u32[]{:S(2)}, u32[]{:S(2)}) collective-permute-start(bf16[16,1024]{1,0:T(8,128)(2,1)S(1)} %slice_bitcast_fusion), channel_id=1, source_target_pairs={{0,16},{16,32},{32,48},{48,64},{64,80},{80,96},{96,112},{1,17},{17... | collective-permute-start | bytes 98312 | tf_op jit(solution)/shard_map/halo/ppermute | solution.py:413
  6.9 0.6 copy-start.15
  18.2 1.9 %collective-permute-start.1 = (bf16[144,1024]{1,0:T(8,128)(2,1)}, bf16[144,1024]{1,0:T(8,128)(2,1)S(1)}, u32[]{:S(2)}, u32[]{:S(2)}) collective-permute-start(bf16[144,1024]{1,0:T(8,128)(2,1)} %get-tuple-element.24), channel_id=1, source_target_pairs={{0,16},{16,0},{1,17},{17,1},{2,18},{18,2},{3,19},{19,3},{4,20},{20... | collective-permute-start | bytes 884744 | tf_op jit(solution)/shard_map/chip/ppermute | solution.py:447
  20.1 1.0 copy-start.2
  21.2 18.5 %copy-start.14 = (bf16[1024,2048]{1,0:T(8,128)(2,1)S(1)}, bf16[1024,2048]{1,0:T(8,128)(2,1)}, u32[]{:S(2)}) copy-start(bf16[1024,2048]{1,0:T(8,128)(2,1)} %param.29) | copy-start | bytes 12582916
  21.2 18.5 %copy-start.16 = (bf16[512,1024]{1,0:T(8,128)(2,1)S(1)}, bf16[512,1024]{1,0:T(8,128)(2,1)}, u32[]{:S(2)}) copy-start(bf16[512,1024]{1,0:T(8,128)(2,1)} %get-tuple-element.32) | copy-start | bytes 3145732
  21.2 20.9 %collective-permute-start.2 = (bf16[144,1024]{1,0:T(8,128)(2,1)S(1)}, bf16[144,1024]{1,0:T(8,128)(2,1)S(1)}, u32[]{:S(2)}, u32[]{:S(2)}) collective-permute-start(bf16[144,1024]{1,0:T(8,128)(2,1)S(1)} %chip.1), channel_id=1, source_target_pairs={{0,32},{32,64},{64,96},{1,33},{33,65},{65,97},{2,34},{34,66},{66,9... | collective-permute-start | bytes 884744 | tf_op jit(solution)/shard_map/chip/ppermute | solution.py:450
  25.4 16.7 %collective-permute-start.3 = (bf16[144,1024]{1,0:T(8,128)(2,1)S(1)}, bf16[144,1024]{1,0:T(8,128)(2,1)S(1)}, u32[]{:S(2)}, u32[]{:S(2)}) collective-permute-start(bf16[144,1024]{1,0:T(8,128)(2,1)S(1)} %chip.1), channel_id=1, source_target_pairs={{0,64},{32,96},{1,65},{33,97},{2,66},{34,98},{3,67},{35,99},{4,68}... | collective-permute-start | bytes 884744 | tf_op jit(solution)/shard_map/chip/ppermute | solution.py:450
  29.8 12.4 %collective-permute-start.4 = (bf16[144,1024]{1,0:T(8,128)(2,1)S(1)}, bf16[144,1024]{1,0:T(8,128)(2,1)S(1)}, u32[]{:S(2)}, u32[]{:S(2)}) collective-permute-start(bf16[144,1024]{1,0:T(8,128)(2,1)S(1)} %chip.1), channel_id=1, source_target_pairs={{0,96},{1,97},{2,98},{3,99},{4,100},{5,101},{6,102},{7,103},{8,104... | collective-permute-start | bytes 884744 | tf_op jit(solution)/shard_map/chip/ppermute | solution.py:450
  39.7 2.5 %copy-start.3 = (bf16[144,1024]{1,0:T(8,128)(2,1)S(1)}, bf16[144,1024]{1,0:T(8,128)(2,1)}, u32[]{:S(2)}) copy-start(bf16[144,1024]{1,0:T(8,128)(2,1)} %get-tuple-element.23.keep) | copy-start | bytes 884740
  39.7 5.0 %copy-start = (bf16[2048,1024]{1,0:T(8,128)(2,1)S(1)}, bf16[2048,1024]{1,0:T(8,128)(2,1)}, u32[]{:S(2)}) copy-start(bf16[2048,1024]{1,0:T(8,128)(2,1)} %w_out.1) | copy-start | bytes 12582916
  39.7 4.9 %copy-start.1 = (bf16[512,2048]{1,0:T(8,128)(2,1)S(1)}, bf16[512,2048]{1,0:T(8,128)(2,1)}, u32[]{:S(2)}) copy-start(bf16[512,2048]{1,0:T(8,128)(2,1)} %scan.1.y) | copy-start | bytes 6291460
  39.7 4.9 %copy-start.4 = (bf16[1,512,1024]{2,1,0:T(8,128)(2,1)S(1)}, bf16[1,512,1024]{2,1,0:T(8,128)(2,1)}, u32[]{:S(2)}) copy-start(bf16[1,512,1024]{2,1,0:T(8,128)(2,1)} %param.20) | copy-start | bytes 3145732
  39.7 4.9 %copy-start.5 = (bf16[128,2048]{1,0:T(8,128)(2,1)S(1)}, bf16[128,2048]{1,0:T(8,128)(2,1)}, u32[]{:S(2)}) copy-start(bf16[128,2048]{1,0:T(8,128)(2,1)} %constant.2.clone.spread_h.spread) | copy-start | bytes 1572868
  39.7 4.9 %copy-start.6 = (bf16[2,512,128]{2,1,0:T(8,128)(2,1)S(1)}, bf16[2,512,128]{2,1,0:T(8,128)(2,1)}, u32[]{:S(2)}) copy-start(bf16[2,512,128]{2,1,0:T(8,128)(2,1)} %get-tuple-element.38.shard) | copy-start | bytes 786436
  39.8 4.9 %copy-start.7 = (bf16[512,256]{1,0:T(8,128)(2,1)S(1)}, bf16[512,256]{1,0:T(8,128)(2,1)}, u32[]{:S(2)}) copy-start(bf16[512,256]{1,0:T(8,128)(2,1)} %get-tuple-element.26.bc) | copy-start | bytes 786436
  39.8 4.9 %copy-start.8 = (f32[2048]{0:T(1024)S(1)}, f32[2048]{0:T(1024)}, u32[]{:S(2)}) copy-start(f32[2048]{0:T(1024)} %param.36) | copy-start | bytes 24580
  39.8 4.9 %copy-start.9 = (f32[1024]{0:T(1024)S(1)}, f32[1024]{0:T(1024)}, u32[]{:S(2)}) copy-start(f32[1024]{0:T(1024)} %param.38) | copy-start | bytes 12292
  39.8 4.9 %copy-start.10 = (s32[1,32]{1,0:T(1,128)S(1)}, s32[1,32]{1,0:T(1,128)}, u32[]{:S(2)}) copy-start(s32[1,32]{1,0:T(1,128)} %wanted.1) | copy-start | bytes 388
  42.5 2.2 %collective-permute-start.5 = (bf16[128,1024]{1,0:T(8,128)(2,1)S(1)}, bf16[128,1024]{1,0:T(8,128)(2,1)S(1)}, u32[]{:S(2)}, u32[]{:S(2)}) collective-permute-start(bf16[128,1024]{1,0:T(8,128)(2,1)S(1)} %get-tuple-element.37), channel_id=1, source_target_pairs={{0,16},{16,0},{1,17},{17,1},{2,18},{18,2},{3,19},{19,3},{4,20},{20... | collective-permute-start | bytes 786440 | tf_op jit(solution)/shard_map/enter/ppermute | solution.py:474
  44.7 14.0 %copy-start.11 = (s32[1,4]{1,0:T(1,128)S(1)}, s32[1,4]{1,0:T(1,128)}, u32[]{:S(2)}) copy-start(s32[1,4]{1,0:T(1,128)} %ids.1) | copy-start | bytes 52
  44.7 39.8 %copy-start.13 = (f32[16]{0:T(128)S(1)}, f32[16]{0:T(128)}, u32[]{:S(2)}) copy-start(f32[16]{0:T(128)} %temper.1) | copy-start | bytes 196
  82.0 2.6 %collective-permute-start.6 = (bf16[256,1152]{1,0:T(8,128)(2,1)S(1)}, bf16[256,1152]{1,0:T(8,128)(2,1)S(1)}, u32[]{:S(2)}, u32[]{:S(2)}) collective-permute-start(bf16[256,1152]{1,0:T(8,128)(2,1)S(1)} %reshape.18.own), channel_id=1, source_target_pairs={{0,16},{16,0},{1,17},{17,1},{2,18},{18,2},{3,19},{19,3},{4,20},{20... | collective-permute-start | bytes 1769480 | tf_op jit(solution)/shard_map/rows/ppermute | solution.py:496
  84.5 3.4 %copy-start.12 = (bf16[4096,1024]{1,0:T(8,128)(2,1)S(1)}, bf16[4096,1024]{1,0:T(8,128)(2,1)}, u32[]{:S(2)}) copy-start(bf16[4096,1024]{1,0:T(8,128)(2,1)} %items.1) | copy-start | bytes 25165828

commit v5 on v4

--- a/solution.py
+++ b/solution.py
@@ -199,6 +199,11 @@
     out[128:] = (first[128:].astype(F32) * second[128:].astype(F32)).astype(BF)
 
 
+def hold_kernel(keep, held):
+    for part in blocks(keep.shape[0], 16):
+        held[part] = keep[part]
+
+
 def chip_kernel(keep, got, chip):
     @pl.when(lax.axis_index("core") == 0)
     def _():
@@ -445,7 +450,8 @@
     entry = shape(128, inner // 2)
     with jax.named_scope("chip"):
         got = lax.ppermute(send, "core", swap)
-        chip = call(chip_kernel, payload, [VMEM] * 2)(keep, got)
+        held = call(hold_kernel, payload, [VMEM])(keep)
+        chip = call(chip_kernel, payload, [VMEM] * 2)(held, got)
         before = [
             lax.ppermute(chip, "x", [(i, i + n) for i in range(4 - n)]) for n in (1, 2, 3)
         ]
@@ -493,7 +499,9 @@
         mine = lax.all_to_all(picked, SEQ, 0, 0, tiled=True)
         sent = call(rows_kernel, shape(128, 2, width + 128), [SMEM, VMEM])(target_ids, mine)
         own_rows = lax.all_to_all(sent, EACH, 0, 0, tiled=True).reshape(256, width + 128)
+        own_rows, source = lax.optimization_barrier((own_rows, items))
         got_rows = lax.ppermute(own_rows, "core", swap)
+        items_v = call(hold_kernel, shape(*items.shape), [VMEM])(source)
 
     with jax.named_scope("logits"):
         stats = call(
@@ -504,7 +512,7 @@
                 pltpu.VMEM((512, width), BF), pltpu.VMEM((1, 512), jnp.int32), pltpu.VMEM((1, 512), F32),
             ],
             2 * 512 * items.shape[0] * width,
-        )(item_block, temper, own_rows, got_rows, items)
+        )(item_block, temper, own_rows, got_rows, items_v)
 
     with jax.named_scope("loss"):
         seen = lax.all_to_all(stats.reshape(128, 2, 16), EACH, 0, 0, tiled=True)

time: 110 us -> 109 us (level)
  waiting for transfers between devices: 4.28 us -> 2.32 us
  transfers between devices with their start and end apart: 7 -> 7, of which waited for: 4 -> 3; matrix products, arithmetic and copies ran while one was open for 2% -> 2% of each run, Pallas kernels for 8% -> 8%
where the time goes in v5:
time: 109 us; the launch traced here: 108 us
  blocking collectives  45.6 us (42%)
  Pallas kernels  33.8 us (31%)
  starting transfers between devices  16 us (15%)
  local copies, waits for them, and re-layouts  6.11 us (6%)
  matrix products  2.34 us (2%)
  waiting for transfers between devices  2.32 us (2%)
  between operations  2.22 us (2%)
    all_to_all x1, blocking collectives, local(): lax.all_to_all(sent, EACH, 0, 0, tiled=True).reshape(256, width + 128)  22.4 us
    all_to_all x1, blocking collectives, local(): seen = lax.all_to_all(stats.reshape(128, 2, 16), EACH, 0, 0, tiled=True)  13.9 us
    pallas_call x1, Pallas kernels, local(): call(mix_kernel, [shape(rows, width), shape(rows, 128), shape(8, 4, rows,...  10.7 us
    ppermute x3, starting transfers between devices, local(): lax.ppermute(chip, 'x', [(i, i + n) for i in range(4 - n)])  9.48 us
    all_to_all x1, blocking collectives, local(): mine = lax.all_to_all(picked, SEQ, 0, 0, tiled=True)  9.29 us
    pallas_call x1, Pallas kernels, local(): call(scan_kernel, shape(rows, inner), [VMEM] * 6, [pltpu.VMEM((chunks, GR...  8.38 us
    pallas_call x1, Pallas kernels, local(): call(logit_kernel, shape(256, 16, dtype=F32), [SMEM, SMEM, VMEM, VMEM, VM...  6.77 us
    pallas_call x1, Pallas kernels, local(): call(out_kernel, [shape(rows, width), shape(8, 4, width)], [VMEM] * 12, [...  5.29 us
  transfers between devices with their start and end apart: 7, of which 3 were waited for; matrix products, arithmetic and copies ran while one was open for 2% of the time, Pallas kernels for 8%

profile of v5, /device:TPU:1, one launch (start us, length us, event | category | flops | bytes accessed | tf_op | source)
XLA Modules:
  0.0 108.4 jit_solution(17466368186973843654)
XLA Ops:
  0.6 0.8 slice_bitcast_fusion
  1.4 4.5 %collective-permute-start = (bf16[16,1024]{1,0:T(8,128)(2,1)S(1)}, bf16[16,1024]{1,0:T(8,128)(2,1)S(1)}, u32[]{:S(2)}, u32[]{:S(2)}) collective-permute-start(bf16[16,1024]{1,0:T(8,128)(2,1)S(1)} %slice_bitcast_fusion), channel_id=1, source_target_pairs={{0,16},{16,32},{32,48},{48,64},{64,80},{80,96},{96,112},{1,17},{17... | collective-permute-start | bytes 98312 | tf_op jit(solution)/shard_map/halo/ppermute | solution.py:418
  6.5 0.4 collective-permute-done.halo_h
  6.9 0.6 copy-done.15
  7.5 10.7 %mix.1 = (bf16[512,1024]{1,0:T(8,128)(2,1)}, bf16[512,128]{1,0:T(8,128)(2,1)}, f32[8,4,512]{2,1,0:T(4,128)}, bf16[2,512,128]{2,1,0:T(8,128)(2,1)}, bf16[3,512,12...) custom-call(s32[1]{0:T(128)S(6)} %copy.22.length, ...), custom_call_target="tpu_custom_call" | custom-call | flops 2415919104 | tf_op jit(solution)/shard_map/mix/pallas_call | solution.py:421
  18.3 1.0 copy-done.3
  19.3 0.8 collective-permute-done.1.got
  20.2 5.5 %collective-permute-start.4 = (bf16[144,1024]{1,0:T(8,128)(2,1)S(1)}, bf16[144,1024]{1,0:T(8,128)(2,1)S(1)}, u32[]{:S(2)}, u32[]{:S(2)}) collective-permute-start(bf16[144,1024]{1,0:T(8,128)(2,1)S(1)} %chip.3), channel_id=1, source_target_pairs={{0,96},{1,97},{2,98},{3,99},{4,100},{5,101},{6,102},{7,103},{8,104... | collective-permute-start | bytes 884744 | tf_op jit(solution)/shard_map/chip/ppermute | solution.py:456
  25.8 1.3 %collective-permute-start.3 = (bf16[144,1024]{1,0:T(8,128)(2,1)S(1)}, bf16[144,1024]{1,0:T(8,128)(2,1)S(1)}, u32[]{:S(2)}, u32[]{:S(2)}) collective-permute-start(bf16[144,1024]{1,0:T(8,128)(2,1)S(1)} %chip.3), channel_id=1, source_target_pairs={{0,64},{32,96},{1,65},{33,97},{2,66},{34,98},{3,67},{35,99},{4,68}... | collective-permute-start | bytes 884744 | tf_op jit(solution)/shard_map/chip/ppermute | solution.py:456
  27.1 2.7 %collective-permute-start.2 = (bf16[144,1024]{1,0:T(8,128)(2,1)S(1)}, bf16[144,1024]{1,0:T(8,128)(2,1)S(1)}, u32[]{:S(2)}, u32[]{:S(2)}) collective-permute-start(bf16[144,1024]{1,0:T(8,128)(2,1)S(1)} %chip.3), channel_id=1, source_target_pairs={{0,32},{32,64},{64,96},{1,33},{33,65},{65,97},{2,34},{34,66},{66,9... | collective-permute-start | bytes 884744 | tf_op jit(solution)/shard_map/chip/ppermute | solution.py:456
  29.7 8.4 %scan.1.y = bf16[512,2048]{1,0:T(8,128)(2,1)} custom-call(bf16[512,2048]{1,0:T(8,128)(2,1)} %get-tuple-element.27.x, bf16[512,256]{1,0:T(8,128)(2,1)} %get-tuple-element.28.bc, bf16[512,128]{1,0:T(8,128)(2,1)} %get-tuple-element.29.cum, f32[8,4,512]{2,1,0:T(4,128)} %get-tuple-element.30.cum_t, bf16[3,512,128]{2,1,0:T(8,128)(2,1)} %get-tuple-element.31.chunk, ...), custom_call_target="tpu_custom_call" | custom-call | flops 2147483648 | tf_op jit(solution)/shard_map/scan/pallas_call | solution.py:460
  38.2 2.3 %convolution_convert_fusion.z = bf16[512,2048]{1,0:T(8,128)(2,1)S(1)} fusion(bf16[512,1024]{1,0:T(8,128)(2,1)S(1)} %copy-done.16, bf16[1024,2048]{1,0:T(8,128)(2,1)S(1)} %copy-done.14), kind=kOutput, calls=%fused_computation | convolution fusion | flops 2148532224 | bytes 7340032 | tf_op jit(solution)/shard_map/gate/dot_general | solution.py:55
  40.9 1.0 collective-permute-start.5
  41.9 1.2 %collective-permute-done.5.got = bf16[128,1024]{1,0:T(8,128)(2,1)S(1)} collective-permute-done((bf16[128,1024]{1,0:T(8,128)(2,1)S(1)}, bf16[128,1024]{1,0:T(8,128)(2,1)S(1)}, u32[]{:S(2)}, u32[]{:S(2)}) %collective-permute-start.5) | collective-permute-done | bytes 262176 | tf_op jit(solution)/shard_map/enter/ppermute | solution.py:480
  43.2 5.3 %out.1 = (bf16[512,1024]{1,0:T(8,128)(2,1)}, bf16[8,4,1024]{2,1,0:T(4,128)(2,1)S(1)}) custom-call(bf16[512,2048]{1,0:T(8,128)(2,1)S(1)} %copy-done.2, bf16[512,256]{1,0:T(8,128)(2,1)S(1)} %copy-done.8, bf16[128,1024]{1,0:T(8,128)(2,1)S(1)} %get-tuple-element.38.kept, bf16[128,1024]{1,0:T(8,128)(2,1)S(1)} %collective-permute-done.5.got, ...), custom_call_target="tpu_custom_call" | custom-call | flops 2684354560 | tf_op jit(solution)/shard_map/out/pallas_call | solution.py:483
  48.4 9.3 %all_to_all.15.got = bf16[8,4,1024]{2,1,0:T(4,128)(2,1)S(1)} all-to-all(bf16[8,4,1024]{2,1,0:T(4,128)(2,1)S(1)} %get-tuple-element.43), channel_id=1, replica_groups=mesh['x'=4,'core'=2,'cand'=16] {'x','core'}, dimensions={0} | all-to-all | bytes 131072 | tf_op jit(solution)/shard_map/rows/all_to_all | solution.py:499
  57.7 0.6 rows.2
  58.4 22.4 %all_to_all.16 = bf16[128,2,1152]{2,1,0:T(2,128)(2,1)S(1)} all-to-all(bf16[128,2,1152]{2,1,0:T(2,128)(2,1)S(1)} %rows.2), channel_id=1, replica_groups=mesh['x'=4,'core'=2,'cand'=16] {'core','x','cand'}, dimensions={0} | all-to-all | bytes 1179648 | tf_op jit(solution)/shard_map/rows/all_to_all | solution.py:501
  81.0 0.9 collective-permute-start.6
  82.6 3.4 %copy-done = bf16[4096,1024]{1,0:T(8,128)(2,1)S(1)} copy-done((bf16[4096,1024]{1,0:T(8,128)(2,1)S(1)}, bf16[4096,1024]{1,0:T(8,128)(2,1)}, u32[]{:S(2)}) %copy-start) | copy-done | bytes 8388632
  86.0 0.5 rows.3.items
  86.6 6.8 %logits.1 = f32[256,16]{1,0:T(8,128)S(1)} custom-call(s32[1]{0:T(128)S(6)} %copy.23.block_id, f32[16]{0:T(128)S(1)} %copy-done.13, bf16[256,1152]{1,0:T(8,128)(2,1)S(1)} %reshape.18.own, bf16[256,1152]{1,0:T(8,128)(2,1)S(1)} %collective-permute-done.6.got, bf16[4096,1024]{1,0:T(8,128)(2,1)S(1)} %rows.3.items), custom_call_target="tpu_custom_call" | custom-call | flops 4294967296 | tf_op jit(solution)/shard_map/logits/pallas_call | solution.py:507
  93.4 13.9 %all_to_all.17.seen = f32[128,2,16]{2,1,0:T(2,128)S(1)} all-to-all(f32[128,2,16]{2,1,0:T(2,128)S(1)} %bitcast.18), channel_id=1, replica_groups=mesh['x'=4,'core'=2,'cand'=16] {'core','x','cand'}, dimensions={0} | all-to-all | bytes 32768 | tf_op jit(solution)/shard_map/loss/all_to_all | solution.py:518
  107.3 1.1 loss.1
  (40 shorter events, 0.9 us)
Async XLA Ops:
  1.4 5.5 %collective-permute-start = (bf16[16,1024]{1,0:T(8,128)(2,1)S(1)}, bf16[16,1024]{1,0:T(8,128)(2,1)S(1)}, u32[]{:S(2)}, u32[]{:S(2)}) collective-permute-start(bf16[16,1024]{1,0:T(8,128)(2,1)S(1)} %slice_bitcast_fusion), channel_id=1, source_target_pairs={{0,16},{16,32},{32,48},{48,64},{64,80},{80,96},{96,112},{1,17},{17... | collective-permute-start | bytes 98312 | tf_op jit(solution)/shard_map/halo/ppermute | solution.py:418
  6.9 0.6 copy-start.15
  18.2 1.9 %collective-permute-start.1 = (bf16[144,1024]{1,0:T(8,128)(2,1)}, bf16[144,1024]{1,0:T(8,128)(2,1)S(1)}, u32[]{:S(2)}, u32[]{:S(2)}) collective-permute-start(bf16[144,1024]{1,0:T(8,128)(2,1)} %get-tuple-element.26), channel_id=1, source_target_pairs={{0,16},{16,0},{1,17},{17,1},{2,18},{18,2},{3,19},{19,3},{4,20},{20... | collective-permute-start | bytes 884744 | tf_op jit(solution)/shard_map/chip/ppermute | solution.py:452
  18.3 1.0 copy-start.3
  20.2 17.9 %copy-start.14 = (bf16[1024,2048]{1,0:T(8,128)(2,1)S(1)}, bf16[1024,2048]{1,0:T(8,128)(2,1)}, u32[]{:S(2)}) copy-start(bf16[1024,2048]{1,0:T(8,128)(2,1)} %param.29) | copy-start | bytes 12582916
  20.2 17.9 %copy-start.16 = (bf16[512,1024]{1,0:T(8,128)(2,1)S(1)}, bf16[512,1024]{1,0:T(8,128)(2,1)}, u32[]{:S(2)}) copy-start(bf16[512,1024]{1,0:T(8,128)(2,1)} %get-tuple-element.34) | copy-start | bytes 3145732
  20.2 20.3 %collective-permute-start.4 = (bf16[144,1024]{1,0:T(8,128)(2,1)S(1)}, bf16[144,1024]{1,0:T(8,128)(2,1)S(1)}, u32[]{:S(2)}, u32[]{:S(2)}) collective-permute-start(bf16[144,1024]{1,0:T(8,128)(2,1)S(1)} %chip.3), channel_id=1, source_target_pairs={{0,96},{1,97},{2,98},{3,99},{4,100},{5,101},{6,102},{7,103},{8,104... | collective-permute-start | bytes 884744 | tf_op jit(solution)/shard_map/chip/ppermute | solution.py:456
  25.8 14.8 %collective-permute-start.3 = (bf16[144,1024]{1,0:T(8,128)(2,1)S(1)}, bf16[144,1024]{1,0:T(8,128)(2,1)S(1)}, u32[]{:S(2)}, u32[]{:S(2)}) collective-permute-start(bf16[144,1024]{1,0:T(8,128)(2,1)S(1)} %chip.3), channel_id=1, source_target_pairs={{0,64},{32,96},{1,65},{33,97},{2,66},{34,98},{3,67},{35,99},{4,68}... | collective-permute-start | bytes 884744 | tf_op jit(solution)/shard_map/chip/ppermute | solution.py:456
  27.1 13.5 %collective-permute-start.2 = (bf16[144,1024]{1,0:T(8,128)(2,1)S(1)}, bf16[144,1024]{1,0:T(8,128)(2,1)S(1)}, u32[]{:S(2)}, u32[]{:S(2)}) collective-permute-start(bf16[144,1024]{1,0:T(8,128)(2,1)S(1)} %chip.3), channel_id=1, source_target_pairs={{0,32},{32,64},{64,96},{1,33},{33,65},{65,97},{2,34},{34,66},{66,9... | collective-permute-start | bytes 884744 | tf_op jit(solution)/shard_map/chip/ppermute | solution.py:456
  38.1 2.5 %copy-start.4 = (bf16[144,1024]{1,0:T(8,128)(2,1)S(1)}, bf16[144,1024]{1,0:T(8,128)(2,1)}, u32[]{:S(2)}) copy-start(bf16[144,1024]{1,0:T(8,128)(2,1)} %get-tuple-element.25.keep) | copy-start | bytes 884740
  38.1 5.0 %copy-start.1 = (bf16[2048,1024]{1,0:T(8,128)(2,1)S(1)}, bf16[2048,1024]{1,0:T(8,128)(2,1)}, u32[]{:S(2)}) copy-start(bf16[2048,1024]{1,0:T(8,128)(2,1)} %w_out.1) | copy-start | bytes 12582916
  38.1 4.9 %copy-start.2 = (bf16[512,2048]{1,0:T(8,128)(2,1)S(1)}, bf16[512,2048]{1,0:T(8,128)(2,1)}, u32[]{:S(2)}) copy-start(bf16[512,2048]{1,0:T(8,128)(2,1)} %scan.1.y) | copy-start | bytes 6291460
  38.1 4.9 %copy-start.5 = (bf16[1,512,1024]{2,1,0:T(8,128)(2,1)S(1)}, bf16[1,512,1024]{2,1,0:T(8,128)(2,1)}, u32[]{:S(2)}) copy-start(bf16[1,512,1024]{2,1,0:T(8,128)(2,1)} %param.20) | copy-start | bytes 3145732
  38.2 4.9 %copy-start.6 = (bf16[128,2048]{1,0:T(8,128)(2,1)S(1)}, bf16[128,2048]{1,0:T(8,128)(2,1)}, u32[]{:S(2)}) copy-start(bf16[128,2048]{1,0:T(8,128)(2,1)} %constant.2.clone.spread_h.spread) | copy-start | bytes 1572868
  38.2 4.9 %copy-start.7 = (bf16[2,512,128]{2,1,0:T(8,128)(2,1)S(1)}, bf16[2,512,128]{2,1,0:T(8,128)(2,1)}, u32[]{:S(2)}) copy-start(bf16[2,512,128]{2,1,0:T(8,128)(2,1)} %get-tuple-element.40.shard) | copy-start | bytes 786436
  38.2 4.9 %copy-start.8 = (bf16[512,256]{1,0:T(8,128)(2,1)S(1)}, bf16[512,256]{1,0:T(8,128)(2,1)}, u32[]{:S(2)}) copy-start(bf16[512,256]{1,0:T(8,128)(2,1)} %get-tuple-element.28.bc) | copy-start | bytes 786436
  38.2 4.9 %copy-start.9 = (f32[2048]{0:T(1024)S(1)}, f32[2048]{0:T(1024)}, u32[]{:S(2)}) copy-start(f32[2048]{0:T(1024)} %param.36) | copy-start | bytes 24580
  38.2 4.9 %copy-start.10 = (f32[1024]{0:T(1024)S(1)}, f32[1024]{0:T(1024)}, u32[]{:S(2)}) copy-start(f32[1024]{0:T(1024)} %param.38) | copy-start | bytes 12292
  38.2 4.9 %copy-start.11 = (s32[1,32]{1,0:T(1,128)S(1)}, s32[1,32]{1,0:T(1,128)}, u32[]{:S(2)}) copy-start(s32[1,32]{1,0:T(1,128)} %wanted.1) | copy-start | bytes 388
  40.9 2.2 %collective-permute-start.5 = (bf16[128,1024]{1,0:T(8,128)(2,1)S(1)}, bf16[128,1024]{1,0:T(8,128)(2,1)S(1)}, u32[]{:S(2)}, u32[]{:S(2)}) collective-permute-start(bf16[128,1024]{1,0:T(8,128)(2,1)S(1)} %get-tuple-element.39), channel_id=1, source_target_pairs={{0,16},{16,0},{1,17},{17,1},{2,18},{18,2},{3,19},{19,3},{4,20},{20... | collective-permute-start | bytes 786440 | tf_op jit(solution)/shard_map/enter/ppermute | solution.py:480
  43.1 14.6 %copy-start.12 = (s32[1,4]{1,0:T(1,128)S(1)}, s32[1,4]{1,0:T(1,128)}, u32[]{:S(2)}) copy-start(s32[1,4]{1,0:T(1,128)} %ids.1) | copy-start | bytes 52
  81.0 5.5 %collective-permute-start.6 = (bf16[256,1152]{1,0:T(8,128)(2,1)S(1)}, bf16[256,1152]{1,0:T(8,128)(2,1)S(1)}, u32[]{:S(2)}, u32[]{:S(2)}) collective-permute-start(bf16[256,1152]{1,0:T(8,128)(2,1)S(1)} %reshape.18.own), channel_id=1, source_target_pairs={{0,16},{16,0},{1,17},{17,1},{2,18},{18,2},{3,19},{19,3},{4,20},{20... | collective-permute-start | bytes 1769480 | tf_op jit(solution)/shard_map/rows/ppermute | solution.py:503
  82.6 3.4 %copy-start = (bf16[4096,1024]{1,0:T(8,128)(2,1)S(1)}, bf16[4096,1024]{1,0:T(8,128)(2,1)}, u32[]{:S(2)}) copy-start(bf16[4096,1024]{1,0:T(8,128)(2,1)} %keep) | copy-start | bytes 25165828
  86.0 0.7 copy-start.13

commit v6 on v5

--- a/solution.py
+++ b/solution.py
@@ -317,7 +317,7 @@
             ahead = spread_state(n + 1)
         for part in blocks(rows, PART):
             v = y[part, cols].astype(F32) + state[part] * decay[part]
-            v = v * silu(z[part, cols].astype(F32))
+            v = v * z[part, cols].astype(F32)
             sq = v * v
             sq = sq[:, :128] + sq[:, 128:]
             square[part] = square[part] + sq if n else sq
@@ -473,7 +473,7 @@
         )(x, bc, cum, cum_t, chunk, d_skip[None])
         y, source = lax.optimization_barrier((y, normed))
     with jax.named_scope("gate"):
-        z = dot(source, w_z).astype(BF)
+        z = silu(dot(source, w_z).astype(BF).astype(F32)).astype(BF)
         before, z = lax.optimization_barrier((before, z))
     with jax.named_scope("enter"):
         here, away = call(enter_kernel, [entry, entry], [VMEM] * 5)(keep, got, *before)

time: 109 us -> 108 us (level)
  no operation moved by 1% of the time
where the time goes in v6:
time: 108 us
  blocking collectives  45.4 us (42%)
  Pallas kernels  33.3 us (31%)
  starting transfers between devices  16 us (15%)
  local copies, waits for them, and re-layouts  6.11 us (6%)
  matrix products  2.56 us (2%)
  waiting for transfers between devices  2.32 us (2%)
  between operations  2.22 us (2%)
    all_to_all x1, blocking collectives, local(): lax.all_to_all(sent, EACH, 0, 0, tiled=True).reshape(256, width + 128)  22.4 us
    all_to_all x1, blocking collectives, local(): seen = lax.all_to_all(stats.reshape(128, 2, 16), EACH, 0, 0, tiled=True)  13.9 us
    pallas_call x1, Pallas kernels, local(): call(mix_kernel, [shape(rows, width), shape(rows, 128), shape(8, 4, rows,...  10.7 us
    ppermute x3, starting transfers between devices, local(): lax.ppermute(chip, 'x', [(i, i + n) for i in range(4 - n)])  9.48 us
    all_to_all x1, blocking collectives, local(): mine = lax.all_to_all(picked, SEQ, 0, 0, tiled=True)  9.07 us
    pallas_call x1, Pallas kernels, local(): call(scan_kernel, shape(rows, inner), [VMEM] * 6, [pltpu.VMEM((chunks, GR...  8.38 us
    pallas_call x1, Pallas kernels, local(): call(logit_kernel, shape(256, 16, dtype=F32), [SMEM, SMEM, VMEM, VMEM, VM...  6.77 us
    unnamed x34, local copies, waits for them, and re-layouts  5.13 us
  transfers between devices with their start and end apart: 7, of which 3 were waited for; matrix products, arithmetic and copies ran while one was open for 2% of the time, Pallas kernels for 8%

profile of v6, /device:TPU:1, one launch (start us, length us, event | category | flops | bytes accessed | tf_op | source)
XLA Modules:
  0.0 108.0 jit_solution(5910433175050405229)
XLA Ops:
  0.6 0.8 slice_bitcast_fusion
  1.4 4.5 %collective-permute-start = (bf16[16,1024]{1,0:T(8,128)(2,1)S(1)}, bf16[16,1024]{1,0:T(8,128)(2,1)S(1)}, u32[]{:S(2)}, u32[]{:S(2)}) collective-permute-start(bf16[16,1024]{1,0:T(8,128)(2,1)S(1)} %slice_bitcast_fusion), channel_id=1, source_target_pairs={{0,16},{16,32},{32,48},{48,64},{64,80},{80,96},{96,112},{1,17},{17... | collective-permute-start | bytes 98312 | tf_op jit(solution)/shard_map/halo/ppermute | solution.py:418
  6.5 0.4 collective-permute-done.halo_h
  6.9 0.6 copy-done.15
  7.5 10.7 %mix.1 = (bf16[512,1024]{1,0:T(8,128)(2,1)}, bf16[512,128]{1,0:T(8,128)(2,1)}, f32[8,4,512]{2,1,0:T(4,128)}, bf16[2,512,128]{2,1,0:T(8,128)(2,1)}, bf16[3,512,12...) custom-call(s32[1]{0:T(128)S(6)} %copy.22.length, ...), custom_call_target="tpu_custom_call" | custom-call | flops 2415919104 | tf_op jit(solution)/shard_map/mix/pallas_call | solution.py:421
  18.3 1.0 copy-done.3
  19.3 0.8 collective-permute-done.1.got
  20.2 5.5 %collective-permute-start.4 = (bf16[144,1024]{1,0:T(8,128)(2,1)S(1)}, bf16[144,1024]{1,0:T(8,128)(2,1)S(1)}, u32[]{:S(2)}, u32[]{:S(2)}) collective-permute-start(bf16[144,1024]{1,0:T(8,128)(2,1)S(1)} %chip.3), channel_id=1, source_target_pairs={{0,96},{1,97},{2,98},{3,99},{4,100},{5,101},{6,102},{7,103},{8,104... | collective-permute-start | bytes 884744 | tf_op jit(solution)/shard_map/chip/ppermute | solution.py:456
  25.8 1.3 %collective-permute-start.3 = (bf16[144,1024]{1,0:T(8,128)(2,1)S(1)}, bf16[144,1024]{1,0:T(8,128)(2,1)S(1)}, u32[]{:S(2)}, u32[]{:S(2)}) collective-permute-start(bf16[144,1024]{1,0:T(8,128)(2,1)S(1)} %chip.3), channel_id=1, source_target_pairs={{0,64},{32,96},{1,65},{33,97},{2,66},{34,98},{3,67},{35,99},{4,68}... | collective-permute-start | bytes 884744 | tf_op jit(solution)/shard_map/chip/ppermute | solution.py:456
  27.1 2.7 %collective-permute-start.2 = (bf16[144,1024]{1,0:T(8,128)(2,1)S(1)}, bf16[144,1024]{1,0:T(8,128)(2,1)S(1)}, u32[]{:S(2)}, u32[]{:S(2)}) collective-permute-start(bf16[144,1024]{1,0:T(8,128)(2,1)S(1)} %chip.3), channel_id=1, source_target_pairs={{0,32},{32,64},{64,96},{1,33},{33,65},{65,97},{2,34},{34,66},{66,9... | collective-permute-start | bytes 884744 | tf_op jit(solution)/shard_map/chip/ppermute | solution.py:456
  29.7 8.4 %scan.1.y = bf16[512,2048]{1,0:T(8,128)(2,1)} custom-call(bf16[512,2048]{1,0:T(8,128)(2,1)} %get-tuple-element.27.x, bf16[512,256]{1,0:T(8,128)(2,1)} %get-tuple-element.28.bc, bf16[512,128]{1,0:T(8,128)(2,1)} %get-tuple-element.29.cum, f32[8,4,512]{2,1,0:T(4,128)} %get-tuple-element.30.cum_t, bf16[3,512,128]{2,1,0:T(8,128)(2,1)} %get-tuple-element.31.chunk, ...), custom_call_target="tpu_custom_call" | custom-call | flops 2147483648 | tf_op jit(solution)/shard_map/scan/pallas_call | solution.py:460
  38.2 2.6 %fusion.z = bf16[512,2048]{1,0:T(8,128)(2,1)S(1)} fusion(bf16[512,1024]{1,0:T(8,128)(2,1)S(1)} %copy-done.16, bf16[1024,2048]{1,0:T(8,128)(2,1)S(1)} %copy-done.14), kind=kOutput, calls=%fused_computation.1 | convolution fusion | flops 2153775104 | bytes 7340032 | tf_op jit(solution)/shard_map/gate/dot_general | solution.py:55
  41.1 1.0 collective-permute-start.5
  42.1 1.2 %collective-permute-done.5.got = bf16[128,1024]{1,0:T(8,128)(2,1)S(1)} collective-permute-done((bf16[128,1024]{1,0:T(8,128)(2,1)S(1)}, bf16[128,1024]{1,0:T(8,128)(2,1)S(1)}, u32[]{:S(2)}, u32[]{:S(2)}) %collective-permute-start.5) | collective-permute-done | bytes 262176 | tf_op jit(solution)/shard_map/enter/ppermute | solution.py:480
  43.4 4.8 %out.1 = (bf16[512,1024]{1,0:T(8,128)(2,1)}, bf16[8,4,1024]{2,1,0:T(4,128)(2,1)S(1)}) custom-call(bf16[512,2048]{1,0:T(8,128)(2,1)S(1)} %copy-done.2, bf16[512,256]{1,0:T(8,128)(2,1)S(1)} %copy-done.8, bf16[128,1024]{1,0:T(8,128)(2,1)S(1)} %get-tuple-element.38.kept, bf16[128,1024]{1,0:T(8,128)(2,1)S(1)} %collective-permute-done.5.got, ...), custom_call_target="tpu_custom_call" | custom-call | flops 2684354560 | tf_op jit(solution)/shard_map/out/pallas_call | solution.py:483
  48.2 9.1 %all_to_all.15.got = bf16[8,4,1024]{2,1,0:T(4,128)(2,1)S(1)} all-to-all(bf16[8,4,1024]{2,1,0:T(4,128)(2,1)S(1)} %get-tuple-element.43), channel_id=1, replica_groups=mesh['x'=4,'core'=2,'cand'=16] {'x','core'}, dimensions={0} | all-to-all | bytes 131072 | tf_op jit(solution)/shard_map/rows/all_to_all | solution.py:499
  57.3 0.6 rows.2
  57.9 22.4 %all_to_all.16 = bf16[128,2,1152]{2,1,0:T(2,128)(2,1)S(1)} all-to-all(bf16[128,2,1152]{2,1,0:T(2,128)(2,1)S(1)} %rows.2), channel_id=1, replica_groups=mesh['x'=4,'core'=2,'cand'=16] {'core','x','cand'}, dimensions={0} | all-to-all | bytes 1179648 | tf_op jit(solution)/shard_map/rows/all_to_all | solution.py:501
  80.6 0.9 collective-permute-start.6
  82.2 3.4 %copy-done = bf16[4096,1024]{1,0:T(8,128)(2,1)S(1)} copy-done((bf16[4096,1024]{1,0:T(8,128)(2,1)S(1)}, bf16[4096,1024]{1,0:T(8,128)(2,1)}, u32[]{:S(2)}) %copy-start) | copy-done | bytes 8388632
  85.6 0.5 rows.3.items
  86.2 6.8 %logits.1 = f32[256,16]{1,0:T(8,128)S(1)} custom-call(s32[1]{0:T(128)S(6)} %copy.23.block_id, f32[16]{0:T(128)S(1)} %copy-done.13, bf16[256,1152]{1,0:T(8,128)(2,1)S(1)} %reshape.18.own, bf16[256,1152]{1,0:T(8,128)(2,1)S(1)} %collective-permute-done.6.got, bf16[4096,1024]{1,0:T(8,128)(2,1)S(1)} %rows.3.items), custom_call_target="tpu_custom_call" | custom-call | flops 4294967296 | tf_op jit(solution)/shard_map/logits/pallas_call | solution.py:507
  93.0 13.9 %all_to_all.17.seen = f32[128,2,16]{2,1,0:T(2,128)S(1)} all-to-all(f32[128,2,16]{2,1,0:T(2,128)S(1)} %bitcast.18), channel_id=1, replica_groups=mesh['x'=4,'core'=2,'cand'=16] {'core','x','cand'}, dimensions={0} | all-to-all | bytes 32768 | tf_op jit(solution)/shard_map/loss/all_to_all | solution.py:518
  106.9 1.1 %loss.1 = f32[1,4]{1,0:T(1,128)} custom-call(f32[128,2,16]{2,1,0:T(2,128)S(1)} %all_to_all.17.seen), custom_call_target="tpu_custom_call" | custom-call | tf_op jit(solution)/shard_map/loss/pallas_call | solution.py:519
  (40 shorter events, 0.9 us)
Async XLA Ops:
  1.4 5.5 %collective-permute-start = (bf16[16,1024]{1,0:T(8,128)(2,1)S(1)}, bf16[16,1024]{1,0:T(8,128)(2,1)S(1)}, u32[]{:S(2)}, u32[]{:S(2)}) collective-permute-start(bf16[16,1024]{1,0:T(8,128)(2,1)S(1)} %slice_bitcast_fusion), channel_id=1, source_target_pairs={{0,16},{16,32},{32,48},{48,64},{64,80},{80,96},{96,112},{1,17},{17... | collective-permute-start | bytes 98312 | tf_op jit(solution)/shard_map/halo/ppermute | solution.py:418
  6.9 0.6 copy-start.15
  18.2 1.9 %collective-permute-start.1 = (bf16[144,1024]{1,0:T(8,128)(2,1)}, bf16[144,1024]{1,0:T(8,128)(2,1)S(1)}, u32[]{:S(2)}, u32[]{:S(2)}) collective-permute-start(bf16[144,1024]{1,0:T(8,128)(2,1)} %get-tuple-element.26), channel_id=1, source_target_pairs={{0,16},{16,0},{1,17},{17,1},{2,18},{18,2},{3,19},{19,3},{4,20},{20... | collective-permute-start | bytes 884744 | tf_op jit(solution)/shard_map/chip/ppermute | solution.py:452
  18.3 1.0 copy-start.3
  20.2 17.9 %copy-start.14 = (bf16[1024,2048]{1,0:T(8,128)(2,1)S(1)}, bf16[1024,2048]{1,0:T(8,128)(2,1)}, u32[]{:S(2)}) copy-start(bf16[1024,2048]{1,0:T(8,128)(2,1)} %param.29) | copy-start | bytes 12582916
  20.2 17.9 %copy-start.16 = (bf16[512,1024]{1,0:T(8,128)(2,1)S(1)}, bf16[512,1024]{1,0:T(8,128)(2,1)}, u32[]{:S(2)}) copy-start(bf16[512,1024]{1,0:T(8,128)(2,1)} %get-tuple-element.34) | copy-start | bytes 3145732
  20.2 20.6 %collective-permute-start.4 = (bf16[144,1024]{1,0:T(8,128)(2,1)S(1)}, bf16[144,1024]{1,0:T(8,128)(2,1)S(1)}, u32[]{:S(2)}, u32[]{:S(2)}) collective-permute-start(bf16[144,1024]{1,0:T(8,128)(2,1)S(1)} %chip.3), channel_id=1, source_target_pairs={{0,96},{1,97},{2,98},{3,99},{4,100},{5,101},{6,102},{7,103},{8,104... | collective-permute-start | bytes 884744 | tf_op jit(solution)/shard_map/chip/ppermute | solution.py:456
  25.8 15.1 %collective-permute-start.3 = (bf16[144,1024]{1,0:T(8,128)(2,1)S(1)}, bf16[144,1024]{1,0:T(8,128)(2,1)S(1)}, u32[]{:S(2)}, u32[]{:S(2)}) collective-permute-start(bf16[144,1024]{1,0:T(8,128)(2,1)S(1)} %chip.3), channel_id=1, source_target_pairs={{0,64},{32,96},{1,65},{33,97},{2,66},{34,98},{3,67},{35,99},{4,68}... | collective-permute-start | bytes 884744 | tf_op jit(solution)/shard_map/chip/ppermute | solution.py:456
  27.1 13.8 %collective-permute-start.2 = (bf16[144,1024]{1,0:T(8,128)(2,1)S(1)}, bf16[144,1024]{1,0:T(8,128)(2,1)S(1)}, u32[]{:S(2)}, u32[]{:S(2)}) collective-permute-start(bf16[144,1024]{1,0:T(8,128)(2,1)S(1)} %chip.3), channel_id=1, source_target_pairs={{0,32},{32,64},{64,96},{1,33},{33,65},{65,97},{2,34},{34,66},{66,9... | collective-permute-start | bytes 884744 | tf_op jit(solution)/shard_map/chip/ppermute | solution.py:456
  38.1 2.7 %copy-start.4 = (bf16[144,1024]{1,0:T(8,128)(2,1)S(1)}, bf16[144,1024]{1,0:T(8,128)(2,1)}, u32[]{:S(2)}) copy-start(bf16[144,1024]{1,0:T(8,128)(2,1)} %get-tuple-element.25.keep) | copy-start | bytes 884740
  38.1 5.2 %copy-start.1 = (bf16[2048,1024]{1,0:T(8,128)(2,1)S(1)}, bf16[2048,1024]{1,0:T(8,128)(2,1)}, u32[]{:S(2)}) copy-start(bf16[2048,1024]{1,0:T(8,128)(2,1)} %w_out.1) | copy-start | bytes 12582916
  38.1 5.2 %copy-start.2 = (bf16[512,2048]{1,0:T(8,128)(2,1)S(1)}, bf16[512,2048]{1,0:T(8,128)(2,1)}, u32[]{:S(2)}) copy-start(bf16[512,2048]{1,0:T(8,128)(2,1)} %scan.1.y) | copy-start | bytes 6291460
  38.1 5.2 %copy-start.5 = (bf16[1,512,1024]{2,1,0:T(8,128)(2,1)S(1)}, bf16[1,512,1024]{2,1,0:T(8,128)(2,1)}, u32[]{:S(2)}) copy-start(bf16[1,512,1024]{2,1,0:T(8,128)(2,1)} %param.20) | copy-start | bytes 3145732
  38.2 5.1 %copy-start.6 = (bf16[128,2048]{1,0:T(8,128)(2,1)S(1)}, bf16[128,2048]{1,0:T(8,128)(2,1)}, u32[]{:S(2)}) copy-start(bf16[128,2048]{1,0:T(8,128)(2,1)} %constant.4.clone.spread_h.spread) | copy-start | bytes 1572868
  38.2 5.1 %copy-start.7 = (bf16[2,512,128]{2,1,0:T(8,128)(2,1)S(1)}, bf16[2,512,128]{2,1,0:T(8,128)(2,1)}, u32[]{:S(2)}) copy-start(bf16[2,512,128]{2,1,0:T(8,128)(2,1)} %get-tuple-element.40.shard) | copy-start | bytes 786436
  38.2 5.1 %copy-start.8 = (bf16[512,256]{1,0:T(8,128)(2,1)S(1)}, bf16[512,256]{1,0:T(8,128)(2,1)}, u32[]{:S(2)}) copy-start(bf16[512,256]{1,0:T(8,128)(2,1)} %get-tuple-element.28.bc) | copy-start | bytes 786436
  38.2 5.1 %copy-start.9 = (f32[2048]{0:T(1024)S(1)}, f32[2048]{0:T(1024)}, u32[]{:S(2)}) copy-start(f32[2048]{0:T(1024)} %param.36) | copy-start | bytes 24580
  38.2 5.1 %copy-start.10 = (f32[1024]{0:T(1024)S(1)}, f32[1024]{0:T(1024)}, u32[]{:S(2)}) copy-start(f32[1024]{0:T(1024)} %param.38) | copy-start | bytes 12292
  38.2 5.1 %copy-start.11 = (s32[1,32]{1,0:T(1,128)S(1)}, s32[1,32]{1,0:T(1,128)}, u32[]{:S(2)}) copy-start(s32[1,32]{1,0:T(1,128)} %wanted.1) | copy-start | bytes 388
  41.1 2.2 %collective-permute-start.5 = (bf16[128,1024]{1,0:T(8,128)(2,1)S(1)}, bf16[128,1024]{1,0:T(8,128)(2,1)S(1)}, u32[]{:S(2)}, u32[]{:S(2)}) collective-permute-start(bf16[128,1024]{1,0:T(8,128)(2,1)S(1)} %get-tuple-element.39), channel_id=1, source_target_pairs={{0,16},{16,0},{1,17},{17,1},{2,18},{18,2},{3,19},{19,3},{4,20},{20... | collective-permute-start | bytes 786440 | tf_op jit(solution)/shard_map/enter/ppermute | solution.py:480
  43.4 13.9 %copy-start.12 = (s32[1,4]{1,0:T(1,128)S(1)}, s32[1,4]{1,0:T(1,128)}, u32[]{:S(2)}) copy-start(s32[1,4]{1,0:T(1,128)} %ids.1) | copy-start | bytes 52
  80.6 5.5 %collective-permute-start.6 = (bf16[256,1152]{1,0:T(8,128)(2,1)S(1)}, bf16[256,1152]{1,0:T(8,128)(2,1)S(1)}, u32[]{:S(2)}, u32[]{:S(2)}) collective-permute-start(bf16[256,1152]{1,0:T(8,128)(2,1)S(1)} %reshape.18.own), channel_id=1, source_target_pairs={{0,16},{16,0},{1,17},{17,1},{2,18},{18,2},{3,19},{19,3},{4,20},{20... | collective-permute-start | bytes 1769480 | tf_op jit(solution)/shard_map/rows/ppermute | solution.py:503
  82.2 3.4 %copy-start = (bf16[4096,1024]{1,0:T(8,128)(2,1)S(1)}, bf16[4096,1024]{1,0:T(8,128)(2,1)}, u32[]{:S(2)}) copy-start(bf16[4096,1024]{1,0:T(8,128)(2,1)} %keep) | copy-start | bytes 25165828
  85.6 0.7 copy-start.13
